TPU v7x, 32 devices: a whole 2x2x4 slice. The times are simulated.
32 devices in a mesh: dp: 8 (over y, x, core), feat: 4 (over z).
Axes of the slice: x: 2, y: 2, z: 4, core: 2. Of those that a mesh axis runs over, the one named last changes fastest.
Arguments:
- hidden_in: bfloat16 [8192, 1024], P(('dp', 'feat')), may hold values from -6 to 6
- query_weight: bfloat16 [1024, 256], P(('dp', 'feat')), may hold values from -0.1875 to 0.1875
- key_weight: bfloat16 [1024, 256], P(('dp', 'feat')), may hold values from -0.1875 to 0.1875
- value_weight: bfloat16 [1024, 1024], P(('dp', 'feat')), may hold values from -0.1875 to 0.1875
- output_weight: bfloat16 [1024, 1024], P(None, ('dp', 'feat')), may hold values from -3 to 3
- gate_weight: bfloat16 [1024, 2752], P('dp', 'feat'), may hold values from -0.1875 to 0.1875
- up_weight: bfloat16 [1024, 2752], P('dp', 'feat'), may hold values from -0.1875 to 0.1875
- down_weight: bfloat16 [2752, 1024], P('feat', 'dp'), may hold values from -0.109375 to 0.109375
- gain_attn: bfloat16 [1024], P(('dp', 'feat')), may hold values from 0.5 to 1.5
- gain_mlp: bfloat16 [1024], P(('dp', 'feat')), may hold values from 0.5 to 1.5
- first_length: int32 [8], P('dp'), may hold values from 128 to 1024, as said below
- cotangent: bfloat16 [8192, 1024], P(('dp', 'feat')), may hold values from -6 to 6
Outputs:
- block_out: bfloat16 [8192, 1024], P(('dp', 'feat'))
- input_grad: float32 [8192, 1024], P(('dp', 'feat'))
- query_grad: float32 [1024, 256], P(('dp', 'feat'))
- key_grad: float32 [1024, 256], P(('dp', 'feat'))
- value_grad: float32 [1024, 1024], P(('dp', 'feat'))
- output_grad: float32 [1024, 1024], P(None, ('dp', 'feat'))
- gate_grad: float32 [1024, 2752], P('dp', 'feat')
- up_grad: float32 [1024, 2752], P('dp', 'feat')
- down_grad: float32 [2752, 1024], P('feat', 'dp')
- gain_attn_grad: float32 [1024], P(('dp', 'feat'))
- gain_mlp_grad: float32 [1024], P(('dp', 'feat'))
Inputs may be any that keep to these rules, and one draw needn't show every extreme that they name: Each pack of 1024 tokens holds one sequence of first_length tokens and, after it, one of the rest; the value is 1024, 896 or 128.
All inputs are finite; a program needn't handle non-finite values.
Results may differ from a plain program's by a relative error of at most 0.018.
Values may be sent and summed in bfloat16 or wider, within the bound.
No kernel may reach another device: no remote copies, remote signals or barrier semaphores. Data moves between devices by JAX's collectives and lax.ppermute only.
A program may use at most 192 MiB of HBM per device.

v0:
```python
from functools import partial

import jax
import jax.numpy as jnp
from jax import lax
from jax.experimental import pallas as pl
from jax.experimental.pallas import tpu as pltpu
from jax.sharding import PartitionSpec as P

H = 16
HF = 16
DV = 64
SEQ_LEN = 1024
EPSILON = 1e-05

LANES = 128
TILE = 256
GROUPS = 4
F32 = jnp.float32
BF16 = jnp.bfloat16

SLOT_MASKS = (0, 2, 1, 3)
SPLIT_BITS = 2
SPLIT = 1 << SPLIT_BITS


def matmul(first_matrix, second_matrix):
    return jnp.dot(first_matrix, second_matrix, preferred_element_type=F32)


def dot_first(first_matrix, second_matrix):
    return lax.dot_general(
        first_matrix, second_matrix, (((0,), (0,)), ((), ())), preferred_element_type=F32
    )


def dot_last(first_matrix, second_matrix):
    return lax.dot_general(
        first_matrix, second_matrix, (((1,), (1,)), ((), ())), preferred_element_type=F32
    )


def hop(block, bit):
    return lax.ppermute(block, f"bit{bit}", [(0, 1), (1, 0)])


def cross(block, mask):
    return lax.ppermute(block, "feat", [(i, i ^ mask) for i in range(GROUPS)])


def home_pairs(mask):
    pairs = []
    for core in range(2):
        for z in range(GROUPS):
            group = 2 * (z & 1) + core
            pairs.append((core * GROUPS + z, (z >> 1) * GROUPS + (group ^ mask)))
    return pairs


def home(block, mask):
    return lax.ppermute(block, ("bit0", "feat"), home_pairs(mask))


def away(block, mask):
    return lax.ppermute(block, ("bit0", "feat"), [(b, a) for a, b in home_pairs(mask)])


def after(block, *earlier):
    return lax.optimization_barrier((block,) + earlier)[0]


def add_rounded(first, second):
    return (first.astype(F32) + second.astype(F32)).astype(BF16)


def pick(blocks, index, axis=0):
    return lax.dynamic_index_in_dim(blocks, index, axis, keepdims=False)


def place(blocks, sources):
    total = jnp.zeros((len(blocks),) + blocks[0].shape, blocks[0].dtype)
    for block, source in zip(blocks, sources):
        total = lax.dynamic_update_index_in_dim(total, block, source, 0)
    return total


def pair_up(bit, own, other, axis):
    return jnp.where(bit == 0, jnp.stack([own, other], axis), jnp.stack([other, own], axis))


def kernel_call(body, outs, operands, scalars=0, remote=0, scratch=(), flops=0, limit=56):
    smem = pl.BlockSpec(memory_space=pltpu.SMEM)
    vmem = pl.BlockSpec(memory_space=pltpu.VMEM)
    hbm = pl.BlockSpec(memory_space=pl.ANY)
    outs = [jax.ShapeDtypeStruct(shape, dtype) for shape, dtype in outs]
    nbytes = sum(o.size * o.dtype.itemsize for o in list(operands) + outs)
    plain = len(operands) - scalars - remote
    return pl.pallas_call(
        body,
        out_shape=outs,
        in_specs=[smem] * scalars + [vmem] * plain + [hbm] * remote,
        out_specs=[vmem] * len(outs),
        scratch_shapes=list(scratch),
        compiler_params=pltpu.CompilerParams(vmem_limit_bytes=limit * 1024 * 1024),
        cost_estimate=pl.CostEstimate(flops=flops, bytes_accessed=nbytes, transcendentals=0),
    )(*operands)


def lane_in(width, low, high):
    lane = lax.broadcasted_iota(jnp.int32, (1, width), 1)
    return (lane >= low) & (lane < high)


def block_at(index, size):
    return pl.ds(pl.multiple_of(index * size, size), size)


def masked(own, values):
    return jnp.where(own, values, jnp.zeros_like(values))


def front_body(
    first_ref, group_ref, h0_ref, h1_ref, pair_ref, w_ref,
    hr_ref, qkv_ref, kept_ref, sent_ref, attf_ref, rden_ref, att_ref,
):
    first, group = first_ref[0], group_ref[0]
    tokens = h0_ref.shape[0]
    length, width = att_ref.shape
    heads = width // DV
    qk = heads * HF
    for k, (h_ref, at) in enumerate(((h0_ref, 0), (h1_ref, 0), (pair_ref, 0), (pair_ref, tokens))):
        rows = h_ref[at : at + tokens, :].astype(F32)
        scale = lax.rsqrt(jnp.mean(rows * rows, axis=1, keepdims=True) + EPSILON)
        normed = (rows * scale).astype(BF16)
        hr_ref[k] = normed
        qkv_ref[block_at(group ^ SLOT_MASKS[k], tokens), :] = matmul(normed, w_ref[...]).astype(BF16)
    lower = lane_in(LANES, 0, DV)
    keys = qkv_ref[:, qk : 2 * qk]
    head_keys = [masked(lane_in(qk, h * HF, (h + 1) * HF), keys) for h in range(heads)]
    head_values = []
    for h in range(heads):
        low = 2 * qk + (h // 2) * LANES
        tile = qkv_ref[:, low : low + LANES]
        own = lower if h % 2 == 0 else jnp.logical_not(lower)
        head_values.append(jnp.where(own, tile, jnp.ones_like(tile)))
    for i in range(length // TILE):
        extent = (i + 1) * TILE
        rows = slice(i * TILE, extent)
        t_pos = i * TILE + lax.broadcasted_iota(jnp.int32, (TILE, 1), 0)
        s_pos = lax.broadcasted_iota(jnp.int32, (1, extent), 1)
        start = jnp.where(t_pos >= first, first, 0)
        allowed = (s_pos <= t_pos) & (s_pos >= start)
        queries = (qkv_ref[rows, :qk].astype(F32) * 0.25).astype(BF16)
        for pair in range(heads // 2):
            outs = []
            for h in (2 * pair, 2 * pair + 1):
                inner = dot_last(queries, head_keys[h][:extent])
                scores = jnp.where(allowed, 1.0 + inner * (1.0 + 0.5 * inner), 0.0)
                outs.append(matmul(scores.astype(BF16), head_values[h][:extent]))
            numer = jnp.where(lower, outs[0], outs[1])
            denom = pltpu.roll(jnp.where(lower, outs[1], outs[0]), DV, 1)
            recip = 1.0 / denom
            attended = numer * recip
            lanes = slice(pair * LANES, (pair + 1) * LANES)
            att_ref[rows, lanes] = attended.astype(BF16)
            attf_ref[rows, lanes] = attended
            rden_ref[rows, lanes] = recip
    for k, mask in enumerate(SLOT_MASKS):
        out_ref = (kept_ref, sent_ref)[k // 2]
        at = (k % 2) * width
        out_ref[:, at : at + width] = att_ref[block_at(group ^ mask, tokens), :]


def back_body(
    first_ref, group_ref, g0_ref, g1_ref, near_ref, qkv_ref, attf_ref, rden_ref, hr_ref, w_ref,
    kept_ref, sent_ref, term_ref, qt_ref, aug_ref, nb_ref, ag_ref, bars_ref,
):
    first, group = first_ref[0], group_ref[0]
    tokens = g0_ref.shape[0]
    length, width = ag_ref.shape
    heads = width // DV
    qk = heads * HF
    for k, (g_ref, at) in enumerate(((g0_ref, 0), (g1_ref, 0), (near_ref, 0), (near_ref, width))):
        ag_ref[block_at(group ^ SLOT_MASKS[k], tokens), :] = g_ref[:, at : at + width]
    lower = lane_in(LANES, 0, DV)
    queries = (qkv_ref[:, :qk].astype(F32) * 0.25).astype(BF16)
    raw_keys = qkv_ref[:, qk : 2 * qk]
    keys = (raw_keys.astype(F32) * 0.25).astype(BF16)
    head_queries, head_keys, head_values = [], [], []
    for h in range(heads):
        own = lane_in(qk, h * HF, (h + 1) * HF)
        head_queries.append(masked(own, queries))
        head_keys.append(masked(own, keys))
    for h in range(heads):
        lanes = slice((h // 2) * LANES, (h // 2 + 1) * LANES)
        own = lower if h % 2 == 0 else jnp.logical_not(lower)
        numer_bar = ag_ref[:, lanes].astype(F32) * rden_ref[:, lanes]
        products = jnp.where(own, numer_bar * attf_ref[:, lanes], 0.0)
        denom_bar = -jnp.sum(products, axis=1, keepdims=True)
        column = DV if h % 2 == 0 else 0
        numer_bar = jnp.where(own, numer_bar, 0.0)
        nb_ref[h] = numer_bar.astype(BF16)
        aug_ref[h] = jnp.where(
            lane_in(LANES, column, column + 1), denom_bar, numer_bar
        ).astype(BF16)
        low = 2 * qk + (h // 2) * LANES
        tile = qkv_ref[:, low : low + LANES]
        head_values.append(jnp.where(own, tile, jnp.ones_like(tile)))
    qt_ref[...] = jnp.zeros_like(qt_ref)
    for i in range(length // TILE):
        low = i * TILE
        extent = length - low
        rows = slice(low, low + TILE)
        s_pos = low + lax.broadcasted_iota(jnp.int32, (TILE, 1), 0)
        t_pos = low + lax.broadcasted_iota(jnp.int32, (1, extent), 1)
        start = jnp.where(t_pos >= first, first, 0)
        allowed = (s_pos <= t_pos) & (s_pos >= start)
        key_total = jnp.zeros((TILE, qk), F32)
        query_total = jnp.zeros((qk, extent), F32)
        for pair in range(heads // 2):
            value_total = jnp.zeros((TILE, LANES), F32)
            for h in (2 * pair, 2 * pair + 1):
                inner = dot_last(raw_keys[rows], head_queries[h][low:])
                scores = jnp.where(allowed, 1.0 + inner * (1.0 + 0.5 * inner), 0.0)
                value_total += matmul(scores.astype(BF16), nb_ref[h, low:, :])
                bar = dot_last(head_values[h][rows], aug_ref[h, low:, :])
                slope = jnp.where(allowed, bar * (1.0 + inner), 0.0).astype(BF16)
                key_total += matmul(slope, head_queries[h][low:])
                query_total += dot_first(head_keys[h][rows], slope)
            lanes = slice(2 * qk + pair * LANES, 2 * qk + (pair + 1) * LANES)
            bars_ref[rows, lanes] = value_total.astype(BF16)
        bars_ref[rows, qk : 2 * qk] = key_total.astype(BF16)
        qt_ref[:, low:] += query_total
    bars_ref[:, :qk] = qt_ref[...].T.astype(BF16)
    term = jnp.zeros((bars_ref.shape[1], hr_ref.shape[2]), F32)
    for k, mask in enumerate(SLOT_MASKS):
        bars = bars_ref[block_at(group ^ mask, tokens), :]
        (kept_ref, sent_ref)[k // 2][k % 2] = dot_last(bars, w_ref[...]).astype(BF16)
        term += dot_first(bars, hr_ref[k])
    term_ref[...] = term.T.astype(BF16)


def middle_body(
    member_ref, a0_ref, a1_ref, hidden_ref, w_ref,
    middle_ref, mlp_ref, att_ref, gain_ref,
):
    member = member_ref[0]
    part = a0_ref.shape[1] // 2
    for m, mask in enumerate((0, 1, 2, 3)):
        at = (m % 2) * part
        att_ref[:, block_at(member ^ mask, part)] = (a0_ref, a1_ref)[m // 2][:, at : at + part]
    width = att_ref.shape[1]
    pick_gain = jnp.where(lane_in(LANES, 0, 1), jnp.ones((8, LANES), BF16), 0)
    gain = dot_last(pick_gain, w_ref[:, width:])
    gain_ref[...] = gain
    middle = hidden_ref[...].astype(F32) + dot_last(att_ref[...], w_ref[:, :width])
    middle_ref[...] = middle
    scale = lax.rsqrt(jnp.mean(middle * middle, axis=1, keepdims=True) + EPSILON)
    mlp_ref[...] = (middle * scale * gain[:1]).astype(BF16)


def middle_back_body(
    member_ref, own_ref, near_ref, far_ref, middle_ref, gain_ref, cot_ref, attended_ref, w_ref,
    grad_ref, g0_ref, g1_ref, out_ref, att_ref,
):
    member = member_ref[0]
    width = att_ref.shape[1]
    part = g0_ref.shape[1] // 2
    gain = gain_ref[:1]
    mlp_grad = own_ref[...].astype(F32) + near_ref[...].astype(F32) + far_ref[...].astype(F32)
    middle = middle_ref[...]
    scale = lax.rsqrt(jnp.mean(middle * middle, axis=1, keepdims=True) + EPSILON)
    normed = middle * scale
    scaled = mlp_grad * gain
    inner = jnp.mean(normed * scaled, axis=1, keepdims=True)
    grad = cot_ref[...].astype(F32) + scale * (scaled - normed * inner)
    grad_ref[...] = grad
    bar = grad.astype(BF16)
    att_ref[...] = matmul(bar, w_ref[:, :width]).astype(BF16)
    for m, mask in enumerate((0, 1, 2, 3)):
        at = (m % 2) * part
        (g0_ref, g1_ref)[m // 2][:, at : at + part] = att_ref[:, block_at(member ^ mask, part)]
    out_ref[:, :width] = dot_first(bar, attended_ref[...]).astype(BF16)
    term = jnp.sum(mlp_grad * normed, axis=0, keepdims=True)
    out_ref[:, width:] = jnp.broadcast_to(term, (LANES, term.shape[1])).T.astype(BF16)


def load_units(units, piece_ref, weight_refs, sems):
    parts, slots, _, part = piece_ref.shape
    copies = []
    for m, w_ref in enumerate(weight_refs):
        for y in range(parts):
            for s in range(slots):
                copies.append(
                    pltpu.make_async_copy(
                        piece_ref.at[y, s, pl.ds(m * units, units), :],
                        w_ref.at[pl.ds(s * units, units), pl.ds(y * part, part)],
                        sems.at[(m * parts + y) * slots + s],
                    )
                )
    for copy in copies:
        copy.start()
    return copies


def forward_units(total, x_ref, c_ref, weight_refs, hidden_refs, put):
    wg_ref, wu_ref, wd_ref = weight_refs
    tokens = TILE
    edges = list(range(0, total, TILE)) + [total]
    spans = list(zip(edges[:-1], edges[1:]))

    for b in range(x_ref.shape[0] // tokens):
        rows = slice(b * tokens, (b + 1) * tokens)
        x_rows = x_ref[rows, :]
        c_rows = c_ref[rows, :]
        kept = []
        for low, high in spans:
            gate = dot_last(x_rows, wg_ref[low:high, :])
            up = dot_last(x_rows, wu_ref[low:high, :])
            back = dot_last(c_rows, wd_ref[low:high, :])
            sig = 1.0 / (1.0 + jnp.exp(-gate))
            silu = gate * sig
            act = (silu * up).astype(BF16)
            gate_bar = (back * up * (sig + silu * (1.0 - sig))).astype(BF16)
            up_bar = (back * silu).astype(BF16)
            for value, ref in zip((act, gate_bar, up_bar), hidden_refs):
                ref[low:high, rows] = value.T
            kept.append((act, gate_bar, up_bar))
        branch = sum(matmul(kept[n][0], wd_ref[low:high, :]) for n, (low, high) in enumerate(spans))
        grad = sum(matmul(kept[n][1], wg_ref[low:high, :]) for n, (low, high) in enumerate(spans))
        grad += sum(matmul(kept[n][2], wu_ref[low:high, :]) for n, (low, high) in enumerate(spans))
        put(b, branch, grad)


def forward_body(units, count, moved, *refs):
    me_ref, x_refs, c_refs, piece_ref, refs = refs[0], refs[1:4], refs[4:7], refs[7], refs[8:]
    grad_refs, branch_refs, refs = refs[:SPLIT], refs[SPLIT : SPLIT + 2], refs[SPLIT + 2 :]
    x_ref, c_ref, hidden_refs, weight_refs, sems = *refs[:2], refs[2:5], refs[5:8], refs[8]
    copies = load_units(units, piece_ref, weight_refs, sems)
    tokens = x_refs[0].shape[0]
    me = me_ref[0]
    block = x_ref.shape[1] // count
    for (own, far, pair), ref_out in ((x_refs, x_ref), (c_refs, c_ref)):
        for low, ref in ((0, own), (tokens, far), (2 * tokens, pair)):
            rows = slice(low, low + ref.shape[0])
            if moved:
                for j in range(count):
                    lanes = slice(j * block, (j + 1) * block)
                    ref_out[rows, lanes] = ref[:, block_at(me ^ j, block)]
            else:
                ref_out[rows, :] = ref[...]
    for copy in copies:
        copy.wait()

    def put(b, branch, grad):
        def store(ref, value):
            value = value.astype(BF16)
            if moved:
                for j in range(count):
                    ref[:, block_at(me ^ j, block)] = value[:, j * block : (j + 1) * block]
            else:
                ref[...] = value

        store(grad_refs[b], grad)
        store(branch_refs[b // 2].at[b % 2], branch)

    forward_units(weight_refs[0].shape[0], x_ref, c_ref, weight_refs, hidden_refs, put)


def weights_body(units, part_ref, x_ref, c_ref, act_ref, gate_ref, up_ref, term_ref):
    slots, _, part = term_ref.shape
    step = min(part, 256)
    for m, (left, right) in enumerate(((gate_ref, x_ref), (up_ref, x_ref), (act_ref, c_ref))):
        for at in range(0, part, step):
            lanes = pl.ds(pl.multiple_of(part_ref[0] * part + at, step), step)
            out = matmul(left[...], right[:, lanes]).astype(BF16)
            rows = slice(m * units, (m + 1) * units)
            for s in range(slots):
                term_ref[s, rows, at : at + step] = out[s * units : (s + 1) * units]


def on_device(
    dp,
    hidden_in,
    query_weight,
    key_weight,
    value_weight,
    output_weight,
    gate_weight,
    up_weight,
    down_weight,
    gain_attn,
    gain_mlp,
    first_length,
    cotangent,
):
    member = lax.axis_index("feat")
    me = lax.axis_index(dp)
    bits = len(dp)
    size = 1 << bits
    links = list(range(1, bits))
    core = me & 1
    group = 2 * (member & 1) + core
    tokens, width = hidden_in.shape
    length = GROUPS * tokens
    place_arr, member_arr, group_arr = (me % SPLIT).reshape(1), member.reshape(1), group.reshape(1)

    latest = {}

    def send(link, how, *blocks):
        blocks = [after(block, *latest.get(link, ())) for block in blocks]
        latest[link] = tuple(how(block) for block in blocks)
        return latest[link] if len(blocks) > 1 else latest[link][0]

    def link_of(bit):
        return ("core", "x", "y")[min(bit, 2)]

    def swap_bit(block, bit):
        return send(link_of(bit), partial(hop, bit=bit), block)

    def reduce_bits(term, order, left):
        left = sorted(left, reverse=True)
        for bit in order:
            axis = left.index(bit)
            mine = (me >> bit) & 1
            other = swap_bit(pick(term, 1 - mine, axis), bit)
            term = add_rounded(pick(term, mine, axis), other)
            left.remove(bit)
        return term

    rows = query_weight.shape[0]
    qk = H * HF // GROUPS
    vw = H * DV // GROUPS
    attn_pack = jnp.concatenate(
        [
            query_weight.reshape(rows, GROUPS, qk),
            key_weight.reshape(rows, GROUPS, qk),
            value_weight.reshape(rows, GROUPS, vw),
        ],
        axis=2,
    )
    attn_pack = (attn_pack.astype(F32) * gain_attn.astype(F32)[:, None, None]).astype(BF16)
    cols = attn_pack.shape[2]
    attn_pack = attn_pack.transpose(1, 0, 2).reshape(2, 2, rows, cols)
    sent = pick(attn_pack, 1 - core, 1).reshape(2 * rows, cols)
    lengths = jnp.broadcast_to(first_length.astype(BF16)[:, None], (16, cols))
    sent = swap_bit(jnp.concatenate([lengths, sent], axis=0), 0)
    first = jnp.where((member >> 1) == core, first_length, sent[0, :1].astype(jnp.int32))
    sent = sent[16:].reshape(2, rows, cols)
    attn_pack = pair_up(core, pick(attn_pack, core, 1), sent, 2)

    output_pack = jnp.concatenate(
        [output_weight.T, jnp.pad(gain_mlp[:, None], ((0, 0), (0, LANES - 1)))], axis=1
    )
    same = pick(attn_pack, member & 1).reshape(rows, 2 * cols)
    flip = pick(attn_pack, 1 - (member & 1)).reshape(rows, 2 * cols)
    far = cross(jnp.concatenate([same, flip, output_pack], axis=1), 2)
    flips = [
        jnp.concatenate([flip, output_pack], axis=1),
        far[:, 2 * cols :],
    ]
    near = cross(jnp.concatenate(flips, axis=0), 1)
    both = [
        jnp.concatenate([same, output_pack], axis=1),
        near[:rows],
        jnp.concatenate([far[:, : 2 * cols], far[:, 4 * cols :]], axis=1),
        near[rows:],
    ]
    hidden = [away(hidden_in, mask) for mask in (0, 2)]
    both = after(place(both, [member ^ m for m in range(GROUPS)]), *hidden)
    hidden_units = down_weight.shape[0]
    units = -(-hidden_units // (16 * SPLIT)) * 16
    stacked = jnp.stack([gate_weight.T, up_weight.T, down_weight])
    stacked = jnp.pad(stacked, ((0, 0), (0, SPLIT * units - hidden_units), (0, 0)))
    block = stacked.shape[2]
    aligned = block % LANES == 0
    stacked = stacked.reshape(3, 2, 2, units, block)
    side = (me >> 1) & 1
    kept = [pick(stacked, side, 1), swap_bit(pick(stacked, 1 - side, 1), 1)]
    sent = swap_bit(jnp.concatenate([pick(part, 1 - core, 1) for part in kept], axis=2), 0)
    kept = [pick(part, core, 1) for part in kept]
    own = jnp.concatenate([kept[0], sent[:, :, :block], kept[1], sent[:, :, block:]], axis=2)
    own = own.reshape(3 * units, SPLIT * block)
    cot_far = swap_bit(cotangent, 1)

    output_mat = both[:, :, 2 * cols :].reshape(GROUPS * rows, -1)
    output_mat = pair_up((me >> links[-1]) & 1, output_mat, swap_bit(output_mat, links[-1]), 0)
    attn_mat = both[:, :, : 2 * cols].reshape(GROUPS, rows, 2, cols).transpose(2, 0, 1, 3)
    for bit in links:
        attn_mat = pair_up((me >> bit) & 1, attn_mat, swap_bit(attn_mat, bit), 0)
        attn_mat = attn_mat.reshape((-1,) + attn_mat.shape[2:])
    attn_mat = attn_mat.reshape(width, cols)
    hidden_pair = swap_bit(jnp.concatenate(hidden, axis=0), 0)

    far_axes = dp[: bits - SPLIT_BITS] + ("feat",)
    pieces = lax.all_gather(after(own, *hidden), far_axes)
    pieces = pieces.reshape(-1, GROUPS, 3 * units, SPLIT * block)
    if not aligned:
        pieces = pieces.transpose(1, 2, 0, 3).reshape(1, GROUPS, 3 * units, width)

    def pair_with(own, far):
        return [own, far, swap_bit(jnp.concatenate([own, far], axis=0), 0)]


    hr, qkv, out, sent, attf, rden = kernel_call(
        front_body,
        [((GROUPS, tokens, width), BF16), ((length, cols), BF16)]
        + [((tokens, 2 * vw), BF16)] * 2
        + [((length, vw), F32)] * 2,
        (first, group_arr, *hidden, hidden_pair, attn_mat),
        scalars=2,
        scratch=(pltpu.VMEM((length, vw), BF16),),
        flops=8 * 2**30,
    )
    sent = swap_bit(sent, 0)
    for axis, bit in enumerate(links[-2::-1] + [0], 1):
        output_mat = pair_up((me >> bit) & 1, output_mat, swap_bit(output_mat, bit), axis)
    output_mat = output_mat.reshape(width, -1)
    cots = pair_with(cotangent, cot_far)
    out = [jnp.concatenate([part[:, at : at + vw] for part in (out, sent)], axis=1) for at in (0, vw)]
    out = [home(out[0], 0), home(out[1], 2)]
    middle, mlp_in, attended, gain8 = kernel_call(
        middle_body,
        [
            ((tokens, width), F32),
            ((tokens, width), BF16),
            ((tokens, H * DV), BF16),
            ((8, width), F32),
        ],
        (member_arr, *out, hidden_in, output_mat),
        scalars=1,
        flops=2**30,
    )

    mlps = pair_with(mlp_in, swap_bit(mlp_in, 1))
    swap = lambda v: v
    if not aligned:
        order = jnp.arange(size) ^ (me % SPLIT)
        swap = lambda v: jnp.take(
            v.reshape(v.shape[:-1] + (size, block)), order, axis=v.ndim - 1
        ).reshape(v.shape)
    rows_shape = ((SPLIT * tokens, width), BF16)

    hidden_shape = (GROUPS * units, SPLIT * tokens)
    *grads, branch, branch_sent, x_all, c_all, act_t, gate_t, up_t = kernel_call(
        partial(forward_body, units, size, aligned),
        [((tokens, width), BF16)] * SPLIT
        + [((2, tokens, width), BF16)] * 2
        + [rows_shape] * 2
        + [(hidden_shape, BF16)] * 3,
        (place_arr, *[swap(v) for v in mlps], *[swap(v) for v in cots], pieces),
        scalars=1,
        remote=1,
        scratch=(
            *[pltpu.VMEM((GROUPS * units, width), BF16)] * 3,
            pltpu.SemaphoreType.DMA((3 * GROUPS * pieces.shape[0],)),
        ),
        flops=12 * 2**30,
    )
    branch, branch_sent, grads = swap(branch), swap(branch_sent), [swap(v) for v in grads]
    grad_far = add_rounded(grads[1], swap_bit(grads[3], 0))
    grad_near = swap_bit(grads[2], 0)
    x_all = after(x_all, grad_far)
    grad_far = swap_bit(grad_far, 1)
    branch_sent = swap_bit(branch_sent, 0)
    branch_sum = add_rounded(branch[1], branch_sent[1])
    branch_far = swap_bit(branch_sum, 1)
    parts = pieces.shape[0]

    def weight_terms(part):
        (term,) = kernel_call(
            partial(weights_body, units),
            [((GROUPS, 3 * units, width // parts), BF16)],
            (part.reshape(1), x_all, c_all, act_t, gate_t, up_t),
            scalars=1,
            flops=6 * 2**30 // parts,
        )
        return term

    if parts == 2:
        part = me >> SPLIT_BITS
        term_sent, term = weight_terms(1 - part), weight_terms(part)
        term_sum = add_rounded(term, swap_bit(term_sent, SPLIT_BITS))
    else:
        far_bits = list(range(SPLIT_BITS, bits))[::-1]
        term = weight_terms(jnp.zeros((), jnp.int32))
        term_sum = term.reshape(GROUPS, 3 * units, -1, SPLIT * block).transpose(2, 0, 1, 3)
        term_sum = term_sum.reshape((2,) * len(far_bits) + term_sum.shape[1:])
        term_sum = reduce_bits(term_sum, far_bits, far_bits)
    total = lax.psum_scatter(term_sum, "feat")

    middle_grad, *att_grad, output_term = kernel_call(
        middle_back_body,
        [((tokens, width), F32)]
        + [((tokens, 2 * vw), BF16)] * 2
        + [((width, H * DV + LANES), BF16)],
        (member_arr, grads[0], grad_near, after(grad_far, term, branch_sum), middle, gain8, cotangent, attended, output_mat),
        scalars=1,
        scratch=(pltpu.VMEM((tokens, H * DV), BF16),),
        flops=2**30,
    )
    att_grad = [away(part, mask) for part, mask in zip(att_grad, (0, 2))]
    output_term = output_term.reshape((2,) * bits + (GROUPS, rows, H * DV + LANES))
    output_term = reduce_bits(output_term, [0], range(bits))
    att_sent = jnp.concatenate([part[:, vw:] for part in att_grad], axis=1)
    att_grad.append(swap_bit(att_sent, 0))
    output_term = reduce_bits(output_term, links[:1], links)
    att_grad = [after(part, term_sum) for part in att_grad]
    input_parts, input_sent, attn_term = kernel_call(
        back_body,
        [((2, tokens, width), BF16)] * 2 + [((width, cols), BF16)],
        (first, group_arr, *att_grad, qkv, attf, rden, hr, attn_mat),
        scalars=2,
        scratch=(
            pltpu.VMEM((qk, length), F32),
            pltpu.VMEM((vw // DV, length, LANES), BF16),
            pltpu.VMEM((vw // DV, length, LANES), BF16),
            pltpu.VMEM((length, vw), BF16),
            pltpu.VMEM((length, cols), BF16),
        ),
        flops=12 * 2**30,
    )
    input_sent = swap_bit(input_sent, 0)
    input_parts = [add_rounded(input_parts[k], input_sent[k]) for k in range(2)]
    input_parts = [home(input_parts[0], 0), home(input_parts[1], 2)]
    scaled_grad = input_parts[0].astype(F32) + input_parts[1].astype(F32)
    residual = hidden_in.astype(F32)
    scale = lax.rsqrt(jnp.mean(residual * residual, axis=1, keepdims=True) + EPSILON)
    normed = residual * scale
    inner = jnp.mean(normed * scaled_grad, axis=1, keepdims=True)
    input_grad = middle_grad + scale * (scaled_grad - normed * inner)

    attn_term = after(attn_term, input_sent).reshape((2,) * len(links) + (2, GROUPS, rows, cols))
    attn_term = reduce_bits(attn_term, links[:0:-1], links)
    output_term = reduce_bits(output_term, links[1:], links[1:])
    attn_term = reduce_bits(attn_term, links[:1], links[:1])
    attn_term = attn_term.transpose(1, 2, 0, 3).reshape(GROUPS, rows, 2 * cols)
    both = jnp.concatenate([attn_term, output_term], axis=2)
    both = [pick(both, member ^ m) for m in range(GROUPS)]
    both = [both[0]] + [cross(after(both[m], total), m) for m in range(1, GROUPS)]
    output_sum = sum(part[:, 2 * cols :].astype(F32) for part in both)
    output_grad = output_sum[:, : H * DV].T
    mlp_gain_grad = output_sum[:, H * DV]
    same = both[0][:, : 2 * cols].astype(F32) + both[2][:, : 2 * cols].astype(F32)
    flip = both[1][:, : 2 * cols].astype(F32) + both[3][:, : 2 * cols].astype(F32)
    halves = pair_up(member & 1, same, flip, 0).reshape(2, rows, 2, cols)
    halves = pair_up(core, pick(halves, core, 2), swap_bit(pick(halves, 1 - core, 2), 0), 1)
    attn_grad = halves.reshape(GROUPS, rows, cols).transpose(1, 0, 2)
    scale_rows = gain_attn.astype(F32)[:, None]
    query_raw = attn_grad[:, :, :qk].reshape(rows, H * HF)
    key_raw = attn_grad[:, :, qk : 2 * qk].reshape(rows, H * HF)
    value_raw = attn_grad[:, :, 2 * qk :].reshape(rows, H * DV)
    attn_gain_grad = (
        jnp.sum(query_raw * query_weight.astype(F32), axis=1)
        + jnp.sum(key_raw * key_weight.astype(F32), axis=1)
        + jnp.sum(value_raw * value_weight.astype(F32), axis=1)
    )

    block_out = (
        middle
        + branch[0].astype(F32)
        + branch_sent[0].astype(F32)
        + branch_far.astype(F32)
    ).astype(BF16)

    total = total.astype(F32)
    lanes = [slice(j * block, (j + 1) * block) for j in range(SPLIT)]
    near = swap_bit(jnp.concatenate([total[:, lanes[1]], total[:, lanes[3]]], axis=1), 0)
    far = jnp.concatenate([total[:, lanes[2]], near[:, block:]], axis=0).astype(BF16)
    far = swap_bit(far, 1).astype(F32)
    shares = [total[:, lanes[0]], near[:, :block], far[: 3 * units], far[3 * units :]]
    shares = [jnp.where(core == 0, shares[k], shares[k ^ 1]) for k in range(SPLIT)]
    shares = [jnp.where(side == 0, shares[k], shares[k ^ 2]) for k in range(SPLIT)]
    total = jnp.stack([share.reshape(3, units, block) for share in shares], axis=1)
    total = total.reshape(3, SPLIT * units, block)[:, :hidden_units]
    return (
        block_out,
        input_grad,
        query_raw * scale_rows,
        key_raw * scale_rows,
        value_raw * scale_rows,
        output_grad,
        total[0].T,
        total[1].T,
        total[2],
        attn_gain_grad,
        mlp_gain_grad,
    )


def solution(mesh):
    bits = mesh.shape["dp"].bit_length() - 1
    dp = tuple(f"bit{bit}" for bit in reversed(range(bits)))
    fine = jax.sharding.Mesh(mesh.devices.reshape((2,) * bits + (GROUPS,)), dp + ("feat",))
    both = dp + ("feat",)
    in_specs = (
        P(both, None),
        P(both, None),
        P(both, None),
        P(both, None),
        P(None, both),
        P(dp, "feat"),
        P(dp, "feat"),
        P("feat", dp),
        P(both),
        P(both),
        P(dp),
        P(both, None),
    )
    out_specs = (
        P(both, None),
        P(both, None),
        P(both, None),
        P(both, None),
        P(both, None),
        P(None, both),
        P(dp, "feat"),
        P(dp, "feat"),
        P("feat", dp),
        P(both),
        P(both),
    )
    return jax.shard_map(
        partial(on_device, dp), mesh=fine, in_specs=in_specs, out_specs=out_specs, check_vma=False
    )
```

profile of v0, /device:TPU:0, one launch (start us, length us, event | category | flops | bytes accessed | tf_op | source)
XLA Modules:
  0.0 348.7 jit_solution(10164719156210669877)
XLA Ops:
  11.8 1.1 fusion.17
  13.0 2.6 collective-permute-start.3
  16.4 2.7 collective-permute-start.6
  19.0 3.7 %collective-permute-done.3 = bf16[3,2,176,128]{3,2,1,0:T(8,128)(2,1)S(1)} collective-permute-done((bf16[3,2,176,128]{3,2,1,0:T(8,128)(2,1)S(1)}, bf16[3,2,176,128]{3,2,1,0:T(8,128)(2,1)S(1)}, u32[]{:S(2)}, u32[]{:S(2)}) %collective-permute-start.3) | collective-permute-done | bytes 270368 | tf_op jit(solution)/shard_map/ppermute | solution.py:44
  23.5 3.4 collective-permute-start.2
  30.1 21.9 %collective-permute-done.2.h1_ref = bf16[256,1024]{1,0:T(8,128)(2,1)S(1)} collective-permute-done((bf16[256,1024]{1,0:T(8,128)(2,1)S(1)}, bf16[256,1024]{1,0:T(8,128)(2,1)S(1)}, u32[]{:S(2)}, u32[]{:S(2)}) %collective-permute-start.2) | collective-permute-done | bytes 524320 | tf_op jit(solution)/shard_map/ppermute | solution.py:65
  52.2 1.6 collective-permute-start.8
  55.7 1.6 collective-permute-start.10
  57.2 1.2 slice.202
  59.4 5.0 %collective-permute-done.8.refs_5_ = bf16[256,1024]{1,0:T(8,128)(2,1)S(1)} collective-permute-done((bf16[256,1024]{1,0:T(8,128)(2,1)S(1)}, bf16[256,1024]{1,0:T(8,128)(2,1)S(1)}, u32[]{:S(2)}, u32[]{:S(2)}) %collective-permute-start.8) | collective-permute-done | bytes 524320 | tf_op jit(solution)/shard_map/ppermute | solution.py:44
  64.4 1.5 collective-permute-start.9
  66.1 5.2 %collective-permute-done.9 = bf16[2,4,32,384]{3,0,2,1:T(2,128)(2,1)S(1)} collective-permute-done((bf16[2,4,32,384]{3,0,2,1:T(2,128)(2,1)S(1)}, bf16[2,4,32,384]{3,0,2,1:T(2,128)(2,1)S(1)}, u32[]{:S(2)}, u32[]{:S(2)}) %collective-permute-start.9) | collective-permute-done | bytes 196640 | tf_op jit(solution)/shard_map/ppermute | solution.py:44
  71.2 1.5 collective-permute-start.15
  73.3 1.6 collective-permute-start.11
  75.2 6.0 %collective-permute-done.11 = bf16[4,4,32,384]{3,2,1,0:T(8,128)(2,1)S(1)} collective-permute-done((bf16[4,4,32,384]{3,2,1,0:T(8,128)(2,1)S(1)}, bf16[4,4,32,384]{3,2,1,0:T(8,128)(2,1)S(1)}, u32[]{:S(2)}, u32[]{:S(2)}) %collective-permute-start.11) | collective-permute-done | bytes 393248 | tf_op jit(solution)/shard_map/ppermute | solution.py:44
  81.2 1.1 maximum_select_fusion.2
  83.0 1.0 copy-done.24
  83.9 8.5 %shard_map.203 = (bf16[4,256,1024]{2,1,0:T(8,128)(2,1)}, bf16[1024,384]{1,0:T(8,128)(2,1)}, bf16[256,512]{1,0:T(8,128)(2,1)}, bf16[256,512]{1,0:T(8,128)(2,1)}, ...) custom-call(s32[1]{0:T(128)S(6)} %select_n.253.first_ref, s32[1]{0:T(128)} %bitcast.7.group_ref, bf16[256,1024]{1,0:T(8,128)(2,1)} %copy-done.13, ...), custom_call_target="tpu_custom_call" | custom-call | flops 8589934592 | bytes 8388616 | tf_op jit(solution)/shard_map/pallas_call | solution.py:98
  92.7 1.5 collective-permute-done.12
  97.0 7.2 %collective-permute-start.18 = (bf16[512,1024]{1,0:T(8,128)(2,1)S(1)}, bf16[512,1024]{1,0:T(8,128)(2,1)S(1)}, u32[]{:S(2)}, u32[]{:S(2)}) collective-permute-start(bf16[512,1024]{1,0:T(8,128)(2,1)S(1)} %pad_maximum_fusion.5), channel_id=1, source_target_pairs={{0,4},{4,0},{1,5},{5,1},{2,6},{6,2},{3,7},{7,3},{8,12},{12,8},{9,1... | collective-permute-start | bytes 3145736 | tf_op jit(solution)/shard_map/ppermute | solution.py:44
  104.2 1.8 maximum_select_fusion
  106.0 8.3 %collective-permute-done.14.a1_ref = bf16[256,512]{1,0:T(8,128)(2,1)S(1)} collective-permute-done((bf16[256,512]{1,0:T(8,128)(2,1)S(1)}, bf16[256,512]{1,0:T(8,128)(2,1)S(1)}, u32[]{:S(2)}, u32[]{:S(2)}) %collective-permute-start.14) | collective-permute-done | bytes 262176 | tf_op jit(solution)/shard_map/ppermute | solution.py:61
  115.1 4.1 %shard_map.204 = (f32[256,1024]{1,0:T(8,128)}, bf16[256,1024]{1,0:T(8,128)(2,1)}, bf16[256,1024]{1,0:T(8,128)(2,1)}, f32[8,1024]{1,0:T(8,128)}) custom-call(s32[1]{0:T(128)} %bitcast.member_ref, bf16[256,512]{1,0:T(8,128)(2,1)} %copy-done.27, bf16[256,512]{1,0:T(8,128)(2,1)} %copy-done.25, bf16[256,1024]{1,0:T(8,128)(2,1)} %hidden_ref.1, ...), custom_call_target="tpu_custom_call" | custom-call | flops 1073741824 | bytes 5537796 | tf_op jit(solution)/shard_map/pallas_call | solution.py:98
  119.2 1.4 collective-permute-start.17
  120.6 8.0 %collective-permute-done.17.refs_2_ = bf16[256,1024]{1,0:T(8,128)(2,1)S(1)} collective-permute-done((bf16[256,1024]{1,0:T(8,128)(2,1)}, bf16[256,1024]{1,0:T(8,128)(2,1)S(1)}, u32[]{:S(2)}, u32[]{:S(2)}) %collective-permute-start.17) | collective-permute-done | bytes 524320 | tf_op jit(solution)/shard_map/ppermute | solution.py:44
  128.6 1.3 pad_maximum_fusion.4
  130.0 14.3 %collective-permute-start.19 = (bf16[512,1024]{1,0:T(8,128)(2,1)S(1)}, bf16[512,1024]{1,0:T(8,128)(2,1)}, u32[]{:S(2)}, u32[]{:S(2)}) collective-permute-start(bf16[512,1024]{1,0:T(8,128)(2,1)S(1)} %pad_maximum_fusion.4), channel_id=1, source_target_pairs={{0,4},{4,0},{1,5},{5,1},{2,6},{6,2},{3,7},{7,3},{8,12},{12,8},{9,1... | collective-permute-start | bytes 3145736 | tf_op jit(solution)/shard_map/ppermute | solution.py:44
  144.3 2.4 collective-permute-done.19.refs_3_
  146.7 32.2 %shard_map.205 = (bf16[256,1024]{1,0:T(8,128)(2,1)}, bf16[256,1024]{1,0:T(8,128)(2,1)}, bf16[256,1024]{1,0:T(8,128)(2,1)}, bf16[256,1024]{1,0:T(8,128)(2,1)}, bf...) custom-call(s32[1]{0:T(128)} %bitcast.43.refs_0_, ...), custom_call_target="tpu_custom_call" | custom-call | flops 12884901888 | bytes 21233668 | tf_op jit(solution)/shard_map/pallas_call | solution.py:98
  179.3 1.7 collective-permute-done.20
  181.5 1.7 collective-permute-done.21.near_ref
  183.6 2.0 add_convert_fusion.3
  185.6 7.3 %shard_map.208 = bf16[4,528,512]{2,1,0:T(8,128)(2,1)} custom-call(s32[1]{0:T(128)} %bitcast.53.part_ref, bf16[1024,1024]{1,0:T(8,128)(2,1)} %get-tuple-element.106.x_ref, bf16[1024,1024]{1,0:T(8,128)(2,1)} %get-tuple-element.107.c_ref, bf16[704,1024]{1,0:T(8,128)(2,1)} %get-tuple-element.108.act_ref, bf16[704,1024]{1,0:T(8,128)(2,1)} %get-tuple-element.109.gate_ref, ...), custom_call_target="tpu_custom_call" | custom-call | flops 3221225472 | bytes 10682372 | tf_op jit(solution)/shard_map/pallas_call | solution.py:98
  192.9 1.5 collective-permute-start.26
  194.4 1.5 collective-permute-start.23
  195.8 7.3 %shard_map.206 = bf16[4,528,512]{2,1,0:T(8,128)(2,1)} custom-call(s32[1]{0:T(128)} %bitcast.52.part_ref, bf16[1024,1024]{1,0:T(8,128)(2,1)} %get-tuple-element.106.x_ref, bf16[1024,1024]{1,0:T(8,128)(2,1)} %get-tuple-element.107.c_ref, bf16[704,1024]{1,0:T(8,128)(2,1)} %get-tuple-element.108.act_ref, bf16[704,1024]{1,0:T(8,128)(2,1)} %get-tuple-element.109.gate_ref, ...), custom_call_target="tpu_custom_call" | custom-call | flops 3221225472 | bytes 10682372 | tf_op jit(solution)/shard_map/pallas_call | solution.py:98
  203.1 1.1 fusion.18
  204.3 4.0 %collective-permute-done.23.far_ref = bf16[256,1024]{1,0:T(8,128)(2,1)S(1)} collective-permute-done((bf16[256,1024]{1,0:T(8,128)(2,1)}, bf16[256,1024]{1,0:T(8,128)(2,1)S(1)}, u32[]{:S(2)}, u32[]{:S(2)}) %collective-permute-start.23) | collective-permute-done | bytes 524320 | tf_op jit(solution)/shard_map/ppermute | solution.py:44
  209.1 6.1 %shard_map.207 = (f32[256,1024]{1,0:T(8,128)}, bf16[256,512]{1,0:T(8,128)(2,1)}, bf16[256,512]{1,0:T(8,128)(2,1)}, bf16[1024,1152]{1,0:T(8,128)(2,1)}) custom-call(s32[1]{0:T(128)} %bitcast.member_ref, bf16[256,1024]{1,0:T(8,128)(2,1)} %get-tuple-element.104.own_ref, bf16[256,1024]{1,0:T(8,128)(2,1)} %copy-done.10, bf16[256,1024]{1,0:T(8,128)(2,1)} %copy-done.11, ...), custom_call_target="tpu_custom_call" | custom-call | flops 1073741824 | bytes 9994244 | tf_op jit(solution)/shard_map/pallas_call | solution.py:98
  215.2 1.4 dynamic-slice_bitcast_fusion
  216.6 3.6 %collective-permute-start.25 = (bf16[256,512]{1,0:T(8,128)(2,1)}, bf16[256,512]{1,0:T(8,128)(2,1)}, u32[]{:S(2)}, u32[]{:S(2)}) collective-permute-start(bf16[256,512]{1,0:T(8,128)(2,1)} %get-tuple-element.115), channel_id=1, source_target_pairs={{0,0},{2,1},{4,2},{6,3},{1,4},{3,5},{5,6},{7,7},{8,8},{10,9},{12,1... | collective-permute-start | bytes 786440 | tf_op jit(solution)/shard_map/ppermute | solution.py:65
  220.7 1.5 collective-permute-start.24
  223.2 10.9 %collective-permute-done.27.g1_ref = bf16[256,512]{1,0:T(8,128)(2,1)} collective-permute-done((bf16[256,512]{1,0:T(8,128)(2,1)}, bf16[256,512]{1,0:T(8,128)(2,1)}, u32[]{:S(2)}, u32[]{:S(2)}) %collective-permute-start.27) | collective-permute-done | bytes 262176 | tf_op jit(solution)/shard_map/ppermute | solution.py:65
  235.7 6.5 %collective-permute-done.26 = bf16[4,528,512]{2,1,0:T(8,128)(2,1)S(1)} collective-permute-done((bf16[4,528,512]{2,1,0:T(8,128)(2,1)}, bf16[4,528,512]{2,1,0:T(8,128)(2,1)S(1)}, u32[]{:S(2)}, u32[]{:S(2)}) %collective-permute-start.26) | collective-permute-done | bytes 2162720 | tf_op jit(solution)/shard_map/ppermute | solution.py:44
  242.2 3.5 %add_convert_fusion = bf16[4,528,512]{2,1,0:T(8,128)(2,1)} fusion(bf16[4,528,512]{2,1,0:T(8,128)(2,1)S(1)} %collective-permute-done.26, bf16[4,528,512]{2,1,0:T(8,128)(2,1)} %shard_map.206), kind=kLoop, calls=%fused_computation | loop fusion | flops 4325376 | bytes 6488064 | tf_op jit(solution)/shard_map/convert_element_type | solution.py:73
  246.7 1.9 fusion
  248.7 1.5 collective-permute-start.34
  251.0 14.2 %shard_map.209 = (bf16[2,256,1024]{2,1,0:T(8,128)(2,1)}, bf16[2,256,1024]{2,1,0:T(8,128)(2,1)}, bf16[1024,384]{1,0:T(8,128)(2,1)}) custom-call(s32[1]{0:T(128)S(6)} %select_n.253.first_ref, s32[1]{0:T(128)} %bitcast.7.group_ref, bf16[256,512]{1,0:T(8,128)(2,1)} %collective-permute-done.25.g0_ref, bf16[256,512]{1,0:T(8,128)(2,1)} %collective-permute-done.27.g1_ref, ...), custom_call_target="tpu_custom_call" | custom-call | flops 12884901888 | bytes 9437192 | tf_op jit(solution)/shard_map/pallas_call | solution.py:98
  265.6 2.5 fusion.13
  268.1 1.3 fusion.3
  269.9 1.8 collective-permute-start.33
  271.7 1.6 fusion.19
  274.0 6.6 %collective-permute-start.32 = (bf16[256,1024]{1,0:T(8,128)(2,1)S(1)}, bf16[256,1024]{1,0:T(8,128)(2,1)S(1)}, u32[]{:S(2)}, u32[]{:S(2)}) collective-permute-start(bf16[256,1024]{1,0:T(8,128)(2,1)S(1)} %get-tuple-element.148), channel_id=1, source_target_pairs={{0,2},{1,0},{2,6},{3,4},{4,3},{5,1},{6,7},{7,5},{8,10},{9,8},{10,1... | collective-permute-start | bytes 1572872 | tf_op jit(solution)/shard_map/ppermute | solution.py:61
  282.8 1.5 collective-permute-start.36
  284.3 18.2 %collective-permute-done.32 = bf16[256,1024]{1,0:T(8,128)(2,1)S(1)} collective-permute-done((bf16[256,1024]{1,0:T(8,128)(2,1)S(1)}, bf16[256,1024]{1,0:T(8,128)(2,1)S(1)}, u32[]{:S(2)}, u32[]{:S(2)}) %collective-permute-start.32) | collective-permute-done | bytes 524320 | tf_op jit(solution)/shard_map/ppermute | solution.py:61
  302.9 1.3 fusion.10
  305.7 12.6 %collective-permute-start.37 = (bf16[32,1920]{1,0:T(8,128)(2,1)S(1)}, bf16[32,1920]{1,0:T(8,128)(2,1)S(1)}, u32[]{:S(2)}, u32[]{:S(2)}) collective-permute-start(bf16[32,1920]{1,0:T(8,128)(2,1)S(1)} %get-tuple-element.137), channel_id=1, source_target_pairs={{0,2},{1,3},{2,0},{3,1},{4,6},{5,7},{6,4},{7,5},{8,10},{9,11},{10,... | collective-permute-start | bytes 368648 | tf_op jit(solution)/shard_map/ppermute | solution.py:48
  318.7 1.2 collective-permute-start.39
  319.9 1.2 bitcast_convert_fusion
  321.1 3.5 %collective-permute-done.37 = bf16[32,1920]{1,0:T(8,128)(2,1)S(1)} collective-permute-done((bf16[32,1920]{1,0:T(8,128)(2,1)S(1)}, bf16[32,1920]{1,0:T(8,128)(2,1)S(1)}, u32[]{:S(2)}, u32[]{:S(2)}) %collective-permute-start.37) | collective-permute-done | bytes 122912 | tf_op jit(solution)/shard_map/ppermute | solution.py:48
  324.9 2.8 collective-permute-done.39
  331.4 1.5 collective-permute-start.42
  334.3 5.9 %collective-permute-done.42 = bf16[1056,128]{1,0:T(8,128)(2,1)S(1)} collective-permute-done((bf16[1056,128]{1,0:T(8,128)(2,1)S(1)}, bf16[1056,128]{1,0:T(8,128)(2,1)S(1)}, u32[]{:S(2)}, u32[]{:S(2)}) %collective-permute-start.42) | collective-permute-done | bytes 270368 | tf_op jit(solution)/shard_map/ppermute | solution.py:44
  340.6 1.0 slice_bitcast_fusion.1
  (205 shorter events, 34.8 us)
Async XLA Ops:
  7.2 139.5 %all-gather.3.cloned.1.call-start = ((), (), s32[]{:S(2)}) async-start(), calls=%async_computation.2 | async-start | bytes 4866048 | tf_op jit(solution)/shard_map/all_gather | solution.py:496
  10.4 5.1 %copy-start.22 = (bf16[32]{0:T(256)(128)(2,1)S(1)}, bf16[32]{0:T(256)(128)(2,1)}, u32[]{:S(2)}) copy-start(bf16[32]{0:T(256)(128)(2,1)} %param.21) | copy-start | bytes 196
  11.3 4.4 %collective-permute-start = (bf16[80,384]{1,0:T(8,128)(2,1)S(1)}, bf16[80,384]{1,0:T(8,128)(2,1)S(1)}, u32[]{:S(2)}, u32[]{:S(2)}) collective-permute-start(bf16[80,384]{1,0:T(8,128)(2,1)S(1)} %concatenate.117), channel_id=1, source_target_pairs={{0,4},{4,0},{1,5},{5,1},{2,6},{6,2},{3,7},{7,3},{8,12},{12,8},{9,1... | collective-permute-start | bytes 184328 | tf_op jit(solution)/shard_map/ppermute | solution.py:44
  12.9 3.4 copy-start.9
  13.0 9.7 %collective-permute-start.3 = (bf16[3,2,176,128]{3,2,1,0:T(8,128)(2,1)S(1)}, bf16[3,2,176,128]{3,2,1,0:T(8,128)(2,1)S(1)}, u32[]{:S(2)}, u32[]{:S(2)}) collective-permute-start(bf16[3,2,176,128]{3,2,1,0:T(8,128)(2,1)S(1)} %dynamic-slice_bitcast_fusion.3), channel_id=1, source_target_pairs={{0,8},{8,0},{1,9},{9,1},{2,10},{10,2},{3,11},{11,3},{4,12},{12,4},... | collective-permute-start | bytes 811016 | tf_op jit(solution)/shard_map/ppermute | solution.py:44
  15.7 7.1 %copy-start = (bf16[256,1024]{1,0:T(8,128)(2,1)S(1)}, bf16[256,1024]{1,0:T(8,128)(2,1)}, u32[]{:S(2)}) copy-start(bf16[256,1024]{1,0:T(8,128)(2,1)} %hidden_ref.1) | copy-start | bytes 1572868
  16.4 11.1 %collective-permute-start.6 = (bf16[32,2688]{1,0:T(8,128)(2,1)S(1)}, bf16[32,2688]{1,0:T(8,128)(2,1)S(1)}, u32[]{:S(2)}, u32[]{:S(2)}) collective-permute-start(bf16[32,2688]{1,0:T(8,128)(2,1)S(1)} %pad_maximum_fusion.14), channel_id=1, source_target_pairs={{0,2},{1,3},{2,0},{3,1},{4,6},{5,7},{6,4},{7,5},{8,10},{9,11},{10,... | collective-permute-start | bytes 516104 | tf_op jit(solution)/shard_map/ppermute | solution.py:48
  22.7 6.4 %collective-permute-start.4 = (bf16[3,176,256]{2,1,0:T(8,128)(2,1)S(1)}, bf16[3,176,256]{2,1,0:T(8,128)(2,1)S(1)}, u32[]{:S(2)}, u32[]{:S(2)}) collective-permute-start(bf16[3,176,256]{2,1,0:T(8,128)(2,1)S(1)} %pad_maximum_fusion.8), channel_id=1, source_target_pairs={{0,4},{4,0},{1,5},{5,1},{2,6},{6,2},{3,7},{7,3},{8,12},{12,8},{9,1... | collective-permute-start | bytes 811016 | tf_op jit(solution)/shard_map/ppermute | solution.py:44
  22.8 7.3 %collective-permute-start.1 = (bf16[256,1024]{1,0:T(8,128)(2,1)S(1)}, bf16[256,1024]{1,0:T(8,128)(2,1)S(1)}, u32[]{:S(2)}, u32[]{:S(2)}) collective-permute-start(bf16[256,1024]{1,0:T(8,128)(2,1)S(1)} %copy-done), channel_id=1, source_target_pairs={{0,0},{2,1},{4,2},{6,3},{1,4},{3,5},{5,6},{7,7},{8,8},{10,9},{12,1... | collective-permute-start | bytes 1572872 | tf_op jit(solution)/shard_map/ppermute | solution.py:65
  23.5 28.5 %collective-permute-start.2 = (bf16[256,1024]{1,0:T(8,128)(2,1)S(1)}, bf16[256,1024]{1,0:T(8,128)(2,1)S(1)}, u32[]{:S(2)}, u32[]{:S(2)}) collective-permute-start(bf16[256,1024]{1,0:T(8,128)(2,1)S(1)} %copy-done), channel_id=1, source_target_pairs={{2,0},{0,1},{6,2},{4,3},{3,4},{1,5},{7,6},{5,7},{10,8},{8,9},{14,1... | collective-permute-start | bytes 1572872 | tf_op jit(solution)/shard_map/ppermute | solution.py:65
  28.2 25.5 %collective-permute-start.7 = (bf16[64,1920]{1,0:T(8,128)(2,1)}, bf16[64,1920]{1,0:T(8,128)(2,1)}, u32[]{:S(2)}, u32[]{:S(2)}) collective-permute-start(bf16[64,1920]{1,0:T(8,128)(2,1)} %pad_maximum_fusion.13), channel_id=1, source_target_pairs={{0,1},{1,0},{2,3},{3,2},{4,5},{5,4},{6,7},{7,6},{8,9},{9,8},{10,11... | collective-permute-start | bytes 737288 | tf_op jit(solution)/shard_map/ppermute | solution.py:48
  29.2 23.0 %copy-start.3 = (bf16[256,1024]{1,0:T(8,128)(2,1)S(1)}, bf16[256,1024]{1,0:T(8,128)(2,1)}, u32[]{:S(2)}) copy-start(bf16[256,1024]{1,0:T(8,128)(2,1)} %cot_ref.1) | copy-start | bytes 1572868
  30.1 29.1 %copy-start.13 = (bf16[256,1024]{1,0:T(8,128)(2,1)}, bf16[256,1024]{1,0:T(8,128)(2,1)S(1)}, u32[]{:S(2)}) copy-start(bf16[256,1024]{1,0:T(8,128)(2,1)S(1)} %collective-permute-done.1.h0_ref) | copy-start | bytes 1572868
  52.0 7.2 %copy-start.14 = (bf16[256,1024]{1,0:T(8,128)(2,1)}, bf16[256,1024]{1,0:T(8,128)(2,1)S(1)}, u32[]{:S(2)}) copy-start(bf16[256,1024]{1,0:T(8,128)(2,1)S(1)} %collective-permute-done.2.h1_ref) | copy-start | bytes 1572868
  52.0 252.7 %reduce-scatter.2.cloned.1.call-start = ((), (), s32[]{:S(2)}) async-start(), calls=%async_computation.1 | async-start | bytes 2703360 | tf_op jit(solution)/shard_map/reduce_scatter | solution.py:590
  52.2 12.2 %collective-permute-start.8 = (bf16[256,1024]{1,0:T(8,128)(2,1)S(1)}, bf16[256,1024]{1,0:T(8,128)(2,1)S(1)}, u32[]{:S(2)}, u32[]{:S(2)}) collective-permute-start(bf16[256,1024]{1,0:T(8,128)(2,1)S(1)} %copy-done.3), channel_id=1, source_target_pairs={{0,8},{8,0},{1,9},{9,1},{2,10},{10,2},{3,11},{11,3},{4,12},{12,4},... | collective-permute-start | bytes 1572872 | tf_op jit(solution)/shard_map/ppermute | solution.py:44
  55.7 10.3 %collective-permute-start.10 = (bf16[128,1152]{1,0:T(8,128)(2,1)S(1)}, bf16[128,1152]{1,0:T(8,128)(2,1)S(1)}, u32[]{:S(2)}, u32[]{:S(2)}) collective-permute-start(bf16[128,1152]{1,0:T(8,128)(2,1)S(1)} %bitcast.164), channel_id=1, source_target_pairs={{0,16},{16,0},{1,17},{17,1},{2,18},{18,2},{3,19},{19,3},{4,20},{20... | collective-permute-start | bytes 884744 | tf_op jit(solution)/shard_map/ppermute | solution.py:44
  59.3 23.7 %collective-permute-start.5 = (bf16[512,1024]{1,0:T(8,128)(2,1)S(1)}, bf16[512,1024]{1,0:T(8,128)(2,1)S(1)}, u32[]{:S(2)}, u32[]{:S(2)}) collective-permute-start(bf16[512,1024]{1,0:T(8,128)(2,1)S(1)} %pad_maximum_fusion.3), channel_id=1, source_target_pairs={{0,4},{4,0},{1,5},{5,1},{2,6},{6,2},{3,7},{7,3},{8,12},{12,8},{9,1... | collective-permute-start | bytes 3145736 | tf_op jit(solution)/shard_map/ppermute | solution.py:44
  64.4 1.7 copy-start.12
  64.4 6.9 %collective-permute-start.9 = (bf16[2,4,32,384]{3,0,2,1:T(2,128)(2,1)S(1)}, bf16[2,4,32,384]{3,0,2,1:T(2,128)(2,1)S(1)}, u32[]{:S(2)}, u32[]{:S(2)}) collective-permute-start(bf16[2,4,32,384]{3,0,2,1:T(2,128)(2,1)S(1)} %bitcast.190), channel_id=1, source_target_pairs={{0,8},{8,0},{1,9},{9,1},{2,10},{10,2},{3,11},{11,3},{4,12},{12,4},... | collective-permute-start | bytes 589832 | tf_op jit(solution)/shard_map/ppermute | solution.py:44
  71.2 11.4 %collective-permute-start.15 = (bf16[2,128,1152]{2,1,0:T(8,128)(2,1)S(1)}, bf16[2,128,1152]{2,1,0:T(8,128)(2,1)S(1)}, u32[]{:S(2)}, u32[]{:S(2)}) collective-permute-start(bf16[2,128,1152]{2,1,0:T(8,128)(2,1)S(1)} %maximum_select_fusion.4), channel_id=1, source_target_pairs={{0,8},{8,0},{1,9},{9,1},{2,10},{10,2},{3,11},{11,3},{4,12},{12,4},... | collective-permute-start | bytes 1769480 | tf_op jit(solution)/shard_map/ppermute | solution.py:44
  73.3 7.8 %collective-permute-start.11 = (bf16[4,4,32,384]{3,2,1,0:T(8,128)(2,1)S(1)}, bf16[4,4,32,384]{3,2,1,0:T(8,128)(2,1)S(1)}, u32[]{:S(2)}, u32[]{:S(2)}) collective-permute-start(bf16[4,4,32,384]{3,2,1,0:T(8,128)(2,1)S(1)} %bitcast.178), channel_id=1, source_target_pairs={{0,16},{16,0},{1,17},{17,1},{2,18},{18,2},{3,19},{19,3},{4,20},{20... | collective-permute-start | bytes 1179656 | tf_op jit(solution)/shard_map/ppermute | solution.py:44
  92.5 1.7 collective-permute-start.12
  94.2 2.8 collective-permute-start.16
  95.4 18.9 %collective-permute-start.14 = (bf16[256,512]{1,0:T(8,128)(2,1)S(1)}, bf16[256,512]{1,0:T(8,128)(2,1)S(1)}, u32[]{:S(2)}, u32[]{:S(2)}) collective-permute-start(bf16[256,512]{1,0:T(8,128)(2,1)S(1)} %pad_maximum_fusion.11), channel_id=1, source_target_pairs={{0,2},{1,0},{2,6},{3,4},{4,3},{5,1},{6,7},{7,5},{8,10},{9,8},{10,1... | collective-permute-start | bytes 786440 | tf_op jit(solution)/shard_map/ppermute | solution.py:61
  95.5 18.8 %collective-permute-start.13 = (bf16[256,512]{1,0:T(8,128)(2,1)S(1)}, bf16[256,512]{1,0:T(8,128)(2,1)S(1)}, u32[]{:S(2)}, u32[]{:S(2)}) collective-permute-start(bf16[256,512]{1,0:T(8,128)(2,1)S(1)} %pad_maximum_fusion.10), channel_id=1, source_target_pairs={{0,0},{1,2},{2,4},{3,6},{4,1},{5,3},{6,5},{7,7},{8,8},{9,10},{10,1... | collective-permute-start | bytes 786440 | tf_op jit(solution)/shard_map/ppermute | solution.py:61
  97.0 32.9 %collective-permute-start.18 = (bf16[512,1024]{1,0:T(8,128)(2,1)S(1)}, bf16[512,1024]{1,0:T(8,128)(2,1)S(1)}, u32[]{:S(2)}, u32[]{:S(2)}) collective-permute-start(bf16[512,1024]{1,0:T(8,128)(2,1)S(1)} %pad_maximum_fusion.5), channel_id=1, source_target_pairs={{0,4},{4,0},{1,5},{5,1},{2,6},{6,2},{3,7},{7,3},{8,12},{12,8},{9,1... | collective-permute-start | bytes 3145736 | tf_op jit(solution)/shard_map/ppermute | solution.py:44
  119.2 9.4 %collective-permute-start.17 = (bf16[256,1024]{1,0:T(8,128)(2,1)}, bf16[256,1024]{1,0:T(8,128)(2,1)S(1)}, u32[]{:S(2)}, u32[]{:S(2)}) collective-permute-start(bf16[256,1024]{1,0:T(8,128)(2,1)} %get-tuple-element.90.refs_1_), channel_id=1, source_target_pairs={{0,8},{8,0},{1,9},{9,1},{2,10},{10,2},{3,11},{11,3},{4,12},{12,4},... | collective-permute-start | bytes 1572872 | tf_op jit(solution)/shard_map/ppermute | solution.py:44
  128.6 18.1 %copy-start.15 = (bf16[256,1024]{1,0:T(8,128)(2,1)}, bf16[256,1024]{1,0:T(8,128)(2,1)S(1)}, u32[]{:S(2)}) copy-start(bf16[256,1024]{1,0:T(8,128)(2,1)S(1)} %collective-permute-done.17.refs_2_) | copy-start | bytes 1572868
  129.9 16.7 %copy-start.23 = (bf16[512,1024]{1,0:T(8,128)(2,1)}, bf16[512,1024]{1,0:T(8,128)(2,1)S(1)}, u32[]{:S(2)}) copy-start(bf16[512,1024]{1,0:T(8,128)(2,1)S(1)} %collective-permute-done.18.refs_6_) | copy-start | bytes 3145732
  130.0 16.7 %collective-permute-start.19 = (bf16[512,1024]{1,0:T(8,128)(2,1)S(1)}, bf16[512,1024]{1,0:T(8,128)(2,1)}, u32[]{:S(2)}, u32[]{:S(2)}) collective-permute-start(bf16[512,1024]{1,0:T(8,128)(2,1)S(1)} %pad_maximum_fusion.4), channel_id=1, source_target_pairs={{0,4},{4,0},{1,5},{5,1},{2,6},{6,2},{3,7},{7,3},{8,12},{12,8},{9,1... | collective-permute-start | bytes 3145736 | tf_op jit(solution)/shard_map/ppermute | solution.py:44
  178.9 2.2 collective-permute-start.20
  181.1 2.1 collective-permute-start.21
  183.2 2.4 copy-start.10
  183.2 19.9 %collective-permute-start.22 = (bf16[2,256,1024]{2,1,0:T(8,128)(2,1)}, bf16[2,256,1024]{2,1,0:T(8,128)(2,1)S(1)}, u32[]{:S(2)}, u32[]{:S(2)}) collective-permute-start(bf16[2,256,1024]{2,1,0:T(8,128)(2,1)} %get-tuple-element.100), channel_id=1, source_target_pairs={{0,4},{4,0},{1,5},{5,1},{2,6},{6,2},{3,7},{7,3},{8,12},{12,8},{9,1... | collective-permute-start | bytes 3145736 | tf_op jit(solution)/shard_map/ppermute | solution.py:44
  192.9 49.3 %collective-permute-start.26 = (bf16[4,528,512]{2,1,0:T(8,128)(2,1)}, bf16[4,528,512]{2,1,0:T(8,128)(2,1)S(1)}, u32[]{:S(2)}, u32[]{:S(2)}) collective-permute-start(bf16[4,528,512]{2,1,0:T(8,128)(2,1)} %shard_map.208), channel_id=1, source_target_pairs={{0,16},{16,0},{1,17},{17,1},{2,18},{18,2},{3,19},{19,3},{4,20},{20... | collective-permute-start | bytes 6488072 | tf_op jit(solution)/shard_map/ppermute | solution.py:44
  194.4 14.0 %collective-permute-start.23 = (bf16[256,1024]{1,0:T(8,128)(2,1)}, bf16[256,1024]{1,0:T(8,128)(2,1)S(1)}, u32[]{:S(2)}, u32[]{:S(2)}) collective-permute-start(bf16[256,1024]{1,0:T(8,128)(2,1)} %add_convert_fusion.3), channel_id=1, source_target_pairs={{0,8},{8,0},{1,9},{9,1},{2,10},{10,2},{3,11},{11,3},{4,12},{12,4},... | collective-permute-start | bytes 1572872 | tf_op jit(solution)/shard_map/ppermute | solution.py:44
  195.8 7.3 %copy-start.6 = (bf16[2,256,1024]{2,1,0:T(8,128)(2,1)S(1)}, bf16[2,256,1024]{2,1,0:T(8,128)(2,1)}, u32[]{:S(2)}) copy-start(bf16[2,256,1024]{2,1,0:T(8,128)(2,1)} %get-tuple-element.94) | copy-start | bytes 3145732
  203.1 12.0 %copy-start.7 = (bf16[2,256,1024]{2,1,0:T(8,128)(2,1)}, bf16[2,256,1024]{2,1,0:T(8,128)(2,1)S(1)}, u32[]{:S(2)}) copy-start(bf16[2,256,1024]{2,1,0:T(8,128)(2,1)S(1)} %collective-permute-done.22) | copy-start | bytes 3145732
  216.6 29.2 %collective-permute-start.28 = (bf16[2,2,4,32,1152]{4,3,2,1,0:T(8,128)(2,1)S(1)}, bf16[2,2,4,32,1152]{4,3,2,1,0:T(8,128)(2,1)}, u32[]{:S(2)}, u32[]{:S(2)}) collective-permute-start(bf16[2,2,4,32,1152]{4,3,2,1,0:T(8,128)(2,1)S(1)} %dynamic-slice_bitcast_fusion), channel_id=1, source_target_pairs={{0,4},{4,0},{1,5},{5,1},{2,6},{6,2},{3,7},{7,3},{8,12},{12,8},{9,1... | collective-permute-start | bytes 3538952 | tf_op jit(solution)/shard_map/ppermute | solution.py:44
  216.6 5.6 %collective-permute-start.25 = (bf16[256,512]{1,0:T(8,128)(2,1)}, bf16[256,512]{1,0:T(8,128)(2,1)}, u32[]{:S(2)}, u32[]{:S(2)}) collective-permute-start(bf16[256,512]{1,0:T(8,128)(2,1)} %get-tuple-element.115), channel_id=1, source_target_pairs={{0,0},{2,1},{4,2},{6,3},{1,4},{3,5},{5,6},{7,7},{8,8},{10,9},{12,1... | collective-permute-start | bytes 786440 | tf_op jit(solution)/shard_map/ppermute | solution.py:65
  220.2 13.8 %collective-permute-start.27 = (bf16[256,512]{1,0:T(8,128)(2,1)}, bf16[256,512]{1,0:T(8,128)(2,1)}, u32[]{:S(2)}, u32[]{:S(2)}) collective-permute-start(bf16[256,512]{1,0:T(8,128)(2,1)} %get-tuple-element.118), channel_id=1, source_target_pairs={{2,0},{0,1},{6,2},{4,3},{3,4},{1,5},{7,6},{5,7},{10,8},{8,9},{14,1... | collective-permute-start | bytes 786440 | tf_op jit(solution)/shard_map/ppermute | solution.py:65
  220.7 28.0 %collective-permute-start.24 = (bf16[256,1024]{1,0:T(8,128)(2,1)}, bf16[256,1024]{1,0:T(8,128)(2,1)}, u32[]{:S(2)}, u32[]{:S(2)}) collective-permute-start(bf16[256,1024]{1,0:T(8,128)(2,1)} %fusion.18), channel_id=1, source_target_pairs={{0,8},{8,0},{1,9},{9,1},{2,10},{10,2},{3,11},{11,3},{4,12},{12,4},... | collective-permute-start | bytes 1572872 | tf_op jit(solution)/shard_map/ppermute | solution.py:44
  246.7 3.5 %collective-permute-start.29 = (bf16[256,512]{1,0:T(8,128)(2,1)S(1)}, bf16[256,512]{1,0:T(8,128)(2,1)S(1)}, u32[]{:S(2)}, u32[]{:S(2)}) collective-permute-start(bf16[256,512]{1,0:T(8,128)(2,1)S(1)} %copy-done.17), channel_id=1, source_target_pairs={{0,4},{4,0},{1,5},{5,1},{2,6},{6,2},{3,7},{7,3},{8,12},{12,8},{9,1... | collective-permute-start | bytes 786440 | tf_op jit(solution)/shard_map/ppermute | solution.py:44
  248.7 19.4 %collective-permute-start.34 = (bf16[2,4,32,1152]{3,2,1,0:T(8,128)(2,1)S(1)}, bf16[2,4,32,1152]{3,2,1,0:T(8,128)(2,1)}, u32[]{:S(2)}, u32[]{:S(2)}) collective-permute-start(bf16[2,4,32,1152]{3,2,1,0:T(8,128)(2,1)S(1)} %dynamic-slice_bitcast_fusion.1), channel_id=1, source_target_pairs={{0,8},{8,0},{1,9},{9,1},{2,10},{10,2},{3,11},{11,3},{4,12},{12,4},... | collective-permute-start | bytes 1769480 | tf_op jit(solution)/shard_map/ppermute | solution.py:44
  251.0 14.4 %copy-start.1 = (bf16[256,1024]{1,0:T(8,128)(2,1)S(1)}, bf16[256,1024]{1,0:T(8,128)(2,1)}, u32[]{:S(2)}) copy-start(bf16[256,1024]{1,0:T(8,128)(2,1)} %hidden_ref.1) | copy-start | bytes 1572868
  251.0 14.6 %copy-start.2 = (f32[256,1024]{1,0:T(8,128)S(1)}, f32[256,1024]{1,0:T(8,128)}, u32[]{:S(2)}) copy-start(f32[256,1024]{1,0:T(8,128)} %get-tuple-element.88.middle_ref) | copy-start | bytes 3145732
  265.2 4.2 %collective-permute-start.30 = (bf16[2,256,1024]{2,1,0:T(8,128)(2,1)}, bf16[2,256,1024]{2,1,0:T(8,128)(2,1)}, u32[]{:S(2)}, u32[]{:S(2)}) collective-permute-start(bf16[2,256,1024]{2,1,0:T(8,128)(2,1)} %get-tuple-element.130), channel_id=1, source_target_pairs={{0,4},{4,0},{1,5},{5,1},{2,6},{6,2},{3,7},{7,3},{8,12},{12,8},{9,1... | collective-permute-start | bytes 3145736 | tf_op jit(solution)/shard_map/ppermute | solution.py:44
  269.4 2.3 copy-start.5
  269.9 11.6 %collective-permute-start.33 = (bf16[2,2,4,32,384]{4,1,3,2,0:T(2,128)(2,1)S(1)}, bf16[2,2,4,32,384]{4,1,3,2,0:T(2,128)(2,1)S(1)}, u32[]{:S(2)}, u32[]{:S(2)}) collective-permute-start(bf16[2,2,4,32,384]{4,1,3,2,0:T(2,128)(2,1)S(1)} %bitcast.205), channel_id=1, source_target_pairs={{0,16},{16,0},{1,17},{17,1},{2,18},{18,2},{3,19},{19,3},{4,20},{20... | collective-permute-start | bytes 1179656 | tf_op jit(solution)/shard_map/ppermute | solution.py:44
  273.3 11.0 %collective-permute-start.31 = (bf16[256,1024]{1,0:T(8,128)(2,1)S(1)}, bf16[256,1024]{1,0:T(8,128)(2,1)S(1)}, u32[]{:S(2)}, u32[]{:S(2)}) collective-permute-start(bf16[256,1024]{1,0:T(8,128)(2,1)S(1)} %get-tuple-element.147), channel_id=1, source_target_pairs={{0,0},{1,2},{2,4},{3,6},{4,1},{5,3},{6,5},{7,7},{8,8},{9,10},{10,1... | collective-permute-start | bytes 1572872 | tf_op jit(solution)/shard_map/ppermute | solution.py:61
  274.0 28.5 %collective-permute-start.32 = (bf16[256,1024]{1,0:T(8,128)(2,1)S(1)}, bf16[256,1024]{1,0:T(8,128)(2,1)S(1)}, u32[]{:S(2)}, u32[]{:S(2)}) collective-permute-start(bf16[256,1024]{1,0:T(8,128)(2,1)S(1)} %get-tuple-element.148), channel_id=1, source_target_pairs={{0,2},{1,0},{2,6},{3,4},{4,3},{5,1},{6,7},{7,5},{8,10},{9,8},{10,1... | collective-permute-start | bytes 1572872 | tf_op jit(solution)/shard_map/ppermute | solution.py:61
  282.1 20.8 %copy-start.4 = (f32[256,1024]{1,0:T(8,128)S(1)}, f32[256,1024]{1,0:T(8,128)}, u32[]{:S(2)}) copy-start(f32[256,1024]{1,0:T(8,128)} %get-tuple-element.114) | copy-start | bytes 3145732
  282.2 22.0 %collective-permute-start.35 = (bf16[2,4,32,384]{3,0,2,1:T(2,128)(2,1)S(1)}, bf16[2,4,32,384]{3,0,2,1:T(2,128)(2,1)S(1)}, u32[]{:S(2)}, u32[]{:S(2)}) collective-permute-start(bf16[2,4,32,384]{3,0,2,1:T(2,128)(2,1)S(1)} %dynamic-slice_bitcast_fusion.4), channel_id=1, source_target_pairs={{0,8},{8,0},{1,9},{9,1},{2,10},{10,2},{3,11},{11,3},{4,12},{12,4},... | collective-permute-start | bytes 589832 | tf_op jit(solution)/shard_map/ppermute | solution.py:44
  282.8 21.8 %collective-permute-start.36 = (bf16[4,32,1152]{2,1,0:T(8,128)(2,1)S(1)}, bf16[4,32,1152]{2,1,0:T(8,128)(2,1)S(1)}, u32[]{:S(2)}, u32[]{:S(2)}) collective-permute-start(bf16[4,32,1152]{2,1,0:T(8,128)(2,1)S(1)} %dynamic-slice_bitcast_fusion.2), channel_id=1, source_target_pairs={{0,16},{16,0},{1,17},{17,1},{2,18},{18,2},{3,19},{19,3},{4,20},{20... | collective-permute-start | bytes 884744 | tf_op jit(solution)/shard_map/ppermute | solution.py:44
  305.7 19.0 %collective-permute-start.37 = (bf16[32,1920]{1,0:T(8,128)(2,1)S(1)}, bf16[32,1920]{1,0:T(8,128)(2,1)S(1)}, u32[]{:S(2)}, u32[]{:S(2)}) collective-permute-start(bf16[32,1920]{1,0:T(8,128)(2,1)S(1)} %get-tuple-element.137), channel_id=1, source_target_pairs={{0,2},{1,3},{2,0},{3,1},{4,6},{5,7},{6,4},{7,5},{8,10},{9,11},{10,... | collective-permute-start | bytes 368648 | tf_op jit(solution)/shard_map/ppermute | solution.py:48
  318.3 6.6 %collective-permute-start.38 = (bf16[32,1920]{1,0:T(8,128)(2,1)S(1)}, bf16[32,1920]{1,0:T(8,128)(2,1)S(1)}, u32[]{:S(2)}, u32[]{:S(2)}) collective-permute-start(bf16[32,1920]{1,0:T(8,128)(2,1)S(1)} %get-tuple-element.138), channel_id=1, source_target_pairs={{0,1},{1,0},{2,3},{3,2},{4,5},{5,4},{6,7},{7,6},{8,9},{9,8},{10,11... | collective-permute-start | bytes 368648 | tf_op jit(solution)/shard_map/ppermute | solution.py:48
  318.7 9.0 %collective-permute-start.39 = (bf16[32,1920]{1,0:T(8,128)(2,1)S(1)}, bf16[32,1920]{1,0:T(8,128)(2,1)S(1)}, u32[]{:S(2)}, u32[]{:S(2)}) collective-permute-start(bf16[32,1920]{1,0:T(8,128)(2,1)S(1)} %get-tuple-element.139), channel_id=1, source_target_pairs={{0,3},{1,2},{2,1},{3,0},{4,7},{5,6},{6,5},{7,4},{8,11},{9,10},{10,... | collective-permute-start | bytes 368648 | tf_op jit(solution)/shard_map/ppermute | solution.py:48
  327.8 2.4 copy-start.16
  327.8 1.5 collective-permute-start.40
  329.4 2.0 collective-permute-start.41
  329.8 3.2 copy-start.19
  329.8 3.2 copy-start.20
  331.4 8.8 %collective-permute-start.42 = (bf16[1056,128]{1,0:T(8,128)(2,1)S(1)}, bf16[1056,128]{1,0:T(8,128)(2,1)S(1)}, u32[]{:S(2)}, u32[]{:S(2)}) collective-permute-start(bf16[1056,128]{1,0:T(8,128)(2,1)S(1)} %pad_maximum_fusion.9), channel_id=1, source_target_pairs={{0,8},{8,0},{1,9},{9,1},{2,10},{10,2},{3,11},{11,3},{4,12},{12,4},... | collective-permute-start | bytes 811016 | tf_op jit(solution)/shard_map/ppermute | solution.py:44
  (9 other events, 7.8 us)
Sparse Core Ops, SparseCore 0:
  52.2 82.9 all-gather.2
  245.9 57.8 reduce-scatter.1
where the time goes:
time: 351 us; the launch traced here: 349 us
  waiting for transfers between devices  121 us (34%)
  starting transfers between devices  82.1 us (23%)
  Pallas kernels  79.7 us (23%)
  other arithmetic  30.7 us (9%)
  local copies, waits for them, and re-layouts  18.9 us (5%)
  between operations  16.5 us (5%)
    pallas_call x7, Pallas kernels, kernel_call(): pl.pallas_call(body, out_shape=outs, in_specs=[smem] * scalars + [vmem] *...  79.7 us
    ppermute x30, waiting for transfers between devices, hop(): return lax.ppermute(block, f'bit{bit}', [(0, 1), (1, 0)])  54.4 us
    ppermute x30, starting transfers between devices, hop(): return lax.ppermute(block, f'bit{bit}', [(0, 1), (1, 0)])  47.8 us
    ppermute x4, waiting for transfers between devices, away(): lax.ppermute(block, ('bit0', 'feat'), [(b, a) for a, b in home_pairs(mask)])  32.8 us
    ppermute x4, waiting for transfers between devices, home(): return lax.ppermute(block, ('bit0', 'feat'), home_pairs(mask))  26.5 us
    ppermute x5, starting transfers between devices, cross(): return lax.ppermute(block, 'feat', [(i, i ^ mask) for i in range(GROUPS)])  17.7 us
    convert_element_type x8, other arithmetic, add_rounded(): return (first.astype(F32) + second.astype(F32)).astype(BF16)  12.1 us
    ppermute x4, starting transfers between devices, home(): return lax.ppermute(block, ('bit0', 'feat'), home_pairs(mask))  8.27 us
  transfers between devices with their start and end apart: 45, of which 25 were waited for; matrix products, arithmetic and copies ran while one was open for 11% of the time, Pallas kernels for 14%

commit v1 on v0

--- a/solution.py
+++ b/solution.py
@@ -22,6 +22,7 @@
 SLOT_MASKS = (0, 2, 1, 3)
 SPLIT_BITS = 2
 SPLIT = 1 << SPLIT_BITS
+TERM_ROWS = ((0, 256), (256, 528))
 
 
 def matmul(first_matrix, second_matrix):
@@ -92,14 +93,15 @@
     smem = pl.BlockSpec(memory_space=pltpu.SMEM)
     vmem = pl.BlockSpec(memory_space=pltpu.VMEM)
     hbm = pl.BlockSpec(memory_space=pl.ANY)
-    outs = [jax.ShapeDtypeStruct(shape, dtype) for shape, dtype in outs]
+    out_specs = [hbm if len(out) > 2 else vmem for out in outs]
+    outs = [jax.ShapeDtypeStruct(out[0], out[1]) for out in outs]
     nbytes = sum(o.size * o.dtype.itemsize for o in list(operands) + outs)
     plain = len(operands) - scalars - remote
     return pl.pallas_call(
         body,
         out_shape=outs,
         in_specs=[smem] * scalars + [vmem] * plain + [hbm] * remote,
-        out_specs=[vmem] * len(outs),
+        out_specs=out_specs,
         scratch_shapes=list(scratch),
         compiler_params=pltpu.CompilerParams(vmem_limit_bytes=limit * 1024 * 1024),
         cost_estimate=pl.CostEstimate(flops=flops, bytes_accessed=nbytes, transcendentals=0),
@@ -267,7 +269,7 @@
     width = att_ref.shape[1]
     part = g0_ref.shape[1] // 2
     gain = gain_ref[:1]
-    mlp_grad = own_ref[...].astype(F32) + near_ref[...].astype(F32) + far_ref[...].astype(F32)
+    mlp_grad = own_ref[0].astype(F32) + near_ref[0].astype(F32) + far_ref[...].astype(F32)
     middle = middle_ref[...]
     scale = lax.rsqrt(jnp.mean(middle * middle, axis=1, keepdims=True) + EPSILON)
     normed = middle * scale
@@ -285,22 +287,51 @@
     out_ref[:, width:] = jnp.broadcast_to(term, (LANES, term.shape[1])).T.astype(BF16)
 
 
-def load_units(units, piece_ref, weight_refs, sems):
-    parts, slots, _, part = piece_ref.shape
-    copies = []
-    for m, w_ref in enumerate(weight_refs):
-        for y in range(parts):
-            for s in range(slots):
-                copies.append(
-                    pltpu.make_async_copy(
-                        piece_ref.at[y, s, pl.ds(m * units, units), :],
-                        w_ref.at[pl.ds(s * units, units), pl.ds(y * part, part)],
-                        sems.at[(m * parts + y) * slots + s],
-                    )
-                )
+def start_copies(pairs, sems, first):
+    copies = [
+        pltpu.make_async_copy(source, target, sems.at[first + n])
+        for n, (source, target) in enumerate(pairs)
+    ]
     for copy in copies:
         copy.start()
     return copies
+
+
+def wait_copies(copies):
+    for copy in copies:
+        copy.wait()
+
+
+def feature_pairs(place, count, moved, own_order, device_order):
+    if not moved:
+        return [(own_order, device_order)]
+    block = own_order.shape[1] // count
+    return [
+        (own_order.at[:, block_at(place ^ j, block)], device_order.at[:, pl.ds(j * block, block)])
+        for j in range(count)
+    ]
+
+
+def row_pairs(place, count, moved, refs, out_ref):
+    pairs, low = [], 0
+    for ref in refs:
+        rows = ref.shape[0]
+        pairs += feature_pairs(place, count, moved, ref, out_ref.at[pl.ds(low, rows), :])
+        low += rows
+    return pairs
+
+
+def unit_pairs(units, piece_ref, weight_refs):
+    parts, slots, _, part = piece_ref.shape
+    return [
+        (
+            piece_ref.at[y, s, pl.ds(m * units, units), :],
+            w_ref.at[pl.ds(s * units, units), pl.ds(y * part, part)],
+        )
+        for m, w_ref in enumerate(weight_refs)
+        for y in range(parts)
+        for s in range(slots)
+    ]
 
 
 def forward_units(total, x_ref, c_ref, weight_refs, hidden_refs, put):
@@ -332,51 +363,47 @@
         put(b, branch, grad)
 
 
-def forward_body(units, count, moved, *refs):
-    me_ref, x_refs, c_refs, piece_ref, refs = refs[0], refs[1:4], refs[4:7], refs[7], refs[8:]
-    grad_refs, branch_refs, refs = refs[:SPLIT], refs[SPLIT : SPLIT + 2], refs[SPLIT + 2 :]
-    x_ref, c_ref, hidden_refs, weight_refs, sems = *refs[:2], refs[2:5], refs[5:8], refs[8]
-    copies = load_units(units, piece_ref, weight_refs, sems)
-    tokens = x_refs[0].shape[0]
-    me = me_ref[0]
-    block = x_ref.shape[1] // count
-    for (own, far, pair), ref_out in ((x_refs, x_ref), (c_refs, c_ref)):
-        for low, ref in ((0, own), (tokens, far), (2 * tokens, pair)):
-            rows = slice(low, low + ref.shape[0])
-            if moved:
-                for j in range(count):
-                    lanes = slice(j * block, (j + 1) * block)
-                    ref_out[rows, lanes] = ref[:, block_at(me ^ j, block)]
-            else:
-                ref_out[rows, :] = ref[...]
-    for copy in copies:
-        copy.wait()
-
-    def put(b, branch, grad):
-        def store(ref, value):
-            value = value.astype(BF16)
-            if moved:
-                for j in range(count):
-                    ref[:, block_at(me ^ j, block)] = value[:, j * block : (j + 1) * block]
-            else:
-                ref[...] = value
-
-        store(grad_refs[b], grad)
-        store(branch_refs[b // 2].at[b % 2], branch)
-
-    forward_units(weight_refs[0].shape[0], x_ref, c_ref, weight_refs, hidden_refs, put)
-
-
-def weights_body(units, part_ref, x_ref, c_ref, act_ref, gate_ref, up_ref, term_ref):
+def weight_units(units, index, x_ref, c_ref, hidden_refs, term_ref):
     slots, _, part = term_ref.shape
     step = min(part, 256)
+    act_ref, gate_ref, up_ref = hidden_refs
     for m, (left, right) in enumerate(((gate_ref, x_ref), (up_ref, x_ref), (act_ref, c_ref))):
         for at in range(0, part, step):
-            lanes = pl.ds(pl.multiple_of(part_ref[0] * part + at, step), step)
+            lanes = pl.ds(pl.multiple_of(index * part + at, step), step)
             out = matmul(left[...], right[:, lanes]).astype(BF16)
             rows = slice(m * units, (m + 1) * units)
             for s in range(slots):
                 term_ref[s, rows, at : at + step] = out[s * units : (s + 1) * units]
+
+
+def feed_forward_body(units, count, moved, parts, *refs):
+    spot_ref, x_refs, c_refs, piece_ref, refs = refs[0], refs[1:4], refs[4:7], refs[7], refs[8:]
+    grad_refs, branch_refs, term_refs, refs = refs[:2], refs[2:4], refs[4 : 4 + 2 * parts], refs[4 + 2 * parts :]
+    x_ref, c_ref, weight_refs, hidden_refs = refs[0], refs[1], refs[2:5], refs[5:8]
+    branch_buf, grad_buf, term_buf, sems = refs[8:]
+    place, index = spot_ref[0], spot_ref[1]
+    pairs = row_pairs(place, count, moved, x_refs, x_ref)
+    pairs += row_pairs(place, count, moved, c_refs, c_ref)
+    pairs += unit_pairs(units, piece_ref, weight_refs)
+    wait_copies(start_copies(pairs, sems, 0))
+    stores = []
+
+    def put(b, branch, grad):
+        branch_buf[b] = branch.astype(BF16)
+        grad_buf[b] = grad.astype(BF16)
+        done = feature_pairs(place, count, moved, grad_refs[b // 2].at[b % 2], grad_buf.at[b])
+        done += feature_pairs(place, count, moved, branch_refs[b // 2].at[b % 2], branch_buf.at[b])
+        done = [(source, target) for target, source in done]
+        stores.extend(start_copies(done, sems, len(pairs) + len(stores)))
+
+    forward_units(weight_refs[0].shape[0], x_ref, c_ref, weight_refs, hidden_refs, put)
+    for n in range(parts):
+        which = index if n == parts - 1 else 1 - index
+        weight_units(units, which, x_ref, c_ref, hidden_refs, term_buf.at[n])
+        for h, rows in enumerate(TERM_ROWS):
+            done = [(term_buf.at[n, :, pl.ds(rows[0], rows[1] - rows[0]), :], term_refs[2 * n + h])]
+            stores.extend(start_copies(done, sems, len(pairs) + len(stores)))
+    wait_copies(stores)
 
 
 def on_device(
@@ -403,7 +430,7 @@
     group = 2 * (member & 1) + core
     tokens, width = hidden_in.shape
     length = GROUPS * tokens
-    place_arr, member_arr, group_arr = (me % SPLIT).reshape(1), member.reshape(1), group.reshape(1)
+    member_arr, group_arr = member.reshape(1), group.reshape(1)
 
     latest = {}
 
@@ -459,14 +486,14 @@
         jnp.concatenate([flip, output_pack], axis=1),
         far[:, 2 * cols :],
     ]
-    near = cross(jnp.concatenate(flips, axis=0), 1)
+    hidden = [away(hidden_in, mask) for mask in (0, 2)]
+    near = cross(after(jnp.concatenate(flips, axis=0), *hidden), 1)
     both = [
         jnp.concatenate([same, output_pack], axis=1),
         near[:rows],
         jnp.concatenate([far[:, : 2 * cols], far[:, 4 * cols :]], axis=1),
         near[rows:],
     ]
-    hidden = [away(hidden_in, mask) for mask in (0, 2)]
     both = after(place(both, [member ^ m for m in range(GROUPS)]), *hidden)
     hidden_units = down_weight.shape[0]
     units = -(-hidden_units // (16 * SPLIT)) * 16
@@ -480,9 +507,6 @@
     sent = swap_bit(jnp.concatenate([pick(part, 1 - core, 1) for part in kept], axis=2), 0)
     kept = [pick(part, core, 1) for part in kept]
     own = jnp.concatenate([kept[0], sent[:, :, :block], kept[1], sent[:, :, block:]], axis=2)
-    own = own.reshape(3 * units, SPLIT * block)
-    cot_far = swap_bit(cotangent, 1)
-
     output_mat = both[:, :, 2 * cols :].reshape(GROUPS * rows, -1)
     output_mat = pair_up((me >> links[-1]) & 1, output_mat, swap_bit(output_mat, links[-1]), 0)
     attn_mat = both[:, :, : 2 * cols].reshape(GROUPS, rows, 2, cols).transpose(2, 0, 1, 3)
@@ -493,14 +517,14 @@
     hidden_pair = swap_bit(jnp.concatenate(hidden, axis=0), 0)
 
     far_axes = dp[: bits - SPLIT_BITS] + ("feat",)
-    pieces = lax.all_gather(after(own, *hidden), far_axes)
+
+    pieces = lax.all_gather(after(own.reshape(3 * units, SPLIT * block), *hidden), far_axes)
     pieces = pieces.reshape(-1, GROUPS, 3 * units, SPLIT * block)
     if not aligned:
         pieces = pieces.transpose(1, 2, 0, 3).reshape(1, GROUPS, 3 * units, width)
 
     def pair_with(own, far):
         return [own, far, swap_bit(jnp.concatenate([own, far], axis=0), 0)]
-
 
     hr, qkv, out, sent, attf, rden = kernel_call(
         front_body,
@@ -513,7 +537,10 @@
         flops=8 * 2**30,
     )
     sent = swap_bit(sent, 0)
-    for axis, bit in enumerate(links[-2::-1] + [0], 1):
+    for axis, bit in enumerate(links[-2::-1], 1):
+        output_mat = pair_up((me >> bit) & 1, output_mat, swap_bit(output_mat, bit), axis)
+    cot_far = swap_bit(cotangent, 1)
+    for axis, bit in ((len(links), 0),):
         output_mat = pair_up((me >> bit) & 1, output_mat, swap_bit(output_mat, bit), axis)
     output_mat = output_mat.reshape(width, -1)
     cots = pair_with(cotangent, cot_far)
@@ -539,62 +566,59 @@
         swap = lambda v: jnp.take(
             v.reshape(v.shape[:-1] + (size, block)), order, axis=v.ndim - 1
         ).reshape(v.shape)
-    rows_shape = ((SPLIT * tokens, width), BF16)
-
-    hidden_shape = (GROUPS * units, SPLIT * tokens)
-    *grads, branch, branch_sent, x_all, c_all, act_t, gate_t, up_t = kernel_call(
-        partial(forward_body, units, size, aligned),
-        [((tokens, width), BF16)] * SPLIT
-        + [((2, tokens, width), BF16)] * 2
-        + [rows_shape] * 2
-        + [(hidden_shape, BF16)] * 3,
-        (place_arr, *[swap(v) for v in mlps], *[swap(v) for v in cots], pieces),
+    rows_scratch = pltpu.VMEM((SPLIT * tokens, width), BF16)
+    blocks = (SPLIT, tokens, width)
+    blocks_scratch = pltpu.VMEM(blocks, BF16)
+    parts = pieces.shape[0]
+    part = me >> SPLIT_BITS if parts == 2 else jnp.zeros((), jnp.int32)
+    spot = jnp.stack([me % SPLIT, part])
+    sems = pltpu.SemaphoreType.DMA((160,))
+    sources = [swap(v) for v in mlps + cots]
+
+    term_shape = (GROUPS, 3 * units, width // parts)
+    outs = kernel_call(
+        partial(feed_forward_body, units, size, aligned, parts),
+        [((2, tokens, width), BF16, True)] * 4
+        + [((GROUPS, high - low, width // parts), BF16, True) for low, high in TERM_ROWS] * parts,
+        (spot, *sources, pieces),
         scalars=1,
-        remote=1,
+        remote=7,
         scratch=(
+            rows_scratch,
+            rows_scratch,
             *[pltpu.VMEM((GROUPS * units, width), BF16)] * 3,
-            pltpu.SemaphoreType.DMA((3 * GROUPS * pieces.shape[0],)),
+            *[pltpu.VMEM((GROUPS * units, SPLIT * tokens), BF16)] * 3,
+            blocks_scratch,
+            blocks_scratch,
+            pltpu.VMEM((parts,) + term_shape, BF16),
+            sems,
         ),
-        flops=12 * 2**30,
-    )
-    branch, branch_sent, grads = swap(branch), swap(branch_sent), [swap(v) for v in grads]
-    grad_far = add_rounded(grads[1], swap_bit(grads[3], 0))
-    grad_near = swap_bit(grads[2], 0)
-    x_all = after(x_all, grad_far)
-    grad_far = swap_bit(grad_far, 1)
+        flops=20 * 2**30,
+    )
+    grads, grads_sent, branch, branch_sent = [swap(v) for v in outs[:4]]
+    terms = outs[4:]
+    grads_sent = swap_bit(grads_sent, 0)
+    grad_far = swap_bit(add_rounded(grads[1], grads_sent[1]), 1)
     branch_sent = swap_bit(branch_sent, 0)
     branch_sum = add_rounded(branch[1], branch_sent[1])
     branch_far = swap_bit(branch_sum, 1)
-    parts = pieces.shape[0]
-
-    def weight_terms(part):
-        (term,) = kernel_call(
-            partial(weights_body, units),
-            [((GROUPS, 3 * units, width // parts), BF16)],
-            (part.reshape(1), x_all, c_all, act_t, gate_t, up_t),
-            scalars=1,
-            flops=6 * 2**30 // parts,
-        )
-        return term
-
-    if parts == 2:
-        part = me >> SPLIT_BITS
-        term_sent, term = weight_terms(1 - part), weight_terms(part)
-        term_sum = add_rounded(term, swap_bit(term_sent, SPLIT_BITS))
-    else:
+    def reduce_terms(terms):
+        if parts == 2:
+            return add_rounded(terms[1], swap_bit(terms[0], SPLIT_BITS))
         far_bits = list(range(SPLIT_BITS, bits))[::-1]
-        term = weight_terms(jnp.zeros((), jnp.int32))
-        term_sum = term.reshape(GROUPS, 3 * units, -1, SPLIT * block).transpose(2, 0, 1, 3)
-        term_sum = term_sum.reshape((2,) * len(far_bits) + term_sum.shape[1:])
-        term_sum = reduce_bits(term_sum, far_bits, far_bits)
-    total = lax.psum_scatter(term_sum, "feat")
+        term = terms[0].reshape(GROUPS, terms[0].shape[1], -1, SPLIT * block).transpose(2, 0, 1, 3)
+        return reduce_bits(term.reshape((2,) * len(far_bits) + term.shape[1:]), far_bits, far_bits)
+
+    terms = [after(term, grad_far) if n >= 2 * (parts - 1) else term for n, term in enumerate(terms)]
+    sums = [reduce_terms(terms[h::2]) for h in range(2)]
+    totals = [lax.psum_scatter(term, "feat") for term in sums]
 
     middle_grad, *att_grad, output_term = kernel_call(
         middle_back_body,
         [((tokens, width), F32)]
         + [((tokens, 2 * vw), BF16)] * 2
         + [((width, H * DV + LANES), BF16)],
-        (member_arr, grads[0], grad_near, after(grad_far, term, branch_sum), middle, gain8, cotangent, attended, output_mat),
+        (member_arr, grads, grads_sent, after(grad_far, branch_sum), middle, gain8, cotangent, attended, output_mat),
         scalars=1,
         scratch=(pltpu.VMEM((tokens, H * DV), BF16),),
         flops=2**30,
@@ -603,9 +627,9 @@
     output_term = output_term.reshape((2,) * bits + (GROUPS, rows, H * DV + LANES))
     output_term = reduce_bits(output_term, [0], range(bits))
     att_sent = jnp.concatenate([part[:, vw:] for part in att_grad], axis=1)
-    att_grad.append(swap_bit(att_sent, 0))
+    att_grad.append(swap_bit(after(att_sent, sums[0]), 0))
     output_term = reduce_bits(output_term, links[:1], links)
-    att_grad = [after(part, term_sum) for part in att_grad]
+    att_grad = [after(part, *sums) for part in att_grad]
     input_parts, input_sent, attn_term = kernel_call(
         back_body,
         [((2, tokens, width), BF16)] * 2 + [((width, cols), BF16)],
@@ -621,7 +645,7 @@
         flops=12 * 2**30,
     )
     input_sent = swap_bit(input_sent, 0)
-    input_parts = [add_rounded(input_parts[k], input_sent[k]) for k in range(2)]
+    input_parts = [after(add_rounded(input_parts[k], input_sent[k]), *totals) for k in range(2)]
     input_parts = [home(input_parts[0], 0), home(input_parts[1], 2)]
     scaled_grad = input_parts[0].astype(F32) + input_parts[1].astype(F32)
     residual = hidden_in.astype(F32)
@@ -630,6 +654,14 @@
     inner = jnp.mean(normed * scaled_grad, axis=1, keepdims=True)
     input_grad = middle_grad + scale * (scaled_grad - normed * inner)
 
+    total = jnp.concatenate(totals, axis=0).astype(F32)
+    lanes = [slice(j * block, (j + 1) * block) for j in range(SPLIT)]
+
+    def share_total():
+        near = swap_bit(jnp.concatenate([total[:, lanes[1]], total[:, lanes[3]]], axis=1), 0)
+        far = jnp.concatenate([total[:, lanes[2]], near[:, block:]], axis=0).astype(BF16)
+        return near, swap_bit(far, 1).astype(F32)
+
     attn_term = after(attn_term, input_sent).reshape((2,) * len(links) + (2, GROUPS, rows, cols))
     attn_term = reduce_bits(attn_term, links[:0:-1], links)
     output_term = reduce_bits(output_term, links[1:], links[1:])
@@ -637,13 +669,15 @@
     attn_term = attn_term.transpose(1, 2, 0, 3).reshape(GROUPS, rows, 2 * cols)
     both = jnp.concatenate([attn_term, output_term], axis=2)
     both = [pick(both, member ^ m) for m in range(GROUPS)]
-    both = [both[0]] + [cross(after(both[m], total), m) for m in range(1, GROUPS)]
+    both = [both[0]] + [cross(after(both[m], *totals), m) for m in range(1, GROUPS)]
     output_sum = sum(part[:, 2 * cols :].astype(F32) for part in both)
     output_grad = output_sum[:, : H * DV].T
     mlp_gain_grad = output_sum[:, H * DV]
     same = both[0][:, : 2 * cols].astype(F32) + both[2][:, : 2 * cols].astype(F32)
     flip = both[1][:, : 2 * cols].astype(F32) + both[3][:, : 2 * cols].astype(F32)
     halves = pair_up(member & 1, same, flip, 0).reshape(2, rows, 2, cols)
+    near, far = share_total()
+    halves = after(halves, far)
     halves = pair_up(core, pick(halves, core, 2), swap_bit(pick(halves, 1 - core, 2), 0), 1)
     attn_grad = halves.reshape(GROUPS, rows, cols).transpose(1, 0, 2)
     scale_rows = gain_attn.astype(F32)[:, None]
@@ -663,11 +697,6 @@
         + branch_far.astype(F32)
     ).astype(BF16)
 
-    total = total.astype(F32)
-    lanes = [slice(j * block, (j + 1) * block) for j in range(SPLIT)]
-    near = swap_bit(jnp.concatenate([total[:, lanes[1]], total[:, lanes[3]]], axis=1), 0)
-    far = jnp.concatenate([total[:, lanes[2]], near[:, block:]], axis=0).astype(BF16)
-    far = swap_bit(far, 1).astype(F32)
     shares = [total[:, lanes[0]], near[:, :block], far[: 3 * units], far[3 * units :]]
     shares = [jnp.where(core == 0, shares[k], shares[k ^ 1]) for k in range(SPLIT)]
     shares = [jnp.where(side == 0, shares[k], shares[k ^ 2]) for k in range(SPLIT)]

time: 351 us -> 325 us (0.926)
  starting transfers between devices: 82.1 us -> 68.6 us
  Pallas kernels: 79.7 us -> 68.1 us
  waiting for transfers between devices: 121 us -> 126 us
    ppermute x4, waiting for transfers between devices: 32.8 us -> 8.81 us  [away(): lax.ppermute(block, ('bit0', 'feat'), [(b, a) for a, b in home_pairs(mask)])]
    ppermute x5, waiting for transfers between devices: 7.03 us -> 28.7 us  [cross(): return lax.ppermute(block, 'feat', [(i, i ^ mask) for i in range(GROUPS)])]
    ppermute x30, waiting for transfers between devices: 54.4 us -> 75.8 us  [hop(): return lax.ppermute(block, f'bit{bit}', [(0, 1), (1, 0)])]
    ppermute x4, waiting for transfers between devices: 26.5 us -> 9.45 us  [home(): return lax.ppermute(block, ('bit0', 'feat'), home_pairs(mask))]
    ppermute x30, starting transfers between devices: 47.8 us -> 36.2 us  [hop(): return lax.ppermute(block, f'bit{bit}', [(0, 1), (1, 0)])]
    pallas_call x7 -> x5, Pallas kernels: 79.7 us -> 68.1 us  [kernel_call(): pl.pallas_call(body, out_shape=outs, in_specs=[smem] * scalars + [vmem] *...]
    ppermute x4, starting transfers between devices: 8.16 us -> 11.7 us  [away(): lax.ppermute(block, ('bit0', 'feat'), [(b, a) for a, b in home_pairs(mask)])]
    convert_element_type x8 -> x9, other arithmetic: 12.1 us -> 9.63 us  [add_rounded(): return (first.astype(F32) + second.astype(F32)).astype(BF16)]
  transfers between devices with their start and end apart: 45 -> 46, of which waited for: 25 -> 19; matrix products, arithmetic and copies ran while one was open for 11% -> 11% of each run, Pallas kernels for 14% -> 10%
where the time goes in v1:
time: 325 us; the launch traced here: 323 us
  waiting for transfers between devices  126 us (39%)
  starting transfers between devices  68.6 us (21%)
  Pallas kernels  68.1 us (21%)
  other arithmetic  27.5 us (8%)
  between operations  16.3 us (5%)
  local copies, waits for them, and re-layouts  16 us (5%)
    ppermute x30, waiting for transfers between devices, hop(): return lax.ppermute(block, f'bit{bit}', [(0, 1), (1, 0)])  75.8 us
    pallas_call x5, Pallas kernels, kernel_call(): pl.pallas_call(body, out_shape=outs, in_specs=[smem] * scalars + [vmem] *...  68.1 us
    ppermute x30, starting transfers between devices, hop(): return lax.ppermute(block, f'bit{bit}', [(0, 1), (1, 0)])  36.2 us
    ppermute x5, waiting for transfers between devices, cross(): return lax.ppermute(block, 'feat', [(i, i ^ mask) for i in range(GROUPS)])  28.7 us
    ppermute x5, starting transfers between devices, cross(): return lax.ppermute(block, 'feat', [(i, i ^ mask) for i in range(GROUPS)])  14.3 us
    ppermute x4, starting transfers between devices, away(): lax.ppermute(block, ('bit0', 'feat'), [(b, a) for a, b in home_pairs(mask)])  11.7 us
    convert_element_type x9, other arithmetic, add_rounded(): return (first.astype(F32) + second.astype(F32)).astype(BF16)  9.63 us
    ppermute x4, waiting for transfers between devices, home(): return lax.ppermute(block, ('bit0', 'feat'), home_pairs(mask))  9.45 us
  transfers between devices with their start and end apart: 46, of which 19 were waited for; matrix products, arithmetic and copies ran while one was open for 11% of the time, Pallas kernels for 10%

profile of v1, /device:TPU:0, one launch (start us, length us, event | category | flops | bytes accessed | tf_op | source)
XLA Modules:
  0.0 322.7 jit_solution(14601191677103058623)
XLA Ops:
  7.2 1.7 collective-permute-start.1
  8.9 3.3 %collective-permute-start.2 = (bf16[256,1024]{1,0:T(8,128)(2,1)}, bf16[256,1024]{1,0:T(8,128)(2,1)S(1)}, u32[]{:S(2)}, u32[]{:S(2)}) collective-permute-start(bf16[256,1024]{1,0:T(8,128)(2,1)} %hidden_ref.1), channel_id=1, source_target_pairs={{2,0},{0,1},{6,2},{4,3},{3,4},{1,5},{7,6},{5,7},{10,8},{8,9},{14,1... | collective-permute-start | bytes 1572872 | tf_op jit(solution)/shard_map/ppermute | solution.py:66
  16.3 2.2 collective-permute-start
  18.5 1.1 fusion.18
  19.6 1.6 collective-permute-start.3
  22.2 5.9 %collective-permute-done.3 = bf16[3,2,176,128]{3,2,1,0:T(8,128)(2,1)S(1)} collective-permute-done((bf16[3,2,176,128]{3,2,1,0:T(8,128)(2,1)S(1)}, bf16[3,2,176,128]{3,2,1,0:T(8,128)(2,1)S(1)}, u32[]{:S(2)}, u32[]{:S(2)}) %collective-permute-start.3) | collective-permute-done | bytes 270368 | tf_op jit(solution)/shard_map/ppermute | solution.py:45
  28.3 16.9 %collective-permute-done.6 = bf16[32,2688]{1,0:T(8,128)(2,1)S(1)} collective-permute-done((bf16[32,2688]{1,0:T(8,128)(2,1)S(1)}, bf16[32,2688]{1,0:T(8,128)(2,1)S(1)}, u32[]{:S(2)}, u32[]{:S(2)}) %collective-permute-start.6) | collective-permute-done | bytes 172064 | tf_op jit(solution)/shard_map/ppermute | solution.py:49
  45.5 1.0 pad_maximum_fusion.7
  46.6 5.0 %collective-permute-done.7 = bf16[64,1920]{1,0:T(8,128)(2,1)S(1)} collective-permute-done((bf16[64,1920]{1,0:T(8,128)(2,1)S(1)}, bf16[64,1920]{1,0:T(8,128)(2,1)S(1)}, u32[]{:S(2)}, u32[]{:S(2)}) %collective-permute-start.7) | collective-permute-done | bytes 245792 | tf_op jit(solution)/shard_map/ppermute | solution.py:49
  51.7 1.6 collective-permute-start.8
  53.3 1.6 collective-permute-start.9
  56.3 1.2 collective-permute-done.8
  58.1 9.8 %collective-permute-done.9 = bf16[128,1152]{1,0:T(8,128)(2,1)S(1)} collective-permute-done((bf16[128,1152]{1,0:T(8,128)(2,1)S(1)}, bf16[128,1152]{1,0:T(8,128)(2,1)S(1)}, u32[]{:S(2)}, u32[]{:S(2)}) %collective-permute-start.9) | collective-permute-done | bytes 294944 | tf_op jit(solution)/shard_map/ppermute | solution.py:45
  68.1 2.0 collective-permute-start.10
  70.3 5.6 %collective-permute-done.10 = bf16[4,4,32,384]{3,2,1,0:T(8,128)(2,1)S(1)} collective-permute-done((bf16[4,4,32,384]{3,2,1,0:T(8,128)(2,1)S(1)}, bf16[4,4,32,384]{3,2,1,0:T(8,128)(2,1)S(1)}, u32[]{:S(2)}, u32[]{:S(2)}) %collective-permute-start.10) | collective-permute-done | bytes 393248 | tf_op jit(solution)/shard_map/ppermute | solution.py:45
  75.9 1.1 maximum_select_fusion.2
  77.0 1.0 copy-done.25
  78.0 8.5 %shard_map.203 = (bf16[4,256,1024]{2,1,0:T(8,128)(2,1)}, bf16[1024,384]{1,0:T(8,128)(2,1)}, bf16[256,512]{1,0:T(8,128)(2,1)}, bf16[256,512]{1,0:T(8,128)(2,1)}, ...) custom-call(s32[1]{0:T(128)S(6)} %select_n.253.first_ref, s32[1]{0:T(128)} %bitcast.7.group_ref, bf16[256,1024]{1,0:T(8,128)(2,1)} %copy-done.16, ...), custom_call_target="tpu_custom_call" | custom-call | flops 8589934592 | bytes 8388616 | tf_op jit(solution)/shard_map/pallas_call | solution.py:100
  86.5 1.0 fusion.41
  87.5 2.0 collective-permute-start.16
  90.5 1.4 collective-permute-start.13
  91.9 0.9 collective-permute-start.12
  92.8 9.3 %collective-permute-done.16.refs_5_ = bf16[256,1024]{1,0:T(8,128)(2,1)S(1)} collective-permute-done((bf16[256,1024]{1,0:T(8,128)(2,1)S(1)}, bf16[256,1024]{1,0:T(8,128)(2,1)S(1)}, u32[]{:S(2)}, u32[]{:S(2)}) %collective-permute-start.16) | collective-permute-done | bytes 524320 | tf_op jit(solution)/shard_map/ppermute | solution.py:45
  102.3 1.8 maximum_select_fusion
  104.1 5.4 %collective-permute-done.13.a1_ref = bf16[256,512]{1,0:T(8,128)(2,1)S(1)} collective-permute-done((bf16[256,512]{1,0:T(8,128)(2,1)S(1)}, bf16[256,512]{1,0:T(8,128)(2,1)S(1)}, u32[]{:S(2)}, u32[]{:S(2)}) %collective-permute-start.13) | collective-permute-done | bytes 262176 | tf_op jit(solution)/shard_map/ppermute | solution.py:62
  110.3 4.2 %shard_map.204 = (f32[256,1024]{1,0:T(8,128)}, bf16[256,1024]{1,0:T(8,128)(2,1)}, bf16[256,1024]{1,0:T(8,128)(2,1)}, f32[8,1024]{1,0:T(8,128)}) custom-call(s32[1]{0:T(128)} %bitcast.member_ref, bf16[256,512]{1,0:T(8,128)(2,1)} %copy-done.27, bf16[256,512]{1,0:T(8,128)(2,1)} %copy-done.26, bf16[256,1024]{1,0:T(8,128)(2,1)} %hidden_ref.1, ...), custom_call_target="tpu_custom_call" | custom-call | flops 1073741824 | bytes 5537796 | tf_op jit(solution)/shard_map/pallas_call | solution.py:100
  115.2 8.7 %collective-permute-done.17.refs_2_ = bf16[256,1024]{1,0:T(8,128)(2,1)S(1)} collective-permute-done((bf16[256,1024]{1,0:T(8,128)(2,1)}, bf16[256,1024]{1,0:T(8,128)(2,1)S(1)}, u32[]{:S(2)}, u32[]{:S(2)}) %collective-permute-start.17) | collective-permute-done | bytes 524320 | tf_op jit(solution)/shard_map/ppermute | solution.py:45
  123.9 1.3 pad_maximum_fusion.4
  125.2 9.9 %collective-permute-start.19 = (bf16[512,1024]{1,0:T(8,128)(2,1)S(1)}, bf16[512,1024]{1,0:T(8,128)(2,1)}, u32[]{:S(2)}, u32[]{:S(2)}) collective-permute-start(bf16[512,1024]{1,0:T(8,128)(2,1)S(1)} %pad_maximum_fusion.4), channel_id=1, source_target_pairs={{0,4},{4,0},{1,5},{5,1},{2,6},{6,2},{3,7},{7,3},{8,12},{12,8},{9,1... | collective-permute-start | bytes 3145736 | tf_op jit(solution)/shard_map/ppermute | solution.py:45
  135.7 1.8 collective-permute-done.19.refs_3_
  137.5 34.9 %shard_map.205 = (bf16[2,256,1024]{2,1,0:T(8,128)(2,1)}, bf16[2,256,1024]{2,1,0:T(8,128)(2,1)}, bf16[2,256,1024]{2,1,0:T(8,128)(2,1)}, bf16[2,256,1024]{2,1,0:T(...) custom-call(s32[2]{0:T(128)} %pad_add_fusion.refs_0_, ...), custom_call_target="tpu_custom_call" | custom-call | flops 21474836480 | bytes 17039368 | tf_op jit(solution)/shard_map/pallas_call | solution.py:100
  172.9 2.7 collective-permute-start.25
  175.6 1.6 fusion.20
  177.8 13.4 %collective-permute-done.22.far_ref = bf16[256,1024]{1,0:T(8,128)(2,1)S(1)} collective-permute-done((bf16[256,1024]{1,0:T(8,128)(2,1)S(1)}, bf16[256,1024]{1,0:T(8,128)(2,1)S(1)}, u32[]{:S(2)}, u32[]{:S(2)}) %collective-permute-start.22) | collective-permute-done | bytes 524320 | tf_op jit(solution)/shard_map/ppermute | solution.py:45
  192.1 7.2 %collective-permute-done.25 = bf16[4,256,512]{2,1,0:T(8,128)(2,1)S(1)} collective-permute-done((bf16[4,256,512]{2,1,0:T(8,128)(2,1)}, bf16[4,256,512]{2,1,0:T(8,128)(2,1)S(1)}, u32[]{:S(2)}, u32[]{:S(2)}) %collective-permute-start.25) | collective-permute-done | bytes 1048608 | tf_op jit(solution)/shard_map/ppermute | solution.py:45
  199.2 1.3 add_convert_fusion.1
  200.6 1.8 collective-permute-start.26
  202.5 1.1 fusion.19
  203.6 6.4 %shard_map.206 = (f32[256,1024]{1,0:T(8,128)}, bf16[256,512]{1,0:T(8,128)(2,1)}, bf16[256,512]{1,0:T(8,128)(2,1)}, bf16[1024,1152]{1,0:T(8,128)(2,1)}) custom-call(s32[1]{0:T(128)} %bitcast.member_ref, bf16[2,256,1024]{2,1,0:T(8,128)(2,1)} %get-tuple-element.103.own_ref, bf16[2,256,1024]{2,1,0:T(8,128)(2,1)} %copy-done.2, bf16[256,1024]{1,0:T(8,128)(2,1)} %copy-done.15, ...), custom_call_target="tpu_custom_call" | custom-call | flops 1073741824 | bytes 11042820 | tf_op jit(solution)/shard_map/pallas_call | solution.py:100
  210.0 1.5 dynamic-slice_bitcast_fusion
  212.2 3.6 %collective-permute-start.24 = (bf16[256,512]{1,0:T(8,128)(2,1)}, bf16[256,512]{1,0:T(8,128)(2,1)}, u32[]{:S(2)}, u32[]{:S(2)}) collective-permute-start(bf16[256,512]{1,0:T(8,128)(2,1)} %get-tuple-element.110), channel_id=1, source_target_pairs={{0,0},{2,1},{4,2},{6,3},{1,4},{3,5},{5,6},{7,7},{8,8},{10,9},{12,1... | collective-permute-start | bytes 786440 | tf_op jit(solution)/shard_map/ppermute | solution.py:66
  215.7 3.1 collective-permute-start.27
  218.8 8.3 %collective-permute-done.26 = bf16[4,272,512]{2,1,0:T(8,128)(2,1)} collective-permute-done((bf16[4,272,512]{2,1,0:T(8,128)(2,1)}, bf16[4,272,512]{2,1,0:T(8,128)(2,1)}, u32[]{:S(2)}, u32[]{:S(2)}) %collective-permute-start.26) | collective-permute-done | bytes 1114144 | tf_op jit(solution)/shard_map/ppermute | solution.py:45
  227.1 2.6 add_convert_fusion
  229.7 1.0 slice.224
  230.7 8.8 %collective-permute-done.27.g1_ref = bf16[256,512]{1,0:T(8,128)(2,1)} collective-permute-done((bf16[256,512]{1,0:T(8,128)(2,1)}, bf16[256,512]{1,0:T(8,128)(2,1)}, u32[]{:S(2)}, u32[]{:S(2)}) %collective-permute-start.27) | collective-permute-done | bytes 262176 | tf_op jit(solution)/shard_map/ppermute | solution.py:66
  240.5 2.5 fusion.13
  243.0 1.6 fusion
  244.7 1.6 collective-permute-start.34
  247.0 14.1 %shard_map.207 = (bf16[2,256,1024]{2,1,0:T(8,128)(2,1)}, bf16[2,256,1024]{2,1,0:T(8,128)(2,1)}, bf16[1024,384]{1,0:T(8,128)(2,1)}) custom-call(s32[1]{0:T(128)S(6)} %select_n.253.first_ref, s32[1]{0:T(128)} %bitcast.7.group_ref, bf16[256,512]{1,0:T(8,128)(2,1)} %collective-permute-done.24.g0_ref, bf16[256,512]{1,0:T(8,128)(2,1)} %collective-permute-done.27.g1_ref, ...), custom_call_target="tpu_custom_call" | custom-call | flops 12884901888 | bytes 9437192 | tf_op jit(solution)/shard_map/pallas_call | solution.py:100
  262.2 3.5 %reduce-scatter.5.cloned.1.call-done = bf16[1,272,512]{2,1,0:T(8,128)(2,1)} async-done(((bf16[4,272,512]{2,1,0:T(8,128)(2,1)}), bf16[1,272,512]{2,1,0:T(8,128)(2,1)}) %reduce-scatter.5.cloned.1.call-update) | async-done | bytes 278544 | tf_op jit(solution)/shard_map/reduce_scatter | solution.py:614
  265.7 1.2 fusion.16
  267.6 1.5 collective-permute-start.33
  270.4 3.2 collective-permute-start.32
  273.8 4.5 %collective-permute-done.33 = bf16[2,2,4,32,384]{4,1,3,2,0:T(2,128)(2,1)S(1)} collective-permute-done((bf16[2,2,4,32,384]{4,1,3,2,0:T(2,128)(2,1)S(1)}, bf16[2,2,4,32,384]{4,1,3,2,0:T(2,128)(2,1)S(1)}, u32[]{:S(2)}, u32[]{:S(2)}) %collective-permute-start.33) | collective-permute-done | bytes 393248 | tf_op jit(solution)/shard_map/ppermute | solution.py:45
  279.0 1.5 collective-permute-start.35
  280.6 1.5 collective-permute-start.36
  282.1 4.0 %collective-permute-done.32 = bf16[256,1024]{1,0:T(8,128)(2,1)S(1)} collective-permute-done((bf16[256,1024]{1,0:T(8,128)(2,1)S(1)}, bf16[256,1024]{1,0:T(8,128)(2,1)S(1)}, u32[]{:S(2)}, u32[]{:S(2)}) %collective-permute-start.32) | collective-permute-done | bytes 524320 | tf_op jit(solution)/shard_map/ppermute | solution.py:62
  286.4 1.3 fusion.10
  288.3 12.1 %collective-permute-start.37 = (bf16[32,1920]{1,0:T(8,128)(2,1)S(1)}, bf16[32,1920]{1,0:T(8,128)(2,1)S(1)}, u32[]{:S(2)}, u32[]{:S(2)}) collective-permute-start(bf16[32,1920]{1,0:T(8,128)(2,1)S(1)} %get-tuple-element.142), channel_id=1, source_target_pairs={{0,2},{1,3},{2,0},{3,1},{4,6},{5,7},{6,4},{7,5},{8,10},{9,11},{10,... | collective-permute-start | bytes 368648 | tf_op jit(solution)/shard_map/ppermute | solution.py:49
  300.5 1.5 collective-permute-start.41
  303.5 4.3 %collective-permute-done.37 = bf16[32,1920]{1,0:T(8,128)(2,1)S(1)} collective-permute-done((bf16[32,1920]{1,0:T(8,128)(2,1)S(1)}, bf16[32,1920]{1,0:T(8,128)(2,1)S(1)}, u32[]{:S(2)}, u32[]{:S(2)}) %collective-permute-start.37) | collective-permute-done | bytes 122912 | tf_op jit(solution)/shard_map/ppermute | solution.py:49
  307.8 2.5 collective-permute-done.38
  311.6 1.0 slice_bitcast_fusion.1
  (210 shorter events, 24.8 us)
Async XLA Ops:
  7.2 130.3 %all-gather.3.cloned.1.call-start = ((), (), s32[]{:S(2)}) async-start(), calls=%async_computation.4 | async-start | bytes 4866048 | tf_op jit(solution)/shard_map/all_gather | solution.py:521
  7.2 38.1 %collective-permute-start.1 = (bf16[256,1024]{1,0:T(8,128)(2,1)}, bf16[256,1024]{1,0:T(8,128)(2,1)S(1)}, u32[]{:S(2)}, u32[]{:S(2)}) collective-permute-start(bf16[256,1024]{1,0:T(8,128)(2,1)} %hidden_ref.1), channel_id=1, source_target_pairs={{0,0},{2,1},{4,2},{6,3},{1,4},{3,5},{5,6},{7,7},{8,8},{10,9},{12,1... | collective-permute-start | bytes 1572872 | tf_op jit(solution)/shard_map/ppermute | solution.py:66
  8.9 36.4 %collective-permute-start.2 = (bf16[256,1024]{1,0:T(8,128)(2,1)}, bf16[256,1024]{1,0:T(8,128)(2,1)S(1)}, u32[]{:S(2)}, u32[]{:S(2)}) collective-permute-start(bf16[256,1024]{1,0:T(8,128)(2,1)} %hidden_ref.1), channel_id=1, source_target_pairs={{2,0},{0,1},{6,2},{4,3},{3,4},{1,5},{7,6},{5,7},{10,8},{8,9},{14,1... | collective-permute-start | bytes 1572872 | tf_op jit(solution)/shard_map/ppermute | solution.py:66
  15.4 5.8 %copy-start.23 = (bf16[32]{0:T(256)(128)(2,1)S(1)}, bf16[32]{0:T(256)(128)(2,1)}, u32[]{:S(2)}) copy-start(bf16[32]{0:T(256)(128)(2,1)} %param.21) | copy-start | bytes 196
  16.3 5.1 %collective-permute-start = (bf16[80,384]{1,0:T(8,128)(2,1)S(1)}, bf16[80,384]{1,0:T(8,128)(2,1)S(1)}, u32[]{:S(2)}, u32[]{:S(2)}) collective-permute-start(bf16[80,384]{1,0:T(8,128)(2,1)S(1)} %concatenate.120), channel_id=1, source_target_pairs={{0,4},{4,0},{1,5},{5,1},{2,6},{6,2},{3,7},{7,3},{8,12},{12,8},{9,1... | collective-permute-start | bytes 184328 | tf_op jit(solution)/shard_map/ppermute | solution.py:45
  19.6 8.5 %collective-permute-start.3 = (bf16[3,2,176,128]{3,2,1,0:T(8,128)(2,1)S(1)}, bf16[3,2,176,128]{3,2,1,0:T(8,128)(2,1)S(1)}, u32[]{:S(2)}, u32[]{:S(2)}) collective-permute-start(bf16[3,2,176,128]{3,2,1,0:T(8,128)(2,1)S(1)} %dynamic-slice_bitcast_fusion.3), channel_id=1, source_target_pairs={{0,8},{8,0},{1,9},{9,1},{2,10},{10,2},{3,11},{11,3},{4,12},{12,4},... | collective-permute-start | bytes 811016 | tf_op jit(solution)/shard_map/ppermute | solution.py:45
  21.6 23.6 %collective-permute-start.6 = (bf16[32,2688]{1,0:T(8,128)(2,1)S(1)}, bf16[32,2688]{1,0:T(8,128)(2,1)S(1)}, u32[]{:S(2)}, u32[]{:S(2)}) collective-permute-start(bf16[32,2688]{1,0:T(8,128)(2,1)S(1)} %pad_maximum_fusion.15), channel_id=1, source_target_pairs={{0,2},{1,3},{2,0},{3,1},{4,6},{5,7},{6,4},{7,5},{8,10},{9,11},{10,... | collective-permute-start | bytes 516104 | tf_op jit(solution)/shard_map/ppermute | solution.py:49
  28.2 17.2 %collective-permute-start.4 = (bf16[3,176,256]{2,1,0:T(8,128)(2,1)S(1)}, bf16[3,176,256]{2,1,0:T(8,128)(2,1)S(1)}, u32[]{:S(2)}, u32[]{:S(2)}) collective-permute-start(bf16[3,176,256]{2,1,0:T(8,128)(2,1)S(1)} %pad_maximum_fusion.9), channel_id=1, source_target_pairs={{0,4},{4,0},{1,5},{5,1},{2,6},{6,2},{3,7},{7,3},{8,12},{12,8},{9,1... | collective-permute-start | bytes 811016 | tf_op jit(solution)/shard_map/ppermute | solution.py:45
  45.3 9.6 %copy-start.16 = (bf16[256,1024]{1,0:T(8,128)(2,1)}, bf16[256,1024]{1,0:T(8,128)(2,1)S(1)}, u32[]{:S(2)}) copy-start(bf16[256,1024]{1,0:T(8,128)(2,1)S(1)} %collective-permute-done.1.h0_ref) | copy-start | bytes 1572868
  45.3 9.6 %copy-start.17 = (bf16[256,1024]{1,0:T(8,128)(2,1)}, bf16[256,1024]{1,0:T(8,128)(2,1)S(1)}, u32[]{:S(2)}) copy-start(bf16[256,1024]{1,0:T(8,128)(2,1)S(1)} %collective-permute-done.2.h1_ref) | copy-start | bytes 1572868
  45.3 6.3 %collective-permute-start.7 = (bf16[64,1920]{1,0:T(8,128)(2,1)S(1)}, bf16[64,1920]{1,0:T(8,128)(2,1)S(1)}, u32[]{:S(2)}, u32[]{:S(2)}) collective-permute-start(bf16[64,1920]{1,0:T(8,128)(2,1)S(1)} %pad_maximum_fusion.14), channel_id=1, source_target_pairs={{0,1},{1,0},{2,3},{3,2},{4,5},{5,4},{6,7},{7,6},{8,9},{9,8},{10,11... | collective-permute-start | bytes 737288 | tf_op jit(solution)/shard_map/ppermute | solution.py:49
  46.5 215.8 %reduce-scatter.3.cloned.1.call-start = ((), (), s32[]{:S(2)}) async-start(), calls=%async_computation.2 | async-start | bytes 1310720 | tf_op jit(solution)/shard_map/reduce_scatter | solution.py:614
  51.7 5.7 %collective-permute-start.8 = (bf16[2,4,32,384]{3,0,2,1:T(2,128)(2,1)S(1)}, bf16[2,4,32,384]{3,0,2,1:T(2,128)(2,1)S(1)}, u32[]{:S(2)}, u32[]{:S(2)}) collective-permute-start(bf16[2,4,32,384]{3,0,2,1:T(2,128)(2,1)S(1)} %bitcast.194), channel_id=1, source_target_pairs={{0,8},{8,0},{1,9},{9,1},{2,10},{10,2},{3,11},{11,3},{4,12},{12,4},... | collective-permute-start | bytes 589832 | tf_op jit(solution)/shard_map/ppermute | solution.py:45
  53.3 14.6 %collective-permute-start.9 = (bf16[128,1152]{1,0:T(8,128)(2,1)S(1)}, bf16[128,1152]{1,0:T(8,128)(2,1)S(1)}, u32[]{:S(2)}, u32[]{:S(2)}) collective-permute-start(bf16[128,1152]{1,0:T(8,128)(2,1)S(1)} %bitcast.165), channel_id=1, source_target_pairs={{0,16},{16,0},{1,17},{17,1},{2,18},{18,2},{3,19},{19,3},{4,20},{20... | collective-permute-start | bytes 884744 | tf_op jit(solution)/shard_map/ppermute | solution.py:45
  55.0 22.0 %collective-permute-start.5 = (bf16[512,1024]{1,0:T(8,128)(2,1)S(1)}, bf16[512,1024]{1,0:T(8,128)(2,1)S(1)}, u32[]{:S(2)}, u32[]{:S(2)}) collective-permute-start(bf16[512,1024]{1,0:T(8,128)(2,1)S(1)} %pad_maximum_fusion.3), channel_id=1, source_target_pairs={{0,4},{4,0},{1,5},{5,1},{2,6},{6,2},{3,7},{7,3},{8,12},{12,8},{9,1... | collective-permute-start | bytes 3145736 | tf_op jit(solution)/shard_map/ppermute | solution.py:45
  68.0 19.5 %collective-permute-start.14 = (bf16[2,128,1152]{2,1,0:T(8,128)(2,1)S(1)}, bf16[2,128,1152]{2,1,0:T(8,128)(2,1)S(1)}, u32[]{:S(2)}, u32[]{:S(2)}) collective-permute-start(bf16[2,128,1152]{2,1,0:T(8,128)(2,1)S(1)} %maximum_select_fusion.4), channel_id=1, source_target_pairs={{0,8},{8,0},{1,9},{9,1},{2,10},{10,2},{3,11},{11,3},{4,12},{12,4},... | collective-permute-start | bytes 1769480 | tf_op jit(solution)/shard_map/ppermute | solution.py:45
  68.1 7.8 %collective-permute-start.10 = (bf16[4,4,32,384]{3,2,1,0:T(8,128)(2,1)S(1)}, bf16[4,4,32,384]{3,2,1,0:T(8,128)(2,1)S(1)}, u32[]{:S(2)}, u32[]{:S(2)}) collective-permute-start(bf16[4,4,32,384]{3,2,1,0:T(8,128)(2,1)S(1)} %bitcast.179), channel_id=1, source_target_pairs={{0,16},{16,0},{1,17},{17,1},{2,18},{18,2},{3,19},{19,3},{4,20},{20... | collective-permute-start | bytes 1179656 | tf_op jit(solution)/shard_map/ppermute | solution.py:45
  78.0 9.5 %copy-start.4 = (bf16[256,1024]{1,0:T(8,128)(2,1)S(1)}, bf16[256,1024]{1,0:T(8,128)(2,1)}, u32[]{:S(2)}) copy-start(bf16[256,1024]{1,0:T(8,128)(2,1)} %cot_ref.1) | copy-start | bytes 1572868
  86.5 3.5 %collective-permute-start.11 = (bf16[256,512]{1,0:T(8,128)(2,1)}, bf16[256,512]{1,0:T(8,128)(2,1)S(1)}, u32[]{:S(2)}, u32[]{:S(2)}) collective-permute-start(bf16[256,512]{1,0:T(8,128)(2,1)} %get-tuple-element.88), channel_id=1, source_target_pairs={{0,4},{4,0},{1,5},{5,1},{2,6},{6,2},{3,7},{7,3},{8,12},{12,8},{9,1... | collective-permute-start | bytes 786440 | tf_op jit(solution)/shard_map/ppermute | solution.py:45
  87.5 14.6 %collective-permute-start.16 = (bf16[256,1024]{1,0:T(8,128)(2,1)S(1)}, bf16[256,1024]{1,0:T(8,128)(2,1)S(1)}, u32[]{:S(2)}, u32[]{:S(2)}) collective-permute-start(bf16[256,1024]{1,0:T(8,128)(2,1)S(1)} %copy-done.4), channel_id=1, source_target_pairs={{0,8},{8,0},{1,9},{9,1},{2,10},{10,2},{3,11},{11,3},{4,12},{12,4},... | collective-permute-start | bytes 1572872 | tf_op jit(solution)/shard_map/ppermute | solution.py:45
  90.0 12.2 %collective-permute-start.15 = (bf16[2,2,128,1152]{3,2,1,0:T(8,128)(2,1)S(1)}, bf16[2,2,128,1152]{3,2,1,0:T(8,128)(2,1)S(1)}, u32[]{:S(2)}, u32[]{:S(2)}) collective-permute-start(bf16[2,2,128,1152]{3,2,1,0:T(8,128)(2,1)S(1)} %maximum_select_fusion.1), channel_id=1, source_target_pairs={{0,4},{4,0},{1,5},{5,1},{2,6},{6,2},{3,7},{7,3},{8,12},{12,8},{9,1... | collective-permute-start | bytes 3538952 | tf_op jit(solution)/shard_map/ppermute | solution.py:45
  90.5 19.0 %collective-permute-start.13 = (bf16[256,512]{1,0:T(8,128)(2,1)S(1)}, bf16[256,512]{1,0:T(8,128)(2,1)S(1)}, u32[]{:S(2)}, u32[]{:S(2)}) collective-permute-start(bf16[256,512]{1,0:T(8,128)(2,1)S(1)} %pad_maximum_fusion.12), channel_id=1, source_target_pairs={{0,2},{1,0},{2,6},{3,4},{4,3},{5,1},{6,7},{7,5},{8,10},{9,8},{10,1... | collective-permute-start | bytes 786440 | tf_op jit(solution)/shard_map/ppermute | solution.py:62
  91.9 17.6 %collective-permute-start.12 = (bf16[256,512]{1,0:T(8,128)(2,1)S(1)}, bf16[256,512]{1,0:T(8,128)(2,1)S(1)}, u32[]{:S(2)}, u32[]{:S(2)}) collective-permute-start(bf16[256,512]{1,0:T(8,128)(2,1)S(1)} %pad_maximum_fusion.11), channel_id=1, source_target_pairs={{0,0},{1,2},{2,4},{3,6},{4,1},{5,3},{6,5},{7,7},{8,8},{9,10},{10,1... | collective-permute-start | bytes 786440 | tf_op jit(solution)/shard_map/ppermute | solution.py:62
  102.2 23.0 %collective-permute-start.18 = (bf16[512,1024]{1,0:T(8,128)(2,1)S(1)}, bf16[512,1024]{1,0:T(8,128)(2,1)S(1)}, u32[]{:S(2)}, u32[]{:S(2)}) collective-permute-start(bf16[512,1024]{1,0:T(8,128)(2,1)S(1)} %pad_maximum_fusion.5), channel_id=1, source_target_pairs={{0,4},{4,0},{1,5},{5,1},{2,6},{6,2},{3,7},{7,3},{8,12},{12,8},{9,1... | collective-permute-start | bytes 3145736 | tf_op jit(solution)/shard_map/ppermute | solution.py:45
  114.5 9.4 %collective-permute-start.17 = (bf16[256,1024]{1,0:T(8,128)(2,1)}, bf16[256,1024]{1,0:T(8,128)(2,1)S(1)}, u32[]{:S(2)}, u32[]{:S(2)}) collective-permute-start(bf16[256,1024]{1,0:T(8,128)(2,1)} %get-tuple-element.94.refs_1_), channel_id=1, source_target_pairs={{0,8},{8,0},{1,9},{9,1},{2,10},{10,2},{3,11},{11,3},{4,12},{12,4},... | collective-permute-start | bytes 1572872 | tf_op jit(solution)/shard_map/ppermute | solution.py:45
  123.9 13.7 %copy-start.19 = (bf16[256,1024]{1,0:T(8,128)(2,1)}, bf16[256,1024]{1,0:T(8,128)(2,1)S(1)}, u32[]{:S(2)}) copy-start(bf16[256,1024]{1,0:T(8,128)(2,1)S(1)} %collective-permute-done.17.refs_2_) | copy-start | bytes 1572868
  125.2 12.4 %copy-start.24 = (bf16[512,1024]{1,0:T(8,128)(2,1)}, bf16[512,1024]{1,0:T(8,128)(2,1)S(1)}, u32[]{:S(2)}) copy-start(bf16[512,1024]{1,0:T(8,128)(2,1)S(1)} %collective-permute-done.18.refs_6_) | copy-start | bytes 3145732
  125.2 12.3 %collective-permute-start.19 = (bf16[512,1024]{1,0:T(8,128)(2,1)S(1)}, bf16[512,1024]{1,0:T(8,128)(2,1)}, u32[]{:S(2)}, u32[]{:S(2)}) collective-permute-start(bf16[512,1024]{1,0:T(8,128)(2,1)S(1)} %pad_maximum_fusion.4), channel_id=1, source_target_pairs={{0,4},{4,0},{1,5},{5,1},{2,6},{6,2},{3,7},{7,3},{8,12},{12,8},{9,1... | collective-permute-start | bytes 3145736 | tf_op jit(solution)/shard_map/ppermute | solution.py:45
  172.4 26.8 %copy-start.9 = (bf16[4,256,512]{2,1,0:T(8,128)(2,1)S(1)}, bf16[4,256,512]{2,1,0:T(8,128)(2,1)}, u32[]{:S(2)}) copy-start(bf16[4,256,512]{2,1,0:T(8,128)(2,1)} %get-tuple-element.112) | copy-start | bytes 3145732
  172.5 3.1 collective-permute-start.20
  172.9 26.3 %collective-permute-start.25 = (bf16[4,256,512]{2,1,0:T(8,128)(2,1)}, bf16[4,256,512]{2,1,0:T(8,128)(2,1)S(1)}, u32[]{:S(2)}, u32[]{:S(2)}) collective-permute-start(bf16[4,256,512]{2,1,0:T(8,128)(2,1)} %get-tuple-element.114), channel_id=1, source_target_pairs={{0,16},{16,0},{1,17},{17,1},{2,18},{18,2},{3,19},{19,3},{4,20},{20... | collective-permute-start | bytes 3145736 | tf_op jit(solution)/shard_map/ppermute | solution.py:45
  175.6 25.0 %copy-start.2 = (bf16[2,256,1024]{2,1,0:T(8,128)(2,1)}, bf16[2,256,1024]{2,1,0:T(8,128)(2,1)S(1)}, u32[]{:S(2)}) copy-start(bf16[2,256,1024]{2,1,0:T(8,128)(2,1)S(1)} %collective-permute-done.20.near_ref) | copy-start | bytes 3145732
  177.2 14.1 %collective-permute-start.22 = (bf16[256,1024]{1,0:T(8,128)(2,1)S(1)}, bf16[256,1024]{1,0:T(8,128)(2,1)S(1)}, u32[]{:S(2)}, u32[]{:S(2)}) collective-permute-start(bf16[256,1024]{1,0:T(8,128)(2,1)S(1)} %fusion.20), channel_id=1, source_target_pairs={{0,8},{8,0},{1,9},{9,1},{2,10},{10,2},{3,11},{11,3},{4,12},{12,4},... | collective-permute-start | bytes 1572872 | tf_op jit(solution)/shard_map/ppermute | solution.py:45
  177.7 24.7 %collective-permute-start.21 = (bf16[2,256,1024]{2,1,0:T(8,128)(2,1)}, bf16[2,256,1024]{2,1,0:T(8,128)(2,1)S(1)}, u32[]{:S(2)}, u32[]{:S(2)}) collective-permute-start(bf16[2,256,1024]{2,1,0:T(8,128)(2,1)} %get-tuple-element.102), channel_id=1, source_target_pairs={{0,4},{4,0},{1,5},{5,1},{2,6},{6,2},{3,7},{7,3},{8,12},{12,8},{9,1... | collective-permute-start | bytes 3145736 | tf_op jit(solution)/shard_map/ppermute | solution.py:45
  200.6 65.1 %reduce-scatter.5.cloned.1.call-start = ((), (), s32[]{:S(2)}) async-start(), calls=%async_computation.3 | async-start | bytes 1392640 | tf_op jit(solution)/shard_map/reduce_scatter | solution.py:614
  200.6 26.5 %collective-permute-start.26 = (bf16[4,272,512]{2,1,0:T(8,128)(2,1)}, bf16[4,272,512]{2,1,0:T(8,128)(2,1)}, u32[]{:S(2)}, u32[]{:S(2)}) collective-permute-start(bf16[4,272,512]{2,1,0:T(8,128)(2,1)} %get-tuple-element.118), channel_id=1, source_target_pairs={{0,16},{16,0},{1,17},{17,1},{2,18},{18,2},{3,19},{19,3},{4,20},{20... | collective-permute-start | bytes 3342344 | tf_op jit(solution)/shard_map/ppermute | solution.py:45
  202.5 7.5 %copy-start.11 = (bf16[2,256,1024]{2,1,0:T(8,128)(2,1)}, bf16[2,256,1024]{2,1,0:T(8,128)(2,1)S(1)}, u32[]{:S(2)}) copy-start(bf16[2,256,1024]{2,1,0:T(8,128)(2,1)S(1)} %collective-permute-done.21) | copy-start | bytes 3145732
  210.0 17.1 %copy-start.6 = (bf16[4,272,512]{2,1,0:T(8,128)(2,1)S(1)}, bf16[4,272,512]{2,1,0:T(8,128)(2,1)}, u32[]{:S(2)}) copy-start(bf16[4,272,512]{2,1,0:T(8,128)(2,1)} %get-tuple-element.116) | copy-start | bytes 3342340
  211.5 31.5 %collective-permute-start.28 = (bf16[2,2,4,32,1152]{4,3,2,1,0:T(8,128)(2,1)S(1)}, bf16[2,2,4,32,1152]{4,3,2,1,0:T(8,128)(2,1)}, u32[]{:S(2)}, u32[]{:S(2)}) collective-permute-start(bf16[2,2,4,32,1152]{4,3,2,1,0:T(8,128)(2,1)S(1)} %dynamic-slice_bitcast_fusion), channel_id=1, source_target_pairs={{0,4},{4,0},{1,5},{5,1},{2,6},{6,2},{3,7},{7,3},{8,12},{12,8},{9,1... | collective-permute-start | bytes 3538952 | tf_op jit(solution)/shard_map/ppermute | solution.py:45
  211.8 28.7 %collective-permute-start.23 = (bf16[256,1024]{1,0:T(8,128)(2,1)}, bf16[256,1024]{1,0:T(8,128)(2,1)S(1)}, u32[]{:S(2)}, u32[]{:S(2)}) collective-permute-start(bf16[256,1024]{1,0:T(8,128)(2,1)} %fusion.19), channel_id=1, source_target_pairs={{0,8},{8,0},{1,9},{9,1},{2,10},{10,2},{3,11},{11,3},{4,12},{12,4},... | collective-permute-start | bytes 1572872 | tf_op jit(solution)/shard_map/ppermute | solution.py:45
  212.2 17.6 %collective-permute-start.24 = (bf16[256,512]{1,0:T(8,128)(2,1)}, bf16[256,512]{1,0:T(8,128)(2,1)}, u32[]{:S(2)}, u32[]{:S(2)}) collective-permute-start(bf16[256,512]{1,0:T(8,128)(2,1)} %get-tuple-element.110), channel_id=1, source_target_pairs={{0,0},{2,1},{4,2},{6,3},{1,4},{3,5},{5,6},{7,7},{8,8},{10,9},{12,1... | collective-permute-start | bytes 786440 | tf_op jit(solution)/shard_map/ppermute | solution.py:66
  215.7 23.8 %collective-permute-start.27 = (bf16[256,512]{1,0:T(8,128)(2,1)}, bf16[256,512]{1,0:T(8,128)(2,1)}, u32[]{:S(2)}, u32[]{:S(2)}) collective-permute-start(bf16[256,512]{1,0:T(8,128)(2,1)} %get-tuple-element.120), channel_id=1, source_target_pairs={{2,0},{0,1},{6,2},{4,3},{3,4},{1,5},{7,6},{5,7},{10,8},{8,9},{14,1... | collective-permute-start | bytes 786440 | tf_op jit(solution)/shard_map/ppermute | solution.py:66
  229.7 10.8 %copy-start.1 = (f32[256,1024]{1,0:T(8,128)S(1)}, f32[256,1024]{1,0:T(8,128)}, u32[]{:S(2)}) copy-start(f32[256,1024]{1,0:T(8,128)} %get-tuple-element.91.middle_ref) | copy-start | bytes 3145732
  240.5 2.5 copy-start.3
  243.0 3.3 %collective-permute-start.29 = (bf16[256,512]{1,0:T(8,128)(2,1)S(1)}, bf16[256,512]{1,0:T(8,128)(2,1)S(1)}, u32[]{:S(2)}, u32[]{:S(2)}) collective-permute-start(bf16[256,512]{1,0:T(8,128)(2,1)S(1)} %pad_maximum_fusion.13), channel_id=1, source_target_pairs={{0,4},{4,0},{1,5},{5,1},{2,6},{6,2},{3,7},{7,3},{8,12},{12,8},{9,1... | collective-permute-start | bytes 786440 | tf_op jit(solution)/shard_map/ppermute | solution.py:45
  244.7 16.7 %collective-permute-start.34 = (bf16[2,4,32,1152]{3,2,1,0:T(8,128)(2,1)S(1)}, bf16[2,4,32,1152]{3,2,1,0:T(8,128)(2,1)S(1)}, u32[]{:S(2)}, u32[]{:S(2)}) collective-permute-start(bf16[2,4,32,1152]{3,2,1,0:T(8,128)(2,1)S(1)} %dynamic-slice_bitcast_fusion.1), channel_id=1, source_target_pairs={{0,8},{8,0},{1,9},{9,1},{2,10},{10,2},{3,11},{11,3},{4,12},{12,4},... | collective-permute-start | bytes 1769480 | tf_op jit(solution)/shard_map/ppermute | solution.py:45
  261.1 5.9 %collective-permute-start.30 = (bf16[2,256,1024]{2,1,0:T(8,128)(2,1)}, bf16[2,256,1024]{2,1,0:T(8,128)(2,1)S(1)}, u32[]{:S(2)}, u32[]{:S(2)}) collective-permute-start(bf16[2,256,1024]{2,1,0:T(8,128)(2,1)} %get-tuple-element.133), channel_id=1, source_target_pairs={{0,4},{4,0},{1,5},{5,1},{2,6},{6,2},{3,7},{7,3},{8,12},{12,8},{9,1... | collective-permute-start | bytes 3145736 | tf_op jit(solution)/shard_map/ppermute | solution.py:45
  267.0 2.1 copy-start.8
  267.6 10.8 %collective-permute-start.33 = (bf16[2,2,4,32,384]{4,1,3,2,0:T(2,128)(2,1)S(1)}, bf16[2,2,4,32,384]{4,1,3,2,0:T(2,128)(2,1)S(1)}, u32[]{:S(2)}, u32[]{:S(2)}) collective-permute-start(bf16[2,2,4,32,384]{4,1,3,2,0:T(2,128)(2,1)S(1)} %bitcast.209), channel_id=1, source_target_pairs={{0,16},{16,0},{1,17},{17,1},{2,18},{18,2},{3,19},{19,3},{4,20},{20... | collective-permute-start | bytes 1179656 | tf_op jit(solution)/shard_map/ppermute | solution.py:45
  269.1 4.5 %copy-start.5 = (bf16[1,272,512]{2,1,0:T(8,128)(2,1)S(1)}, bf16[1,272,512]{2,1,0:T(8,128)(2,1)}, u32[]{:S(2)}) copy-start(bf16[1,272,512]{2,1,0:T(8,128)(2,1)} %reduce-scatter.5.cloned.1.call-done) | copy-start | bytes 835588
  269.1 4.5 %copy-start.12 = (bf16[1,256,512]{2,1,0:T(8,128)(2,1)S(1)}, bf16[1,256,512]{2,1,0:T(8,128)(2,1)}, u32[]{:S(2)}) copy-start(bf16[1,256,512]{2,1,0:T(8,128)(2,1)} %reduce-scatter.3.cloned.1.call-done) | copy-start | bytes 786436
  269.7 12.3 %collective-permute-start.31 = (bf16[256,1024]{1,0:T(8,128)(2,1)S(1)}, bf16[256,1024]{1,0:T(8,128)(2,1)S(1)}, u32[]{:S(2)}, u32[]{:S(2)}) collective-permute-start(bf16[256,1024]{1,0:T(8,128)(2,1)S(1)} %get-tuple-element.134), channel_id=1, source_target_pairs={{0,0},{1,2},{2,4},{3,6},{4,1},{5,3},{6,5},{7,7},{8,8},{9,10},{10,1... | collective-permute-start | bytes 1572872 | tf_op jit(solution)/shard_map/ppermute | solution.py:62
  270.4 15.6 %collective-permute-start.32 = (bf16[256,1024]{1,0:T(8,128)(2,1)S(1)}, bf16[256,1024]{1,0:T(8,128)(2,1)S(1)}, u32[]{:S(2)}, u32[]{:S(2)}) collective-permute-start(bf16[256,1024]{1,0:T(8,128)(2,1)S(1)} %get-tuple-element.135), channel_id=1, source_target_pairs={{0,2},{1,0},{2,6},{3,4},{4,3},{5,1},{6,7},{7,5},{8,10},{9,8},{10,1... | collective-permute-start | bytes 1572872 | tf_op jit(solution)/shard_map/ppermute | solution.py:62
  273.7 14.1 %collective-permute-start.40 = (f32[528,256]{1,0:T(8,128)S(1)}, f32[528,256]{1,0:T(8,128)S(1)}, u32[]{:S(2)}, u32[]{:S(2)}) collective-permute-start(f32[528,256]{1,0:T(8,128)S(1)} %pad_maximum_fusion.8), channel_id=1, source_target_pairs={{0,4},{4,0},{1,5},{5,1},{2,6},{6,2},{3,7},{7,3},{8,12},{12,8},{9,1... | collective-permute-start | bytes 1622024 | tf_op jit(solution)/shard_map/ppermute | solution.py:45
  278.9 7.5 %copy-start.7 = (f32[256,1024]{1,0:T(8,128)S(1)}, f32[256,1024]{1,0:T(8,128)}, u32[]{:S(2)}) copy-start(f32[256,1024]{1,0:T(8,128)} %get-tuple-element.109) | copy-start | bytes 3145732
  279.0 8.8 %collective-permute-start.35 = (bf16[2,4,32,384]{3,0,2,1:T(2,128)(2,1)S(1)}, bf16[2,4,32,384]{3,0,2,1:T(2,128)(2,1)S(1)}, u32[]{:S(2)}, u32[]{:S(2)}) collective-permute-start(bf16[2,4,32,384]{3,0,2,1:T(2,128)(2,1)S(1)} %dynamic-slice_bitcast_fusion.4), channel_id=1, source_target_pairs={{0,8},{8,0},{1,9},{9,1},{2,10},{10,2},{3,11},{11,3},{4,12},{12,4},... | collective-permute-start | bytes 589832 | tf_op jit(solution)/shard_map/ppermute | solution.py:45
  280.6 7.6 %collective-permute-start.36 = (bf16[4,32,1152]{2,1,0:T(8,128)(2,1)}, bf16[4,32,1152]{2,1,0:T(8,128)(2,1)S(1)}, u32[]{:S(2)}, u32[]{:S(2)}) collective-permute-start(bf16[4,32,1152]{2,1,0:T(8,128)(2,1)} %dynamic-slice_bitcast_fusion.2), channel_id=1, source_target_pairs={{0,16},{16,0},{1,17},{17,1},{2,18},{18,2},{3,19},{19,3},{4,20},{20... | collective-permute-start | bytes 884744 | tf_op jit(solution)/shard_map/ppermute | solution.py:45
  288.3 19.4 %collective-permute-start.37 = (bf16[32,1920]{1,0:T(8,128)(2,1)S(1)}, bf16[32,1920]{1,0:T(8,128)(2,1)S(1)}, u32[]{:S(2)}, u32[]{:S(2)}) collective-permute-start(bf16[32,1920]{1,0:T(8,128)(2,1)S(1)} %get-tuple-element.142), channel_id=1, source_target_pairs={{0,2},{1,3},{2,0},{3,1},{4,6},{5,7},{6,4},{7,5},{8,10},{9,11},{10,... | collective-permute-start | bytes 368648 | tf_op jit(solution)/shard_map/ppermute | solution.py:49
  300.5 10.7 %collective-permute-start.41 = (bf16[1056,128]{1,0:T(8,128)(2,1)S(1)}, bf16[1056,128]{1,0:T(8,128)(2,1)S(1)}, u32[]{:S(2)}, u32[]{:S(2)}) collective-permute-start(bf16[1056,128]{1,0:T(8,128)(2,1)S(1)} %pad_maximum_fusion.10), channel_id=1, source_target_pairs={{0,8},{8,0},{1,9},{9,1},{2,10},{10,2},{3,11},{11,3},{4,12},{12,4},... | collective-permute-start | bytes 811016 | tf_op jit(solution)/shard_map/ppermute | solution.py:45
  302.0 8.3 %collective-permute-start.38 = (bf16[32,1920]{1,0:T(8,128)(2,1)S(1)}, bf16[32,1920]{1,0:T(8,128)(2,1)S(1)}, u32[]{:S(2)}, u32[]{:S(2)}) collective-permute-start(bf16[32,1920]{1,0:T(8,128)(2,1)S(1)} %get-tuple-element.143), channel_id=1, source_target_pairs={{0,1},{1,0},{2,3},{3,2},{4,5},{5,4},{6,7},{7,6},{8,9},{9,8},{10,11... | collective-permute-start | bytes 368648 | tf_op jit(solution)/shard_map/ppermute | solution.py:49
  303.0 7.3 %collective-permute-start.39 = (bf16[32,1920]{1,0:T(8,128)(2,1)S(1)}, bf16[32,1920]{1,0:T(8,128)(2,1)S(1)}, u32[]{:S(2)}, u32[]{:S(2)}) collective-permute-start(bf16[32,1920]{1,0:T(8,128)(2,1)S(1)} %get-tuple-element.144), channel_id=1, source_target_pairs={{0,3},{1,2},{2,1},{3,0},{4,7},{5,6},{6,5},{7,4},{8,11},{9,10},{10,... | collective-permute-start | bytes 368648 | tf_op jit(solution)/shard_map/ppermute | solution.py:49
  311.2 1.4 collective-permute-start.42
  312.6 2.0 copy-start.21
  312.6 2.0 copy-start.22
  (11 other events, 13.5 us)
Sparse Core Ops, SparseCore 0:
  46.6 84.5 all-gather.2
  200.7 34.7 reduce-scatter.2
  237.9 27.7 reduce-scatter.4

commit v2 on v1

--- a/solution.py
+++ b/solution.py
@@ -22,7 +22,7 @@
 SLOT_MASKS = (0, 2, 1, 3)
 SPLIT_BITS = 2
 SPLIT = 1 << SPLIT_BITS
-TERM_ROWS = ((0, 256), (256, 528))
+TERM_ROWS = ((0, 176), (176, 528))
 
 
 def matmul(first_matrix, second_matrix):
@@ -96,11 +96,10 @@
     out_specs = [hbm if len(out) > 2 else vmem for out in outs]
     outs = [jax.ShapeDtypeStruct(out[0], out[1]) for out in outs]
     nbytes = sum(o.size * o.dtype.itemsize for o in list(operands) + outs)
-    plain = len(operands) - scalars - remote
     return pl.pallas_call(
         body,
         out_shape=outs,
-        in_specs=[smem] * scalars + [vmem] * plain + [hbm] * remote,
+        in_specs=[smem] * scalars + [vmem] * (len(operands) - scalars - remote) + [hbm] * remote,
         out_specs=out_specs,
         scratch_shapes=list(scratch),
         compiler_params=pltpu.CompilerParams(vmem_limit_bytes=limit * 1024 * 1024),
@@ -174,9 +173,10 @@
 
 
 def back_body(
-    first_ref, group_ref, g0_ref, g1_ref, near_ref, qkv_ref, attf_ref, rden_ref, hr_ref, w_ref,
-    kept_ref, sent_ref, term_ref, qt_ref, aug_ref, nb_ref, ag_ref, bars_ref,
+    first_ref, group_ref, g0_ref, g1_ref, near_ref, qkv_ref, attf_ref, rden_ref, hr_in, w_in,
+    kept_ref, sent_ref, term_ref, qt_ref, aug_ref, nb_ref, ag_ref, bars_ref, hr_ref, w_ref, sems,
 ):
+    loads = start_copies([(hr_in, hr_ref), (w_in, w_ref)], sems, 0)
     first, group = first_ref[0], group_ref[0]
     tokens = g0_ref.shape[0]
     length, width = ag_ref.shape
@@ -234,6 +234,8 @@
         bars_ref[rows, qk : 2 * qk] = key_total.astype(BF16)
         qt_ref[:, low:] += query_total
     bars_ref[:, :qk] = qt_ref[...].T.astype(BF16)
+    for copy in loads:
+        copy.wait()
     term = jnp.zeros((bars_ref.shape[1], hr_ref.shape[2]), F32)
     for k, mask in enumerate(SLOT_MASKS):
         bars = bars_ref[block_at(group ^ mask, tokens), :]
@@ -297,53 +299,17 @@
     return copies
 
 
-def wait_copies(copies):
-    for copy in copies:
-        copy.wait()
-
-
-def feature_pairs(place, count, moved, own_order, device_order):
-    if not moved:
-        return [(own_order, device_order)]
-    block = own_order.shape[1] // count
-    return [
-        (own_order.at[:, block_at(place ^ j, block)], device_order.at[:, pl.ds(j * block, block)])
-        for j in range(count)
-    ]
-
-
-def row_pairs(place, count, moved, refs, out_ref):
-    pairs, low = [], 0
-    for ref in refs:
-        rows = ref.shape[0]
-        pairs += feature_pairs(place, count, moved, ref, out_ref.at[pl.ds(low, rows), :])
-        low += rows
-    return pairs
-
-
-def unit_pairs(units, piece_ref, weight_refs):
-    parts, slots, _, part = piece_ref.shape
-    return [
-        (
-            piece_ref.at[y, s, pl.ds(m * units, units), :],
-            w_ref.at[pl.ds(s * units, units), pl.ds(y * part, part)],
-        )
-        for m, w_ref in enumerate(weight_refs)
-        for y in range(parts)
-        for s in range(slots)
-    ]
-
-
-def forward_units(total, x_ref, c_ref, weight_refs, hidden_refs, put):
-    wg_ref, wu_ref, wd_ref = weight_refs
-    tokens = TILE
+def forward_units(x_blocks, c_blocks, weights_ref, hidden_refs, put):
+    wg_ref, wu_ref, wd_ref = (weights_ref.at[m] for m in range(3))
+    total = weights_ref.shape[1]
     edges = list(range(0, total, TILE)) + [total]
     spans = list(zip(edges[:-1], edges[1:]))
-
-    for b in range(x_ref.shape[0] // tokens):
+    tokens = TILE
+
+    for b, (x_ref, c_ref) in enumerate(zip(x_blocks, c_blocks)):
         rows = slice(b * tokens, (b + 1) * tokens)
-        x_rows = x_ref[rows, :]
-        c_rows = c_ref[rows, :]
+        x_rows = x_ref[...]
+        c_rows = c_ref[...]
         kept = []
         for low, high in spans:
             gate = dot_last(x_rows, wg_ref[low:high, :])
@@ -363,47 +329,67 @@
         put(b, branch, grad)
 
 
-def weight_units(units, index, x_ref, c_ref, hidden_refs, term_ref):
+def weight_units(units, index, x_blocks, c_blocks, hidden_refs, term_ref):
     slots, _, part = term_ref.shape
     step = min(part, 256)
     act_ref, gate_ref, up_ref = hidden_refs
-    for m, (left, right) in enumerate(((gate_ref, x_ref), (up_ref, x_ref), (act_ref, c_ref))):
+    for m, (left, right) in enumerate(
+        ((gate_ref, x_blocks), (up_ref, x_blocks), (act_ref, c_blocks))
+    ):
         for at in range(0, part, step):
             lanes = pl.ds(pl.multiple_of(index * part + at, step), step)
-            out = matmul(left[...], right[:, lanes]).astype(BF16)
-            rows = slice(m * units, (m + 1) * units)
+            rows = jnp.concatenate([ref[:, lanes] for ref in right], axis=0)
+            out = matmul(left[...], rows).astype(BF16)
             for s in range(slots):
-                term_ref[s, rows, at : at + step] = out[s * units : (s + 1) * units]
-
-
-def feed_forward_body(units, count, moved, parts, *refs):
-    spot_ref, x_refs, c_refs, piece_ref, refs = refs[0], refs[1:4], refs[4:7], refs[7], refs[8:]
+                term_ref[s, m * units : (m + 1) * units, at : at + step] = out[
+                    s * units : (s + 1) * units
+                ]
+
+
+def feed_forward_body(units, parts, *refs):
+    index_ref, sources, piece_ref, refs = refs[0], refs[1:7], refs[7], refs[8:]
     grad_refs, branch_refs, term_refs, refs = refs[:2], refs[2:4], refs[4 : 4 + 2 * parts], refs[4 + 2 * parts :]
-    x_ref, c_ref, weight_refs, hidden_refs = refs[0], refs[1], refs[2:5], refs[5:8]
-    branch_buf, grad_buf, term_buf, sems = refs[8:]
-    place, index = spot_ref[0], spot_ref[1]
-    pairs = row_pairs(place, count, moved, x_refs, x_ref)
-    pairs += row_pairs(place, count, moved, c_refs, c_ref)
-    pairs += unit_pairs(units, piece_ref, weight_refs)
-    wait_copies(start_copies(pairs, sems, 0))
+    rows_ref, weights_ref, hidden_refs, branch_buf, grad_buf, term_buf, sems = *refs[:2], refs[2:5], *refs[5:]
+    tokens = sources[0].shape[0]
+    pairs = [
+        (source, rows_ref.at[n // 3, pl.ds(tokens * (n % 3), source.shape[0]), :])
+        for n, source in enumerate(sources)
+    ]
+    count, slots, _, part = piece_ref.shape
+    pairs += [
+        (
+            piece_ref.at[y, s, pl.ds(m * units, units), :],
+            weights_ref.at[m, pl.ds(s * units, units), pl.ds(y * part, part)],
+        )
+        for m in range(3)
+        for y in range(count)
+        for s in range(slots)
+    ]
+    for copy in start_copies(pairs, sems, 0):
+        copy.wait()
+    x_blocks, c_blocks = (
+        [rows_ref.at[n, pl.ds(tokens * b, tokens), :] for b in range(SPLIT)] for n in range(2)
+    )
     stores = []
 
     def put(b, branch, grad):
         branch_buf[b] = branch.astype(BF16)
         grad_buf[b] = grad.astype(BF16)
-        done = feature_pairs(place, count, moved, grad_refs[b // 2].at[b % 2], grad_buf.at[b])
-        done += feature_pairs(place, count, moved, branch_refs[b // 2].at[b % 2], branch_buf.at[b])
-        done = [(source, target) for target, source in done]
+        done = [
+            (grad_buf.at[b], grad_refs[b // 2].at[b % 2]),
+            (branch_buf.at[b], branch_refs[b // 2].at[b % 2]),
+        ]
         stores.extend(start_copies(done, sems, len(pairs) + len(stores)))
 
-    forward_units(weight_refs[0].shape[0], x_ref, c_ref, weight_refs, hidden_refs, put)
+    forward_units(x_blocks, c_blocks, weights_ref, hidden_refs, put)
     for n in range(parts):
-        which = index if n == parts - 1 else 1 - index
-        weight_units(units, which, x_ref, c_ref, hidden_refs, term_buf.at[n])
+        which = index_ref[0] if n == parts - 1 else 1 - index_ref[0]
+        weight_units(units, which, x_blocks, c_blocks, hidden_refs, term_buf.at[n])
         for h, rows in enumerate(TERM_ROWS):
             done = [(term_buf.at[n, :, pl.ds(rows[0], rows[1] - rows[0]), :], term_refs[2 * n + h])]
             stores.extend(start_copies(done, sems, len(pairs) + len(stores)))
-    wait_copies(stores)
+    for copy in stores:
+        copy.wait()
 
 
 def on_device(
@@ -455,6 +441,12 @@
             left.remove(bit)
         return term
 
+    side = (me >> 1) & 1
+
+    def in_place(shares):
+        shares = [jnp.where(core == 0, shares[k], shares[k ^ 1]) for k in range(SPLIT)]
+        return [jnp.where(side == 0, shares[k], shares[k ^ 2]) for k in range(SPLIT)]
+
     rows = query_weight.shape[0]
     qk = H * HF // GROUPS
     vw = H * DV // GROUPS
@@ -502,11 +494,11 @@
     block = stacked.shape[2]
     aligned = block % LANES == 0
     stacked = stacked.reshape(3, 2, 2, units, block)
-    side = (me >> 1) & 1
     kept = [pick(stacked, side, 1), swap_bit(pick(stacked, 1 - side, 1), 1)]
     sent = swap_bit(jnp.concatenate([pick(part, 1 - core, 1) for part in kept], axis=2), 0)
     kept = [pick(part, core, 1) for part in kept]
-    own = jnp.concatenate([kept[0], sent[:, :, :block], kept[1], sent[:, :, block:]], axis=2)
+    own = in_place([kept[0], sent[:, :, :block], kept[1], sent[:, :, block:]])
+    own = jnp.concatenate(own, axis=2)
     output_mat = both[:, :, 2 * cols :].reshape(GROUPS * rows, -1)
     output_mat = pair_up((me >> links[-1]) & 1, output_mat, swap_bit(output_mat, links[-1]), 0)
     attn_mat = both[:, :, : 2 * cols].reshape(GROUPS, rows, 2, cols).transpose(2, 0, 1, 3)
@@ -518,10 +510,10 @@
 
     far_axes = dp[: bits - SPLIT_BITS] + ("feat",)
 
-    pieces = lax.all_gather(after(own.reshape(3 * units, SPLIT * block), *hidden), far_axes)
-    pieces = pieces.reshape(-1, GROUPS, 3 * units, SPLIT * block)
+    weights = lax.all_gather(after(own.reshape(3 * units, SPLIT * block), *hidden), far_axes)
+    weights = weights.reshape(-1, GROUPS, 3 * units, SPLIT * block)
     if not aligned:
-        pieces = pieces.transpose(1, 2, 0, 3).reshape(1, GROUPS, 3 * units, width)
+        weights = weights.transpose(1, 2, 0, 3).reshape(1, GROUPS, 3 * units, width)
 
     def pair_with(own, far):
         return [own, far, swap_bit(jnp.concatenate([own, far], axis=0), 0)]
@@ -535,6 +527,7 @@
         scalars=2,
         scratch=(pltpu.VMEM((length, vw), BF16),),
         flops=8 * 2**30,
+        limit=24,
     )
     sent = swap_bit(sent, 0)
     for axis, bit in enumerate(links[-2::-1], 1):
@@ -557,51 +550,38 @@
         (member_arr, *out, hidden_in, output_mat),
         scalars=1,
         flops=2**30,
+        limit=12,
     )
 
     mlps = pair_with(mlp_in, swap_bit(mlp_in, 1))
-    swap = lambda v: v
-    if not aligned:
-        order = jnp.arange(size) ^ (me % SPLIT)
-        swap = lambda v: jnp.take(
-            v.reshape(v.shape[:-1] + (size, block)), order, axis=v.ndim - 1
-        ).reshape(v.shape)
-    rows_scratch = pltpu.VMEM((SPLIT * tokens, width), BF16)
     blocks = (SPLIT, tokens, width)
-    blocks_scratch = pltpu.VMEM(blocks, BF16)
-    parts = pieces.shape[0]
+    parts = 2 if aligned and bits == SPLIT_BITS + 1 else 1
     part = me >> SPLIT_BITS if parts == 2 else jnp.zeros((), jnp.int32)
-    spot = jnp.stack([me % SPLIT, part])
-    sems = pltpu.SemaphoreType.DMA((160,))
-    sources = [swap(v) for v in mlps + cots]
-
     term_shape = (GROUPS, 3 * units, width // parts)
     outs = kernel_call(
-        partial(feed_forward_body, units, size, aligned, parts),
+        partial(feed_forward_body, units, parts),
         [((2, tokens, width), BF16, True)] * 4
         + [((GROUPS, high - low, width // parts), BF16, True) for low, high in TERM_ROWS] * parts,
-        (spot, *sources, pieces),
+        (part.reshape(1), *mlps, *cots, weights),
         scalars=1,
         remote=7,
         scratch=(
-            rows_scratch,
-            rows_scratch,
-            *[pltpu.VMEM((GROUPS * units, width), BF16)] * 3,
+            pltpu.VMEM((2, SPLIT * tokens, width), BF16),
+            pltpu.VMEM((3, GROUPS * units, width), BF16),
             *[pltpu.VMEM((GROUPS * units, SPLIT * tokens), BF16)] * 3,
-            blocks_scratch,
-            blocks_scratch,
+            pltpu.VMEM(blocks, BF16),
+            pltpu.VMEM(blocks, BF16),
             pltpu.VMEM((parts,) + term_shape, BF16),
-            sems,
+            pltpu.SemaphoreType.DMA((6 + 3 * weights.shape[0] * GROUPS + 2 * SPLIT + 2 * parts,)),
         ),
         flops=20 * 2**30,
-    )
-    grads, grads_sent, branch, branch_sent = [swap(v) for v in outs[:4]]
+        limit=56,
+    )
+    grads, grads_sent, branch, branch_sent = outs[:4]
     terms = outs[4:]
     grads_sent = swap_bit(grads_sent, 0)
     grad_far = swap_bit(add_rounded(grads[1], grads_sent[1]), 1)
     branch_sent = swap_bit(branch_sent, 0)
-    branch_sum = add_rounded(branch[1], branch_sent[1])
-    branch_far = swap_bit(branch_sum, 1)
     def reduce_terms(terms):
         if parts == 2:
             return add_rounded(terms[1], swap_bit(terms[0], SPLIT_BITS))
@@ -618,18 +598,20 @@
         [((tokens, width), F32)]
         + [((tokens, 2 * vw), BF16)] * 2
         + [((width, H * DV + LANES), BF16)],
-        (member_arr, grads, grads_sent, after(grad_far, branch_sum), middle, gain8, cotangent, attended, output_mat),
+        (member_arr, grads, grads_sent, after(grad_far, sums[0]), middle, gain8, cotangent, attended, output_mat),
         scalars=1,
         scratch=(pltpu.VMEM((tokens, H * DV), BF16),),
         flops=2**30,
+        limit=56,
     )
     att_grad = [away(part, mask) for part, mask in zip(att_grad, (0, 2))]
-    output_term = output_term.reshape((2,) * bits + (GROUPS, rows, H * DV + LANES))
+    output_term = after(output_term, *att_grad).reshape((2,) * bits + (GROUPS, rows, H * DV + LANES))
     output_term = reduce_bits(output_term, [0], range(bits))
     att_sent = jnp.concatenate([part[:, vw:] for part in att_grad], axis=1)
     att_grad.append(swap_bit(after(att_sent, sums[0]), 0))
     output_term = reduce_bits(output_term, links[:1], links)
-    att_grad = [after(part, *sums) for part in att_grad]
+    branch_far = swap_bit(add_rounded(branch[1], branch_sent[1]), 1)
+    att_grad = [after(part, sums[0]) for part in att_grad]
     input_parts, input_sent, attn_term = kernel_call(
         back_body,
         [((2, tokens, width), BF16)] * 2 + [((width, cols), BF16)],
@@ -641,12 +623,41 @@
             pltpu.VMEM((vw // DV, length, LANES), BF16),
             pltpu.VMEM((length, vw), BF16),
             pltpu.VMEM((length, cols), BF16),
+            pltpu.VMEM(hr.shape, BF16),
+            pltpu.VMEM(attn_mat.shape, BF16),
+            pltpu.SemaphoreType.DMA((2,)),
         ),
         flops=12 * 2**30,
+        remote=2,
+        limit=56,
     )
     input_sent = swap_bit(input_sent, 0)
-    input_parts = [after(add_rounded(input_parts[k], input_sent[k]), *totals) for k in range(2)]
+    input_parts = [after(add_rounded(input_parts[k], input_sent[k]), sums[1]) for k in range(2)]
     input_parts = [home(input_parts[0], 0), home(input_parts[1], 2)]
+    total = jnp.concatenate(totals, axis=0).astype(F32)
+    lanes = [total[:, j * block : (j + 1) * block] for j in range(SPLIT)]
+
+    def share_total():
+        own = [jnp.where(core == 0, lanes[x], lanes[x + 1]) for x in (0, 2)]
+        sent = [jnp.where(core == 0, lanes[x + 1], lanes[x]) for x in (0, 2)]
+        near = swap_bit(jnp.concatenate(sent, axis=1), 0)
+        near = [near[:, :block], near[:, block:]]
+        mine = [jnp.where(side == 0, both[0], both[1]) for both in (own, near)]
+        sent = [jnp.where(side == 0, both[1], both[0]) for both in (own, near)]
+        far = swap_bit(jnp.concatenate(sent, axis=0).astype(BF16), 1).astype(F32)
+        return in_place([*mine, far[: 3 * units], far[3 * units :]]), far
+
+    attn_term = after(attn_term, input_sent).reshape((2,) * len(links) + (2, GROUPS, rows, cols))
+    attn_term = reduce_bits(attn_term, links[:0:-1], links)
+    output_term = reduce_bits(output_term, links[1:], links[1:])
+    attn_term = reduce_bits(attn_term, links[:1], links[:1])
+    shares, shares_last = share_total()
+    other = swap_bit(pick(attn_term, 1 - core), 0)
+    attn_term = pair_up(core, pick(attn_term, core), other, 2).reshape(GROUPS, rows, 2 * cols)
+    both = jnp.concatenate([attn_term, output_term], axis=2)
+    kept, sent = ([pick(both, member ^ m) for m in pair] for pair in ((0, 2), (1, 3)))
+    sent = after(jnp.stack(sent), *totals)
+    input_parts = [after(part, sent) for part in input_parts]
     scaled_grad = input_parts[0].astype(F32) + input_parts[1].astype(F32)
     residual = hidden_in.astype(F32)
     scale = lax.rsqrt(jnp.mean(residual * residual, axis=1, keepdims=True) + EPSILON)
@@ -654,32 +665,18 @@
     inner = jnp.mean(normed * scaled_grad, axis=1, keepdims=True)
     input_grad = middle_grad + scale * (scaled_grad - normed * inner)
 
-    total = jnp.concatenate(totals, axis=0).astype(F32)
-    lanes = [slice(j * block, (j + 1) * block) for j in range(SPLIT)]
-
-    def share_total():
-        near = swap_bit(jnp.concatenate([total[:, lanes[1]], total[:, lanes[3]]], axis=1), 0)
-        far = jnp.concatenate([total[:, lanes[2]], near[:, block:]], axis=0).astype(BF16)
-        return near, swap_bit(far, 1).astype(F32)
-
-    attn_term = after(attn_term, input_sent).reshape((2,) * len(links) + (2, GROUPS, rows, cols))
-    attn_term = reduce_bits(attn_term, links[:0:-1], links)
-    output_term = reduce_bits(output_term, links[1:], links[1:])
-    attn_term = reduce_bits(attn_term, links[:1], links[:1])
-    attn_term = attn_term.transpose(1, 2, 0, 3).reshape(GROUPS, rows, 2 * cols)
-    both = jnp.concatenate([attn_term, output_term], axis=2)
-    both = [pick(both, member ^ m) for m in range(GROUPS)]
-    both = [both[0]] + [cross(after(both[m], *totals), m) for m in range(1, GROUPS)]
-    output_sum = sum(part[:, 2 * cols :].astype(F32) for part in both)
+    sent = cross(sent, 1)
+    out = [add_rounded(kept[k][:, 2 * cols :], sent[k][:, 2 * cols :]) for k in range(2)]
+    same, flip = ([part[k][:, : 2 * cols] for k in range(2)] for part in (kept, sent))
+    last = after(jnp.concatenate([same[1], flip[1], out[1]], axis=1), shares_last)
+    last = cross(last, 2).astype(F32)
+    output_sum = out[0].astype(F32) + last[:, 4 * cols :]
     output_grad = output_sum[:, : H * DV].T
     mlp_gain_grad = output_sum[:, H * DV]
-    same = both[0][:, : 2 * cols].astype(F32) + both[2][:, : 2 * cols].astype(F32)
-    flip = both[1][:, : 2 * cols].astype(F32) + both[3][:, : 2 * cols].astype(F32)
-    halves = pair_up(member & 1, same, flip, 0).reshape(2, rows, 2, cols)
-    near, far = share_total()
-    halves = after(halves, far)
-    halves = pair_up(core, pick(halves, core, 2), swap_bit(pick(halves, 1 - core, 2), 0), 1)
-    attn_grad = halves.reshape(GROUPS, rows, cols).transpose(1, 0, 2)
+    same = same[0].astype(F32) + last[:, : 2 * cols]
+    flip = flip[0].astype(F32) + last[:, 2 * cols : 4 * cols]
+    attn_grad = pair_up(member & 1, same, flip, 0).reshape(2, rows, 2, cols)
+    attn_grad = attn_grad.transpose(1, 0, 2, 3).reshape(rows, GROUPS, cols)
     scale_rows = gain_attn.astype(F32)[:, None]
     query_raw = attn_grad[:, :, :qk].reshape(rows, H * HF)
     key_raw = attn_grad[:, :, qk : 2 * qk].reshape(rows, H * HF)
@@ -697,9 +694,6 @@
         + branch_far.astype(F32)
     ).astype(BF16)
 
-    shares = [total[:, lanes[0]], near[:, :block], far[: 3 * units], far[3 * units :]]
-    shares = [jnp.where(core == 0, shares[k], shares[k ^ 1]) for k in range(SPLIT)]
-    shares = [jnp.where(side == 0, shares[k], shares[k ^ 2]) for k in range(SPLIT)]
     total = jnp.stack([share.reshape(3, units, block) for share in shares], axis=1)
     total = total.reshape(3, SPLIT * units, block)[:, :hidden_units]
     return (

time: 325 us -> 309 us (0.951)
  starting transfers between devices: 68.6 us -> 54.8 us
  Pallas kernels: 68.1 us -> 58 us
  waiting for transfers between devices: 126 us -> 132 us
    ppermute x4, waiting for transfers between devices: 8.81 us -> 25.8 us  [away(): lax.ppermute(block, ('bit0', 'feat'), [(b, a) for a, b in home_pairs(mask)])]
    ppermute x5 -> x4, starting transfers between devices: 14.3 us -> 0.86 us  [cross(): return lax.ppermute(block, 'feat', [(i, i ^ mask) for i in range(GROUPS)])]
    pallas_call x5, Pallas kernels: 68.1 us -> 58 us  [kernel_call(): pl.pallas_call(body, out_shape=outs, in_specs=[smem] * scalars + [vmem] *...]
    ppermute x30, waiting for transfers between devices: 75.8 us -> 65.9 us  [hop(): return lax.ppermute(block, f'bit{bit}', [(0, 1), (1, 0)])]
    ppermute x5 -> x4, waiting for transfers between devices: 28.7 us -> 33.6 us  [cross(): return lax.ppermute(block, 'feat', [(i, i ^ mask) for i in range(GROUPS)])]
    convert_element_type x9 -> x11, other arithmetic: 9.63 us -> 13.4 us  [add_rounded(): return (first.astype(F32) + second.astype(F32)).astype(BF16)]
    reduce_scatter x2, waiting for transfers between devices: 3.5 us -> 0.01 us  [on_device(): totals = [lax.psum_scatter(term, 'feat') for term in sums]]
    unnamed x62 -> x76, local copies, waits for them, and re-layouts: 4.15 us -> 7.29 us
  transfers between devices with their start and end apart: 46 -> 45, of which waited for: 19 -> 21; matrix products, arithmetic and copies ran while one was open for 11% -> 11% of each run, Pallas kernels for 10% -> 8%
where the time goes in v2:
time: 309 us; the launch traced here: 307 us
  waiting for transfers between devices  132 us (43%)
  Pallas kernels  58 us (19%)
  starting transfers between devices  54.8 us (18%)
  other arithmetic  27.6 us (9%)
  local copies, waits for them, and re-layouts  17.8 us (6%)
  between operations  16.4 us (5%)
    ppermute x30, waiting for transfers between devices, hop(): return lax.ppermute(block, f'bit{bit}', [(0, 1), (1, 0)])  65.9 us
    pallas_call x5, Pallas kernels, kernel_call(): pl.pallas_call(body, out_shape=outs, in_specs=[smem] * scalars + [vmem] *...  58 us
    ppermute x30, starting transfers between devices, hop(): return lax.ppermute(block, f'bit{bit}', [(0, 1), (1, 0)])  36.1 us
    ppermute x4, waiting for transfers between devices, cross(): return lax.ppermute(block, 'feat', [(i, i ^ mask) for i in range(GROUPS)])  33.6 us
    ppermute x4, waiting for transfers between devices, away(): lax.ppermute(block, ('bit0', 'feat'), [(b, a) for a, b in home_pairs(mask)])  25.8 us
    convert_element_type x11, other arithmetic, add_rounded(): return (first.astype(F32) + second.astype(F32)).astype(BF16)  13.4 us
    ppermute x4, starting transfers between devices, away(): lax.ppermute(block, ('bit0', 'feat'), [(b, a) for a, b in home_pairs(mask)])  10.8 us
    unnamed x76, local copies, waits for them, and re-layouts  7.29 us
  transfers between devices with their start and end apart: 45, of which 21 were waited for; matrix products, arithmetic and copies ran while one was open for 11% of the time, Pallas kernels for 8%

profile of v2, /device:TPU:0, one launch (start us, length us, event | category | flops | bytes accessed | tf_op | source)
XLA Modules:
  0.0 306.6 jit_solution(12479214214811304900)
XLA Ops:
  7.2 1.7 collective-permute-start.1
  8.9 3.3 %collective-permute-start.2 = (bf16[256,1024]{1,0:T(8,128)(2,1)}, bf16[256,1024]{1,0:T(8,128)(2,1)S(1)}, u32[]{:S(2)}, u32[]{:S(2)}) collective-permute-start(bf16[256,1024]{1,0:T(8,128)(2,1)} %hidden_ref.1), channel_id=1, source_target_pairs={{2,0},{0,1},{6,2},{4,3},{3,4},{1,5},{7,6},{5,7},{10,8},{8,9},{14,1... | collective-permute-start | bytes 1572872 | tf_op jit(solution)/shard_map/ppermute | solution.py:66
  16.3 2.2 collective-permute-start
  18.5 1.2 fusion.17
  19.7 1.6 collective-permute-start.3
  22.3 5.9 %collective-permute-done.3 = bf16[3,2,176,128]{3,2,1,0:T(8,128)(2,1)S(1)} collective-permute-done((bf16[3,2,176,128]{3,2,1,0:T(8,128)(2,1)S(1)}, bf16[3,2,176,128]{3,2,1,0:T(8,128)(2,1)S(1)}, u32[]{:S(2)}, u32[]{:S(2)}) %collective-permute-start.3) | collective-permute-done | bytes 270368 | tf_op jit(solution)/shard_map/ppermute | solution.py:45
  28.3 16.9 %collective-permute-done.6 = bf16[32,2688]{1,0:T(8,128)(2,1)S(1)} collective-permute-done((bf16[32,2688]{1,0:T(8,128)(2,1)S(1)}, bf16[32,2688]{1,0:T(8,128)(2,1)S(1)}, u32[]{:S(2)}, u32[]{:S(2)}) %collective-permute-start.6) | collective-permute-done | bytes 172064 | tf_op jit(solution)/shard_map/ppermute | solution.py:49
  45.5 0.9 pad_maximum_fusion.6
  46.5 5.1 %collective-permute-done.7 = bf16[64,1920]{1,0:T(8,128)(2,1)S(1)} collective-permute-done((bf16[64,1920]{1,0:T(8,128)(2,1)S(1)}, bf16[64,1920]{1,0:T(8,128)(2,1)S(1)}, u32[]{:S(2)}, u32[]{:S(2)}) %collective-permute-start.7) | collective-permute-done | bytes 245792 | tf_op jit(solution)/shard_map/ppermute | solution.py:49
  51.7 1.6 collective-permute-start.8
  53.3 1.6 collective-permute-start.9
  54.9 1.0 pad_maximum_fusion.3
  58.1 9.5 %collective-permute-done.9 = bf16[128,1152]{1,0:T(8,128)(2,1)S(1)} collective-permute-done((bf16[128,1152]{1,0:T(8,128)(2,1)S(1)}, bf16[128,1152]{1,0:T(8,128)(2,1)S(1)}, u32[]{:S(2)}, u32[]{:S(2)}) %collective-permute-start.9) | collective-permute-done | bytes 294944 | tf_op jit(solution)/shard_map/ppermute | solution.py:45
  67.7 2.1 collective-permute-start.10
  70.0 5.5 %collective-permute-done.10 = bf16[4,4,32,384]{3,2,1,0:T(8,128)(2,1)S(1)} collective-permute-done((bf16[4,4,32,384]{3,2,1,0:T(8,128)(2,1)S(1)}, bf16[4,4,32,384]{3,2,1,0:T(8,128)(2,1)S(1)}, u32[]{:S(2)}, u32[]{:S(2)}) %collective-permute-start.10) | collective-permute-done | bytes 393248 | tf_op jit(solution)/shard_map/ppermute | solution.py:45
  75.8 5.2 %shard_map.203 = (bf16[4,256,1024]{2,1,0:T(8,128)(2,1)S(1)}, bf16[1024,384]{1,0:T(8,128)(2,1)S(1)}, bf16[256,512]{1,0:T(8,128)(2,1)S(1)}, bf16[256,512]{1,0:T(8,...) custom-call(s32[1]{0:T(128)S(6)} %select_n.316.first_ref, s32[1]{0:T(128)} %bitcast.7.group_ref, ...), custom_call_target="tpu_custom_call" | custom-call | flops 8589934592 | bytes 8388616 | tf_op jit(solution)/shard_map/pallas_call | solution.py:99
  81.0 1.0 copy-done.10
  82.1 2.0 collective-permute-start.16
  85.0 1.7 collective-permute-start.13
  86.8 0.9 collective-permute-start.12
  87.7 8.9 %collective-permute-done.16.refs_5_ = bf16[256,1024]{1,0:T(8,128)(2,1)S(1)} collective-permute-done((bf16[256,1024]{1,0:T(8,128)(2,1)S(1)}, bf16[256,1024]{1,0:T(8,128)(2,1)S(1)}, u32[]{:S(2)}, u32[]{:S(2)}) %collective-permute-start.16) | collective-permute-done | bytes 524320 | tf_op jit(solution)/shard_map/ppermute | solution.py:45
  97.5 6.2 %collective-permute-done.13.a1_ref = bf16[256,512]{1,0:T(8,128)(2,1)S(1)} collective-permute-done((bf16[256,512]{1,0:T(8,128)(2,1)S(1)}, bf16[256,512]{1,0:T(8,128)(2,1)S(1)}, u32[]{:S(2)}, u32[]{:S(2)}) %collective-permute-start.13) | collective-permute-done | bytes 262176 | tf_op jit(solution)/shard_map/ppermute | solution.py:62
  103.8 0.9 shard_map.204
  104.7 1.0 copy-done.2
  107.1 1.4 collective-permute-start.17
  108.5 7.8 %collective-permute-done.17.refs_2_ = bf16[256,1024]{1,0:T(8,128)(2,1)S(1)} collective-permute-done((bf16[256,1024]{1,0:T(8,128)(2,1)S(1)}, bf16[256,1024]{1,0:T(8,128)(2,1)S(1)}, u32[]{:S(2)}, u32[]{:S(2)}) %collective-permute-start.17) | collective-permute-done | bytes 524320 | tf_op jit(solution)/shard_map/ppermute | solution.py:45
  116.4 12.0 %collective-permute-start.19 = (bf16[512,1024]{1,0:T(8,128)(2,1)S(1)}, bf16[512,1024]{1,0:T(8,128)(2,1)}, u32[]{:S(2)}, u32[]{:S(2)}) collective-permute-start(bf16[512,1024]{1,0:T(8,128)(2,1)S(1)} %pad_maximum_fusion.4), channel_id=1, source_target_pairs={{0,4},{4,0},{1,5},{5,1},{2,6},{6,2},{3,7},{7,3},{8,12},{12,8},{9,1... | collective-permute-start | bytes 3145736 | tf_op jit(solution)/shard_map/ppermute | solution.py:45
  128.4 2.4 collective-permute-done.19.refs_3_
  131.2 32.0 %shard_map.205 = (bf16[2,256,1024]{2,1,0:T(8,128)(2,1)}, bf16[2,256,1024]{2,1,0:T(8,128)(2,1)}, bf16[2,256,1024]{2,1,0:T(8,128)(2,1)}, bf16[2,256,1024]{2,1,0:T(...) custom-call(s32[1]{0:T(128)} %bitcast.43.refs_0_, ...), custom_call_target="tpu_custom_call" | custom-call | flops 21474836480 | bytes 17039364 | tf_op jit(solution)/shard_map/pallas_call | solution.py:99
  163.3 1.6 collective-permute-start.23
  164.9 1.2 collective-permute-done.20.near_ref
  166.2 1.6 fusion.19
  167.8 1.5 collective-permute-start.22
  169.3 12.8 %collective-permute-done.23 = bf16[4,176,512]{2,1,0:T(8,128)(2,1)S(1)} collective-permute-done((bf16[4,176,512]{2,1,0:T(8,128)(2,1)}, bf16[4,176,512]{2,1,0:T(8,128)(2,1)S(1)}, u32[]{:S(2)}, u32[]{:S(2)}) %collective-permute-start.23) | collective-permute-done | bytes 720928 | tf_op jit(solution)/shard_map/ppermute | solution.py:45
  182.1 1.4 collective-permute-start.31
  183.5 1.1 add_convert_fusion.1
  184.6 6.4 %shard_map.206 = (f32[256,1024]{1,0:T(8,128)}, bf16[256,512]{1,0:T(8,128)(2,1)}, bf16[256,512]{1,0:T(8,128)(2,1)}, bf16[1024,1152]{1,0:T(8,128)(2,1)}) custom-call(s32[1]{0:T(128)} %bitcast.member_ref, bf16[2,256,1024]{2,1,0:T(8,128)(2,1)} %get-tuple-element.104.own_ref, bf16[2,256,1024]{2,1,0:T(8,128)(2,1)} %copy-done.12, bf16[256,1024]{1,0:T(8,128)(2,1)} %copy-done.25, ...), custom_call_target="tpu_custom_call" | custom-call | flops 1073741824 | bytes 11042820 | tf_op jit(solution)/shard_map/pallas_call | solution.py:99
  191.0 1.6 collective-permute-start.24
  192.6 4.2 %collective-permute-start.25 = (bf16[256,512]{1,0:T(8,128)(2,1)}, bf16[256,512]{1,0:T(8,128)(2,1)S(1)}, u32[]{:S(2)}, u32[]{:S(2)}) collective-permute-start(bf16[256,512]{1,0:T(8,128)(2,1)} %get-tuple-element.115), channel_id=1, source_target_pairs={{2,0},{0,1},{6,2},{4,3},{3,4},{1,5},{7,6},{5,7},{10,8},{8,9},{14,1... | collective-permute-start | bytes 786440 | tf_op jit(solution)/shard_map/ppermute | solution.py:66
  196.8 25.8 %collective-permute-done.25.g1_ref = bf16[256,512]{1,0:T(8,128)(2,1)S(1)} collective-permute-done((bf16[256,512]{1,0:T(8,128)(2,1)}, bf16[256,512]{1,0:T(8,128)(2,1)S(1)}, u32[]{:S(2)}, u32[]{:S(2)}) %collective-permute-start.25) | collective-permute-done | bytes 262176 | tf_op jit(solution)/shard_map/ppermute | solution.py:66
  222.6 2.0 constant_dynamic-slice_fusion.1
  224.6 1.2 copy.88
  225.8 1.0 copy-done.18
  227.5 2.9 add_convert_fusion
  231.5 1.5 fusion
  234.7 13.4 %shard_map.207 = (bf16[2,256,1024]{2,1,0:T(8,128)(2,1)}, bf16[2,256,1024]{2,1,0:T(8,128)(2,1)}, bf16[1024,384]{1,0:T(8,128)(2,1)}) custom-call(s32[1]{0:T(128)S(6)} %select_n.316.first_ref, s32[1]{0:T(128)} %bitcast.7.group_ref, bf16[256,512]{1,0:T(8,128)(2,1)} %copy-done.31, bf16[256,512]{1,0:T(8,128)(2,1)} %copy-done.32, bf16[256,512]{1,0:T(8,128)(2,1)} %copy-done.35, ...), custom_call_target="tpu_custom_call" | custom-call | flops 12884901888 | bytes 9437192 | tf_op jit(solution)/shard_map/pallas_call | solution.py:99
  248.6 1.3 fusion.18
  249.9 1.3 collective-permute-start.28
  251.2 1.2 fusion.3
  253.9 2.6 fusion.20
  256.5 1.7 collective-permute-start.32
  258.2 2.5 collective-permute-start.38
  260.7 2.9 collective-permute-done.33
  264.4 1.0 collective-permute-start.34
  265.4 0.9 collective-permute-start.37
  266.4 1.2 maximum_convert_fusion
  267.8 3.0 collective-permute-done.34
  270.8 1.0 fusion.22
  271.8 1.9 collective-permute-done.37
  277.2 2.5 fusion.10
  279.7 3.3 %collective-permute-done.40 = bf16[1056,128]{1,0:T(8,128)(2,1)S(1)} collective-permute-done((bf16[1056,128]{1,0:T(8,128)(2,1)S(1)}, bf16[1056,128]{1,0:T(8,128)(2,1)S(1)}, u32[]{:S(2)}, u32[]{:S(2)}) %collective-permute-start.40) | collective-permute-done | bytes 270368 | tf_op jit(solution)/shard_map/ppermute | solution.py:45
  283.4 3.1 %collective-permute-done.39 = bf16[2,32,1920]{2,1,0:T(8,128)(2,1)S(1)} collective-permute-done((bf16[2,32,1920]{2,1,0:T(8,128)(2,1)S(1)}, bf16[2,32,1920]{2,1,0:T(8,128)(2,1)S(1)}, u32[]{:S(2)}, u32[]{:S(2)}) %collective-permute-start.39) | collective-permute-done | bytes 245792 | tf_op jit(solution)/shard_map/ppermute | solution.py:49
  286.7 1.0 slice_bitcast_fusion.1
  287.6 8.6 %collective-permute-done.41 = bf16[32,2688]{1,0:T(8,128)(2,1)S(1)} collective-permute-done((bf16[32,2688]{1,0:T(8,128)(2,1)S(1)}, bf16[32,2688]{1,0:T(8,128)(2,1)S(1)}, u32[]{:S(2)}, u32[]{:S(2)}) %collective-permute-start.41) | collective-permute-done | bytes 172064 | tf_op jit(solution)/shard_map/ppermute | solution.py:49
  (225 shorter events, 24.5 us)
Async XLA Ops:
  7.2 124.0 %all-gather.3.cloned.1.call-start = ((), (), s32[]{:S(2)}) async-start(), calls=%async_computation.4 | async-start | bytes 4866048 | tf_op jit(solution)/shard_map/all_gather | solution.py:513
  7.2 38.1 %collective-permute-start.1 = (bf16[256,1024]{1,0:T(8,128)(2,1)}, bf16[256,1024]{1,0:T(8,128)(2,1)S(1)}, u32[]{:S(2)}, u32[]{:S(2)}) collective-permute-start(bf16[256,1024]{1,0:T(8,128)(2,1)} %hidden_ref.1), channel_id=1, source_target_pairs={{0,0},{2,1},{4,2},{6,3},{1,4},{3,5},{5,6},{7,7},{8,8},{10,9},{12,1... | collective-permute-start | bytes 1572872 | tf_op jit(solution)/shard_map/ppermute | solution.py:66
  8.9 36.4 %collective-permute-start.2 = (bf16[256,1024]{1,0:T(8,128)(2,1)}, bf16[256,1024]{1,0:T(8,128)(2,1)S(1)}, u32[]{:S(2)}, u32[]{:S(2)}) collective-permute-start(bf16[256,1024]{1,0:T(8,128)(2,1)} %hidden_ref.1), channel_id=1, source_target_pairs={{2,0},{0,1},{6,2},{4,3},{3,4},{1,5},{7,6},{5,7},{10,8},{8,9},{14,1... | collective-permute-start | bytes 1572872 | tf_op jit(solution)/shard_map/ppermute | solution.py:66
  15.4 5.8 %copy-start.33 = (bf16[32]{0:T(256)(128)(2,1)S(1)}, bf16[32]{0:T(256)(128)(2,1)}, u32[]{:S(2)}) copy-start(bf16[32]{0:T(256)(128)(2,1)} %param.21) | copy-start | bytes 196
  16.3 5.1 %collective-permute-start = (bf16[80,384]{1,0:T(8,128)(2,1)S(1)}, bf16[80,384]{1,0:T(8,128)(2,1)S(1)}, u32[]{:S(2)}, u32[]{:S(2)}) collective-permute-start(bf16[80,384]{1,0:T(8,128)(2,1)S(1)} %concatenate.114), channel_id=1, source_target_pairs={{0,4},{4,0},{1,5},{5,1},{2,6},{6,2},{3,7},{7,3},{8,12},{12,8},{9,1... | collective-permute-start | bytes 184328 | tf_op jit(solution)/shard_map/ppermute | solution.py:45
  18.5 3.1 %copy-start.24 = (bf16[1024,32]{0,1:T(8,128)(2,1)S(1)}, bf16[1024,32]{0,1:T(8,128)(2,1)}, u32[]{:S(2)}) copy-start(bf16[1024,32]{0,1:T(8,128)(2,1)} %param.16) | copy-start | bytes 196612
  19.7 8.5 %collective-permute-start.3 = (bf16[3,2,176,128]{3,2,1,0:T(8,128)(2,1)S(1)}, bf16[3,2,176,128]{3,2,1,0:T(8,128)(2,1)S(1)}, u32[]{:S(2)}, u32[]{:S(2)}) collective-permute-start(bf16[3,2,176,128]{3,2,1,0:T(8,128)(2,1)S(1)} %dynamic-slice_bitcast_fusion.3), channel_id=1, source_target_pairs={{0,8},{8,0},{1,9},{9,1},{2,10},{10,2},{3,11},{11,3},{4,12},{12,4},... | collective-permute-start | bytes 811016 | tf_op jit(solution)/shard_map/ppermute | solution.py:45
  21.6 23.6 %collective-permute-start.6 = (bf16[32,2688]{1,0:T(8,128)(2,1)S(1)}, bf16[32,2688]{1,0:T(8,128)(2,1)S(1)}, u32[]{:S(2)}, u32[]{:S(2)}) collective-permute-start(bf16[32,2688]{1,0:T(8,128)(2,1)S(1)} %pad_maximum_fusion.15), channel_id=1, source_target_pairs={{0,2},{1,3},{2,0},{3,1},{4,6},{5,7},{6,4},{7,5},{8,10},{9,11},{10,... | collective-permute-start | bytes 516104 | tf_op jit(solution)/shard_map/ppermute | solution.py:49
  28.2 17.2 %collective-permute-start.4 = (bf16[3,176,256]{2,1,0:T(8,128)(2,1)S(1)}, bf16[3,176,256]{2,1,0:T(8,128)(2,1)S(1)}, u32[]{:S(2)}, u32[]{:S(2)}) collective-permute-start(bf16[3,176,256]{2,1,0:T(8,128)(2,1)S(1)} %pad_maximum_fusion.8), channel_id=1, source_target_pairs={{0,4},{4,0},{1,5},{5,1},{2,6},{6,2},{3,7},{7,3},{8,12},{12,8},{9,1... | collective-permute-start | bytes 811016 | tf_op jit(solution)/shard_map/ppermute | solution.py:45
  45.3 6.3 %collective-permute-start.7 = (bf16[64,1920]{1,0:T(8,128)(2,1)S(1)}, bf16[64,1920]{1,0:T(8,128)(2,1)S(1)}, u32[]{:S(2)}, u32[]{:S(2)}) collective-permute-start(bf16[64,1920]{1,0:T(8,128)(2,1)S(1)} %pad_maximum_fusion.13), channel_id=1, source_target_pairs={{0,1},{1,0},{2,3},{3,2},{4,5},{5,4},{6,7},{7,6},{8,9},{9,8},{10,11... | collective-permute-start | bytes 737288 | tf_op jit(solution)/shard_map/ppermute | solution.py:49
  46.4 220.0 %reduce-scatter.3.cloned.1.call-start = ((), (), s32[]{:S(2)}) async-start(), calls=%async_computation.2 | async-start | bytes 901120 | tf_op jit(solution)/shard_map/reduce_scatter | solution.py:594
  51.7 5.7 %collective-permute-start.8 = (bf16[2,4,32,384]{3,0,2,1:T(2,128)(2,1)S(1)}, bf16[2,4,32,384]{3,0,2,1:T(2,128)(2,1)S(1)}, u32[]{:S(2)}, u32[]{:S(2)}) collective-permute-start(bf16[2,4,32,384]{3,0,2,1:T(2,128)(2,1)S(1)} %bitcast.210), channel_id=1, source_target_pairs={{0,8},{8,0},{1,9},{9,1},{2,10},{10,2},{3,11},{11,3},{4,12},{12,4},... | collective-permute-start | bytes 589832 | tf_op jit(solution)/shard_map/ppermute | solution.py:45
  53.3 14.3 %collective-permute-start.9 = (bf16[128,1152]{1,0:T(8,128)(2,1)S(1)}, bf16[128,1152]{1,0:T(8,128)(2,1)S(1)}, u32[]{:S(2)}, u32[]{:S(2)}) collective-permute-start(bf16[128,1152]{1,0:T(8,128)(2,1)S(1)} %bitcast.186), channel_id=1, source_target_pairs={{0,16},{16,0},{1,17},{17,1},{2,18},{18,2},{3,19},{19,3},{4,20},{20... | collective-permute-start | bytes 884744 | tf_op jit(solution)/shard_map/ppermute | solution.py:45
  55.9 19.8 %collective-permute-start.5 = (bf16[512,1024]{1,0:T(8,128)(2,1)}, bf16[512,1024]{1,0:T(8,128)(2,1)S(1)}, u32[]{:S(2)}, u32[]{:S(2)}) collective-permute-start(bf16[512,1024]{1,0:T(8,128)(2,1)} %pad_maximum_fusion.3), channel_id=1, source_target_pairs={{0,4},{4,0},{1,5},{5,1},{2,6},{6,2},{3,7},{7,3},{8,12},{12,8},{9,1... | collective-permute-start | bytes 3145736 | tf_op jit(solution)/shard_map/ppermute | solution.py:45
  67.7 14.4 %collective-permute-start.14 = (bf16[2,128,1152]{2,1,0:T(8,128)(2,1)S(1)}, bf16[2,128,1152]{2,1,0:T(8,128)(2,1)S(1)}, u32[]{:S(2)}, u32[]{:S(2)}) collective-permute-start(bf16[2,128,1152]{2,1,0:T(8,128)(2,1)S(1)} %maximum_select_fusion.4), channel_id=1, source_target_pairs={{0,8},{8,0},{1,9},{9,1},{2,10},{10,2},{3,11},{11,3},{4,12},{12,4},... | collective-permute-start | bytes 1769480 | tf_op jit(solution)/shard_map/ppermute | solution.py:45
  67.7 7.8 %collective-permute-start.10 = (bf16[4,4,32,384]{3,2,1,0:T(8,128)(2,1)S(1)}, bf16[4,4,32,384]{3,2,1,0:T(8,128)(2,1)S(1)}, u32[]{:S(2)}, u32[]{:S(2)}) collective-permute-start(bf16[4,4,32,384]{3,2,1,0:T(8,128)(2,1)S(1)} %bitcast.201), channel_id=1, source_target_pairs={{0,16},{16,0},{1,17},{17,1},{2,18},{18,2},{3,19},{19,3},{4,20},{20... | collective-permute-start | bytes 1179656 | tf_op jit(solution)/shard_map/ppermute | solution.py:45
  75.7 5.3 %copy-start.4 = (bf16[2,4,4,32,384]{4,3,2,1,0:T(8,128)(2,1)}, bf16[2,4,4,32,384]{4,3,2,1,0:T(8,128)(2,1)S(1)}, u32[]{:S(2)}) copy-start(bf16[2,4,4,32,384]{4,3,2,1,0:T(8,128)(2,1)S(1)} %maximum_select_fusion.2) | copy-start | bytes 2359300
  75.8 6.3 %copy-start.13 = (bf16[256,1024]{1,0:T(8,128)(2,1)S(1)}, bf16[256,1024]{1,0:T(8,128)(2,1)}, u32[]{:S(2)}) copy-start(bf16[256,1024]{1,0:T(8,128)(2,1)} %cot_ref.1) | copy-start | bytes 1572868
  82.0 2.3 copy-start.9
  82.0 2.3 copy-start.11
  82.0 2.6 collective-permute-start.11
  82.1 14.6 %collective-permute-start.16 = (bf16[256,1024]{1,0:T(8,128)(2,1)S(1)}, bf16[256,1024]{1,0:T(8,128)(2,1)S(1)}, u32[]{:S(2)}, u32[]{:S(2)}) collective-permute-start(bf16[256,1024]{1,0:T(8,128)(2,1)S(1)} %copy-done.13), channel_id=1, source_target_pairs={{0,8},{8,0},{1,9},{9,1},{2,10},{10,2},{3,11},{11,3},{4,12},{12,4},... | collective-permute-start | bytes 1572872 | tf_op jit(solution)/shard_map/ppermute | solution.py:45
  84.6 12.2 %collective-permute-start.15 = (bf16[2,2,128,1152]{3,2,1,0:T(8,128)(2,1)S(1)}, bf16[2,2,128,1152]{3,2,1,0:T(8,128)(2,1)S(1)}, u32[]{:S(2)}, u32[]{:S(2)}) collective-permute-start(bf16[2,2,128,1152]{3,2,1,0:T(8,128)(2,1)S(1)} %maximum_select_fusion.1), channel_id=1, source_target_pairs={{0,4},{4,0},{1,5},{5,1},{2,6},{6,2},{3,7},{7,3},{8,12},{12,8},{9,1... | collective-permute-start | bytes 3538952 | tf_op jit(solution)/shard_map/ppermute | solution.py:45
  85.0 18.7 %collective-permute-start.13 = (bf16[256,512]{1,0:T(8,128)(2,1)S(1)}, bf16[256,512]{1,0:T(8,128)(2,1)S(1)}, u32[]{:S(2)}, u32[]{:S(2)}) collective-permute-start(bf16[256,512]{1,0:T(8,128)(2,1)S(1)} %pad_maximum_fusion.11), channel_id=1, source_target_pairs={{0,2},{1,0},{2,6},{3,4},{4,3},{5,1},{6,7},{7,5},{8,10},{9,8},{10,1... | collective-permute-start | bytes 786440 | tf_op jit(solution)/shard_map/ppermute | solution.py:62
  86.8 17.0 %collective-permute-start.12 = (bf16[256,512]{1,0:T(8,128)(2,1)S(1)}, bf16[256,512]{1,0:T(8,128)(2,1)S(1)}, u32[]{:S(2)}, u32[]{:S(2)}) collective-permute-start(bf16[256,512]{1,0:T(8,128)(2,1)S(1)} %pad_maximum_fusion.10), channel_id=1, source_target_pairs={{0,0},{1,2},{2,4},{3,6},{4,1},{5,3},{6,5},{7,7},{8,8},{9,10},{10,1... | collective-permute-start | bytes 786440 | tf_op jit(solution)/shard_map/ppermute | solution.py:62
  96.7 19.6 %collective-permute-start.18 = (bf16[512,1024]{1,0:T(8,128)(2,1)S(1)}, bf16[512,1024]{1,0:T(8,128)(2,1)S(1)}, u32[]{:S(2)}, u32[]{:S(2)}) collective-permute-start(bf16[512,1024]{1,0:T(8,128)(2,1)S(1)} %pad_maximum_fusion.5), channel_id=1, source_target_pairs={{0,4},{4,0},{1,5},{5,1},{2,6},{6,2},{3,7},{7,3},{8,12},{12,8},{9,1... | collective-permute-start | bytes 3145736 | tf_op jit(solution)/shard_map/ppermute | solution.py:45
  96.8 6.9 %copy-start.1 = (bf16[256,1024]{1,0:T(8,128)(2,1)S(1)}, bf16[256,1024]{1,0:T(8,128)(2,1)}, u32[]{:S(2)}) copy-start(bf16[256,1024]{1,0:T(8,128)(2,1)} %hidden_ref.1) | copy-start | bytes 1572868
  97.5 7.2 %copy-start = (bf16[2,2,2,128,1152]{4,3,2,1,0:T(8,128)(2,1)}, bf16[2,2,2,128,1152]{4,3,2,1,0:T(8,128)(2,1)S(1)}, u32[]{:S(2)}) copy-start(bf16[2,2,2,128,1152]{4,3,2,1,0:T(8,128)(2,1)S(1)} %maximum_select_fusion) | copy-start | bytes 7077892
  107.1 24.0 %copy-start.6 = (bf16[256,1024]{1,0:T(8,128)(2,1)}, bf16[256,1024]{1,0:T(8,128)(2,1)S(1)}, u32[]{:S(2)}) copy-start(bf16[256,1024]{1,0:T(8,128)(2,1)S(1)} %get-tuple-element.95.refs_1_) | copy-start | bytes 1572868
  107.1 9.2 %collective-permute-start.17 = (bf16[256,1024]{1,0:T(8,128)(2,1)S(1)}, bf16[256,1024]{1,0:T(8,128)(2,1)S(1)}, u32[]{:S(2)}, u32[]{:S(2)}) collective-permute-start(bf16[256,1024]{1,0:T(8,128)(2,1)S(1)} %get-tuple-element.95.refs_1_), channel_id=1, source_target_pairs={{0,8},{8,0},{1,9},{9,1},{2,10},{10,2},{3,11},{11,3},{4,12},{12,4},... | collective-permute-start | bytes 1572872 | tf_op jit(solution)/shard_map/ppermute | solution.py:45
  116.3 14.9 %copy-start.27 = (bf16[256,1024]{1,0:T(8,128)(2,1)}, bf16[256,1024]{1,0:T(8,128)(2,1)S(1)}, u32[]{:S(2)}) copy-start(bf16[256,1024]{1,0:T(8,128)(2,1)S(1)} %collective-permute-done.17.refs_2_) | copy-start | bytes 1572868
  116.4 14.8 %copy-start.34 = (bf16[512,1024]{1,0:T(8,128)(2,1)}, bf16[512,1024]{1,0:T(8,128)(2,1)S(1)}, u32[]{:S(2)}) copy-start(bf16[512,1024]{1,0:T(8,128)(2,1)S(1)} %collective-permute-done.18.refs_6_) | copy-start | bytes 3145732
  116.4 14.4 %collective-permute-start.19 = (bf16[512,1024]{1,0:T(8,128)(2,1)S(1)}, bf16[512,1024]{1,0:T(8,128)(2,1)}, u32[]{:S(2)}, u32[]{:S(2)}) collective-permute-start(bf16[512,1024]{1,0:T(8,128)(2,1)S(1)} %pad_maximum_fusion.4), channel_id=1, source_target_pairs={{0,4},{4,0},{1,5},{5,1},{2,6},{6,2},{3,7},{7,3},{8,12},{12,8},{9,1... | collective-permute-start | bytes 3145736 | tf_op jit(solution)/shard_map/ppermute | solution.py:45
  163.2 20.3 %copy-start.23 = (bf16[4,176,512]{2,1,0:T(8,128)(2,1)S(1)}, bf16[4,176,512]{2,1,0:T(8,128)(2,1)}, u32[]{:S(2)}) copy-start(bf16[4,176,512]{2,1,0:T(8,128)(2,1)} %get-tuple-element.107) | copy-start | bytes 2162692
  163.2 2.9 collective-permute-start.20
  163.3 18.8 %collective-permute-start.23 = (bf16[4,176,512]{2,1,0:T(8,128)(2,1)}, bf16[4,176,512]{2,1,0:T(8,128)(2,1)S(1)}, u32[]{:S(2)}, u32[]{:S(2)}) collective-permute-start(bf16[4,176,512]{2,1,0:T(8,128)(2,1)} %get-tuple-element.109), channel_id=1, source_target_pairs={{0,16},{16,0},{1,17},{17,1},{2,18},{18,2},{3,19},{19,3},{4,20},{20... | collective-permute-start | bytes 2162696 | tf_op jit(solution)/shard_map/ppermute | solution.py:45
  166.2 18.4 %copy-start.12 = (bf16[2,256,1024]{2,1,0:T(8,128)(2,1)}, bf16[2,256,1024]{2,1,0:T(8,128)(2,1)S(1)}, u32[]{:S(2)}) copy-start(bf16[2,256,1024]{2,1,0:T(8,128)(2,1)S(1)} %collective-permute-done.20.near_ref) | copy-start | bytes 3145732
  167.8 15.8 %collective-permute-start.22 = (bf16[256,1024]{1,0:T(8,128)(2,1)S(1)}, bf16[256,1024]{1,0:T(8,128)(2,1)S(1)}, u32[]{:S(2)}, u32[]{:S(2)}) collective-permute-start(bf16[256,1024]{1,0:T(8,128)(2,1)S(1)} %fusion.19), channel_id=1, source_target_pairs={{0,8},{8,0},{1,9},{9,1},{2,10},{10,2},{3,11},{11,3},{4,12},{12,4},... | collective-permute-start | bytes 1572872 | tf_op jit(solution)/shard_map/ppermute | solution.py:45
  169.3 56.5 %collective-permute-start.21 = (bf16[2,256,1024]{2,1,0:T(8,128)(2,1)}, bf16[2,256,1024]{2,1,0:T(8,128)(2,1)S(1)}, u32[]{:S(2)}, u32[]{:S(2)}) collective-permute-start(bf16[2,256,1024]{2,1,0:T(8,128)(2,1)} %get-tuple-element.103), channel_id=1, source_target_pairs={{0,4},{4,0},{1,5},{5,1},{2,6},{6,2},{3,7},{7,3},{8,12},{12,8},{9,1... | collective-permute-start | bytes 3145736 | tf_op jit(solution)/shard_map/ppermute | solution.py:45
  182.1 45.5 %collective-permute-start.31 = (bf16[4,352,512]{2,1,0:T(8,128)(2,1)}, bf16[4,352,512]{2,1,0:T(8,128)(2,1)}, u32[]{:S(2)}, u32[]{:S(2)}) collective-permute-start(bf16[4,352,512]{2,1,0:T(8,128)(2,1)} %get-tuple-element.136), channel_id=1, source_target_pairs={{0,16},{16,0},{1,17},{17,1},{2,18},{18,2},{3,19},{19,3},{4,20},{20... | collective-permute-start | bytes 4325384 | tf_op jit(solution)/shard_map/ppermute | solution.py:45
  191.0 5.9 %collective-permute-start.24 = (bf16[256,512]{1,0:T(8,128)(2,1)}, bf16[256,512]{1,0:T(8,128)(2,1)S(1)}, u32[]{:S(2)}, u32[]{:S(2)}) collective-permute-start(bf16[256,512]{1,0:T(8,128)(2,1)} %get-tuple-element.114), channel_id=1, source_target_pairs={{0,0},{2,1},{4,2},{6,3},{1,4},{3,5},{5,6},{7,7},{8,8},{10,9},{12,1... | collective-permute-start | bytes 786440 | tf_op jit(solution)/shard_map/ppermute | solution.py:66
  192.6 30.0 %collective-permute-start.25 = (bf16[256,512]{1,0:T(8,128)(2,1)}, bf16[256,512]{1,0:T(8,128)(2,1)S(1)}, u32[]{:S(2)}, u32[]{:S(2)}) collective-permute-start(bf16[256,512]{1,0:T(8,128)(2,1)} %get-tuple-element.115), channel_id=1, source_target_pairs={{2,0},{0,1},{6,2},{4,3},{3,4},{1,5},{7,6},{5,7},{10,8},{8,9},{14,1... | collective-permute-start | bytes 786440 | tf_op jit(solution)/shard_map/ppermute | solution.py:66
  196.8 69.6 %reduce-scatter.5.cloned.1.call-start = ((), (), s32[]{:S(2)}) async-start(), calls=%async_computation.3 | async-start | bytes 1802240 | tf_op jit(solution)/shard_map/reduce_scatter | solution.py:594
  196.8 29.9 %copy-start.31 = (bf16[256,512]{1,0:T(8,128)(2,1)}, bf16[256,512]{1,0:T(8,128)(2,1)S(1)}, u32[]{:S(2)}) copy-start(bf16[256,512]{1,0:T(8,128)(2,1)S(1)} %collective-permute-done.24.g0_ref) | copy-start | bytes 786436
  222.6 4.2 %copy-start.32 = (bf16[256,512]{1,0:T(8,128)(2,1)}, bf16[256,512]{1,0:T(8,128)(2,1)S(1)}, u32[]{:S(2)}) copy-start(bf16[256,512]{1,0:T(8,128)(2,1)S(1)} %collective-permute-done.25.g1_ref) | copy-start | bytes 786436
  224.6 3.0 copy-start.14
  226.8 3.7 %collective-permute-start.26 = (bf16[2,2,4,32,1152]{4,3,2,0,1:T(8,128)(2,1)}, bf16[2,2,4,32,1152]{4,3,2,0,1:T(8,128)(2,1)S(1)}, u32[]{:S(2)}, u32[]{:S(2)}) collective-permute-start(bf16[2,2,4,32,1152]{4,3,2,0,1:T(8,128)(2,1)} %bitcast.181), channel_id=1, source_target_pairs={{0,4},{4,0},{1,5},{5,1},{2,6},{6,2},{3,7},{7,3},{8,12},{12,8},{9,1... | collective-permute-start | bytes 3538952 | tf_op jit(solution)/shard_map/ppermute | solution.py:45
  230.5 3.5 %collective-permute-start.29 = (bf16[256,512]{1,0:T(8,128)(2,1)}, bf16[256,512]{1,0:T(8,128)(2,1)S(1)}, u32[]{:S(2)}, u32[]{:S(2)}) collective-permute-start(bf16[256,512]{1,0:T(8,128)(2,1)} %pad_maximum_fusion.12), channel_id=1, source_target_pairs={{0,4},{4,0},{1,5},{5,1},{2,6},{6,2},{3,7},{7,3},{8,12},{12,8},{9,1... | collective-permute-start | bytes 786440 | tf_op jit(solution)/shard_map/ppermute | solution.py:45
  233.1 16.8 %collective-permute-start.27 = (bf16[2,4,32,1152]{3,2,1,0:T(8,128)(2,1)S(1)}, bf16[2,4,32,1152]{3,2,1,0:T(8,128)(2,1)}, u32[]{:S(2)}, u32[]{:S(2)}) collective-permute-start(bf16[2,4,32,1152]{3,2,1,0:T(8,128)(2,1)S(1)} %dynamic-slice_bitcast_fusion), channel_id=1, source_target_pairs={{0,8},{8,0},{1,9},{9,1},{2,10},{10,2},{3,11},{11,3},{4,12},{12,4},... | collective-permute-start | bytes 1769480 | tf_op jit(solution)/shard_map/ppermute | solution.py:45
  234.7 13.9 %copy-start.16 = (bf16[2,256,1024]{2,1,0:T(8,128)(2,1)S(1)}, bf16[2,256,1024]{2,1,0:T(8,128)(2,1)}, u32[]{:S(2)}) copy-start(bf16[2,256,1024]{2,1,0:T(8,128)(2,1)} %get-tuple-element.99) | copy-start | bytes 3145732
  248.0 4.4 %collective-permute-start.30 = (bf16[2,256,1024]{2,1,0:T(8,128)(2,1)}, bf16[2,256,1024]{2,1,0:T(8,128)(2,1)}, u32[]{:S(2)}, u32[]{:S(2)}) collective-permute-start(bf16[2,256,1024]{2,1,0:T(8,128)(2,1)} %get-tuple-element.132), channel_id=1, source_target_pairs={{0,4},{4,0},{1,5},{5,1},{2,6},{6,2},{3,7},{7,3},{8,12},{12,8},{9,1... | collective-permute-start | bytes 3145736 | tf_op jit(solution)/shard_map/ppermute | solution.py:45
  248.5 3.9 %copy-start.22 = (bf16[1024,384]{1,0:T(8,128)(2,1)S(1)}, bf16[1024,384]{1,0:T(8,128)(2,1)}, u32[]{:S(2)}) copy-start(bf16[1024,384]{1,0:T(8,128)(2,1)} %get-tuple-element.139) | copy-start | bytes 2359300
  249.9 4.0 %copy-start.21 = (bf16[2,256,1024]{2,1,0:T(8,128)(2,1)S(1)}, bf16[2,256,1024]{2,1,0:T(8,128)(2,1)}, u32[]{:S(2)}) copy-start(bf16[2,256,1024]{2,1,0:T(8,128)(2,1)} %get-tuple-element.130) | copy-start | bytes 3145732
  249.9 14.5 %collective-permute-start.28 = (bf16[256,1024]{1,0:T(8,128)(2,1)S(1)}, bf16[256,1024]{1,0:T(8,128)(2,1)}, u32[]{:S(2)}, u32[]{:S(2)}) collective-permute-start(bf16[256,1024]{1,0:T(8,128)(2,1)S(1)} %fusion.18), channel_id=1, source_target_pairs={{0,8},{8,0},{1,9},{9,1},{2,10},{10,2},{3,11},{11,3},{4,12},{12,4},... | collective-permute-start | bytes 1572872 | tf_op jit(solution)/shard_map/ppermute | solution.py:45
  252.5 11.1 %collective-permute-start.33 = (bf16[2,2,4,32,384]{4,3,2,1,0:T(8,128)(2,1)S(1)}, bf16[2,2,4,32,384]{4,3,2,1,0:T(8,128)(2,1)S(1)}, u32[]{:S(2)}, u32[]{:S(2)}) collective-permute-start(bf16[2,2,4,32,384]{4,3,2,1,0:T(8,128)(2,1)S(1)} %dynamic-slice_bitcast_fusion.1), channel_id=1, source_target_pairs={{0,16},{16,0},{1,17},{17,1},{2,18},{18,2},{3,19},{19,3},{4,20},{20... | collective-permute-start | bytes 1179656 | tf_op jit(solution)/shard_map/ppermute | solution.py:45
  256.5 19.0 %collective-permute-start.32 = (bf16[256,1024]{1,0:T(8,128)(2,1)}, bf16[256,1024]{1,0:T(8,128)(2,1)S(1)}, u32[]{:S(2)}, u32[]{:S(2)}) collective-permute-start(bf16[256,1024]{1,0:T(8,128)(2,1)} %get-tuple-element.137), channel_id=1, source_target_pairs={{0,0},{1,2},{2,4},{3,6},{4,1},{5,3},{6,5},{7,7},{8,8},{9,10},{10,1... | collective-permute-start | bytes 1572872 | tf_op jit(solution)/shard_map/ppermute | solution.py:62
  258.2 17.3 %collective-permute-start.38 = (bf16[256,1024]{1,0:T(8,128)(2,1)S(1)}, bf16[256,1024]{1,0:T(8,128)(2,1)S(1)}, u32[]{:S(2)}, u32[]{:S(2)}) collective-permute-start(bf16[256,1024]{1,0:T(8,128)(2,1)S(1)} %get-tuple-element.147), channel_id=1, source_target_pairs={{0,2},{1,0},{2,6},{3,4},{4,3},{5,1},{6,7},{7,5},{8,10},{9,8},{10,1... | collective-permute-start | bytes 1572872 | tf_op jit(solution)/shard_map/ppermute | solution.py:62
  264.4 6.4 %collective-permute-start.34 = (bf16[2,4,32,384]{3,2,1,0:T(8,128)(2,1)}, bf16[2,4,32,384]{3,2,1,0:T(8,128)(2,1)}, u32[]{:S(2)}, u32[]{:S(2)}) collective-permute-start(bf16[2,4,32,384]{3,2,1,0:T(8,128)(2,1)} %dynamic-slice_bitcast_fusion.4), channel_id=1, source_target_pairs={{0,8},{8,0},{1,9},{9,1},{2,10},{10,2},{3,11},{11,3},{4,12},{12,4},... | collective-permute-start | bytes 589832 | tf_op jit(solution)/shard_map/ppermute | solution.py:45
  265.4 8.3 %collective-permute-start.37 = (bf16[4,32,1152]{2,1,0:T(8,128)(2,1)}, bf16[4,32,1152]{2,1,0:T(8,128)(2,1)S(1)}, u32[]{:S(2)}, u32[]{:S(2)}) collective-permute-start(bf16[4,32,1152]{2,1,0:T(8,128)(2,1)} %dynamic-slice_bitcast_fusion.2), channel_id=1, source_target_pairs={{0,16},{16,0},{1,17},{17,1},{2,18},{18,2},{3,19},{19,3},{4,20},{20... | collective-permute-start | bytes 884744 | tf_op jit(solution)/shard_map/ppermute | solution.py:45
  267.7 6.2 %collective-permute-start.35 = (f32[528,256]{1,0:T(8,128)S(1)}, f32[528,256]{1,0:T(8,128)S(1)}, u32[]{:S(2)}, u32[]{:S(2)}) collective-permute-start(f32[528,256]{1,0:T(8,128)S(1)} %pad_maximum_fusion.7), channel_id=1, source_target_pairs={{0,4},{4,0},{1,5},{5,1},{2,6},{6,2},{3,7},{7,3},{8,12},{12,8},{9,1... | collective-permute-start | bytes 1622024 | tf_op jit(solution)/shard_map/ppermute | solution.py:45
  273.8 1.4 collective-permute-start.36
  274.0 8.9 %collective-permute-start.40 = (bf16[1056,128]{1,0:T(8,128)(2,1)S(1)}, bf16[1056,128]{1,0:T(8,128)(2,1)S(1)}, u32[]{:S(2)}, u32[]{:S(2)}) collective-permute-start(bf16[1056,128]{1,0:T(8,128)(2,1)S(1)} %pad_maximum_fusion.9), channel_id=1, source_target_pairs={{0,8},{8,0},{1,9},{9,1},{2,10},{10,2},{3,11},{11,3},{4,12},{12,4},... | collective-permute-start | bytes 811016 | tf_op jit(solution)/shard_map/ppermute | solution.py:45
  275.4 11.1 %collective-permute-start.39 = (bf16[2,32,1920]{2,1,0:T(8,128)(2,1)S(1)}, bf16[2,32,1920]{2,1,0:T(8,128)(2,1)S(1)}, u32[]{:S(2)}, u32[]{:S(2)}) collective-permute-start(bf16[2,32,1920]{2,1,0:T(8,128)(2,1)S(1)} %pad_maximum_fusion.14), channel_id=1, source_target_pairs={{0,1},{1,0},{2,3},{3,2},{4,5},{5,4},{6,7},{7,6},{8,9},{9,8},{10,11... | collective-permute-start | bytes 737288 | tf_op jit(solution)/shard_map/ppermute | solution.py:49
  286.6 9.7 %collective-permute-start.41 = (bf16[32,2688]{1,0:T(8,128)(2,1)S(1)}, bf16[32,2688]{1,0:T(8,128)(2,1)S(1)}, u32[]{:S(2)}, u32[]{:S(2)}) collective-permute-start(bf16[32,2688]{1,0:T(8,128)(2,1)S(1)} %pad_maximum_fusion.16), channel_id=1, source_target_pairs={{0,2},{1,3},{2,0},{3,1},{4,6},{5,7},{6,4},{7,5},{8,10},{9,11},{10,... | collective-permute-start | bytes 516104 | tf_op jit(solution)/shard_map/ppermute | solution.py:49
  (17 other events, 21.7 us)
Sparse Core Ops, SparseCore 0:
  46.5 84.6 all-gather.2
  196.9 23.8 reduce-scatter.2
  230.6 30.5 reduce-scatter.4

commit v3 on v2

--- a/solution.py
+++ b/solution.py
@@ -22,7 +22,6 @@
 SLOT_MASKS = (0, 2, 1, 3)
 SPLIT_BITS = 2
 SPLIT = 1 << SPLIT_BITS
-TERM_ROWS = ((0, 176), (176, 528))
 
 
 def matmul(first_matrix, second_matrix):
@@ -329,26 +328,38 @@
         put(b, branch, grad)
 
 
-def weight_units(units, index, x_blocks, c_blocks, hidden_refs, term_ref):
+def weight_terms(units, index, m, left_ref, rows_ref, term_ref):
     slots, _, part = term_ref.shape
     step = min(part, 256)
-    act_ref, gate_ref, up_ref = hidden_refs
-    for m, (left, right) in enumerate(
-        ((gate_ref, x_blocks), (up_ref, x_blocks), (act_ref, c_blocks))
-    ):
-        for at in range(0, part, step):
-            lanes = pl.ds(pl.multiple_of(index * part + at, step), step)
-            rows = jnp.concatenate([ref[:, lanes] for ref in right], axis=0)
-            out = matmul(left[...], rows).astype(BF16)
-            for s in range(slots):
-                term_ref[s, m * units : (m + 1) * units, at : at + step] = out[
-                    s * units : (s + 1) * units
-                ]
+    for at in range(0, part, step):
+        lanes = pl.ds(pl.multiple_of(index * part + at, step), step)
+        out = matmul(left_ref[...], rows_ref[:, lanes]).astype(BF16)
+        for s in range(slots):
+            term_ref[s, m * units : (m + 1) * units, at : at + step] = out[s * units : (s + 1) * units]
+
+
+def weight_body(units, parts, sides, *refs):
+    index_ref, lefts, refs = refs[0], refs[1 : 1 + len(sides)], refs[1 + len(sides) :]
+    count = 3 * len(set(sides))
+    sources, term_refs, refs = refs[:count], refs[count : count + parts], refs[count + parts :]
+    rows_ref, left_refs, sems = refs[0], refs[1 : 1 + len(sides)], refs[1 + len(sides)]
+    tokens = sources[0].shape[0]
+    pairs = [
+        (source, rows_ref.at[n // 3, pl.ds(tokens * (n % 3), source.shape[0]), :])
+        for n, source in enumerate(sources)
+    ]
+    for copy in start_copies(pairs + list(zip(lefts, left_refs)), sems, 0):
+        copy.wait()
+    for n, term_ref in enumerate(term_refs):
+        index = index_ref[0] if n == parts - 1 else 1 - index_ref[0]
+        for m, side in enumerate(sides):
+            weight_terms(units, index, m, left_refs[m], rows_ref.at[side], term_ref)
 
 
 def feed_forward_body(units, parts, *refs):
     index_ref, sources, piece_ref, refs = refs[0], refs[1:7], refs[7], refs[8:]
-    grad_refs, branch_refs, term_refs, refs = refs[:2], refs[2:4], refs[4 : 4 + 2 * parts], refs[4 + 2 * parts :]
+    grad_refs, branch_refs, hidden_outs, refs = refs[:2], refs[2:4], refs[4:6], refs[6:]
+    term_refs, refs = refs[:parts], refs[parts:]
     rows_ref, weights_ref, hidden_refs, branch_buf, grad_buf, term_buf, sems = *refs[:2], refs[2:5], *refs[5:]
     tokens = sources[0].shape[0]
     pairs = [
@@ -379,15 +390,16 @@
             (grad_buf.at[b], grad_refs[b // 2].at[b % 2]),
             (branch_buf.at[b], branch_refs[b // 2].at[b % 2]),
         ]
+        lanes = pl.ds(b * tokens, tokens)
+        outs = zip((hidden_refs[0], hidden_refs[2]), hidden_outs)
+        done += [(ref.at[:, lanes], out.at[:, lanes]) for ref, out in outs]
         stores.extend(start_copies(done, sems, len(pairs) + len(stores)))
 
     forward_units(x_blocks, c_blocks, weights_ref, hidden_refs, put)
-    for n in range(parts):
-        which = index_ref[0] if n == parts - 1 else 1 - index_ref[0]
-        weight_units(units, which, x_blocks, c_blocks, hidden_refs, term_buf.at[n])
-        for h, rows in enumerate(TERM_ROWS):
-            done = [(term_buf.at[n, :, pl.ds(rows[0], rows[1] - rows[0]), :], term_refs[2 * n + h])]
-            stores.extend(start_copies(done, sems, len(pairs) + len(stores)))
+    for n, term_ref in enumerate(term_refs):
+        index = index_ref[0] if n == parts - 1 else 1 - index_ref[0]
+        weight_terms(units, index, 0, hidden_refs[1], rows_ref.at[0], term_buf.at[n])
+        stores.extend(start_copies([(term_buf.at[n], term_ref)], sems, len(pairs) + len(stores)))
     for copy in stores:
         copy.wait()
 
@@ -557,28 +569,44 @@
     blocks = (SPLIT, tokens, width)
     parts = 2 if aligned and bits == SPLIT_BITS + 1 else 1
     part = me >> SPLIT_BITS if parts == 2 else jnp.zeros((), jnp.int32)
-    term_shape = (GROUPS, 3 * units, width // parts)
+    hidden_shape = (GROUPS * units, SPLIT * tokens)
     outs = kernel_call(
         partial(feed_forward_body, units, parts),
         [((2, tokens, width), BF16, True)] * 4
-        + [((GROUPS, high - low, width // parts), BF16, True) for low, high in TERM_ROWS] * parts,
+        + [(hidden_shape, BF16, True)] * 2
+        + [((GROUPS, units, width // parts), BF16, True)] * parts,
         (part.reshape(1), *mlps, *cots, weights),
         scalars=1,
         remote=7,
         scratch=(
             pltpu.VMEM((2, SPLIT * tokens, width), BF16),
             pltpu.VMEM((3, GROUPS * units, width), BF16),
-            *[pltpu.VMEM((GROUPS * units, SPLIT * tokens), BF16)] * 3,
+            *[pltpu.VMEM(hidden_shape, BF16)] * 3,
             pltpu.VMEM(blocks, BF16),
             pltpu.VMEM(blocks, BF16),
-            pltpu.VMEM((parts,) + term_shape, BF16),
-            pltpu.SemaphoreType.DMA((6 + 3 * weights.shape[0] * GROUPS + 2 * SPLIT + 2 * parts,)),
+            pltpu.VMEM((parts, GROUPS, units, width // parts), BF16),
+            pltpu.SemaphoreType.DMA((6 + 3 * weights.shape[0] * GROUPS + 4 * SPLIT + parts,)),
         ),
-        flops=20 * 2**30,
+        flops=14 * 2**30,
         limit=56,
     )
-    grads, grads_sent, branch, branch_sent = outs[:4]
-    terms = outs[4:]
+    grads, grads_sent, branch, branch_sent, act_t, up_t = outs[:6]
+
+    late = kernel_call(
+        partial(weight_body, units, parts, (0, 1)),
+        [((GROUPS, 2 * units, width // parts), BF16)] * parts,
+        (part.reshape(1), up_t, act_t, *mlps, *cots),
+        scalars=1,
+        remote=8,
+        scratch=(
+            pltpu.VMEM((2, SPLIT * tokens, width), BF16),
+            *[pltpu.VMEM(hidden_shape, BF16)] * 2,
+            pltpu.SemaphoreType.DMA((8,)),
+        ),
+        flops=4 * 2**30,
+        limit=56,
+    )
+    terms = [pair[n] for n in range(parts) for pair in (outs[6:], late)]
     grads_sent = swap_bit(grads_sent, 0)
     grad_far = swap_bit(add_rounded(grads[1], grads_sent[1]), 1)
     branch_sent = swap_bit(branch_sent, 0)

time: 309 us -> 306 us (level)
  waiting for transfers between devices: 132 us -> 125 us
  Pallas kernels: 58 us -> 62.6 us
    ppermute x30, waiting for transfers between devices: 65.9 us -> 58.5 us  [hop(): return lax.ppermute(block, f'bit{bit}', [(0, 1), (1, 0)])]
    pallas_call x5 -> x6, Pallas kernels: 58 us -> 62.6 us  [kernel_call(): pl.pallas_call(body, out_shape=outs, in_specs=[smem] * scalars + [vmem] *...]
  transfers between devices with their start and end apart: 45 -> 45, of which waited for: 21 -> 21; matrix products, arithmetic and copies ran while one was open for 11% -> 11% of each run, Pallas kernels for 8% -> 11%
where the time goes in v3:
time: 306 us; the launch traced here: 304 us
  waiting for transfers between devices  125 us (41%)
  Pallas kernels  62.6 us (20%)
  starting transfers between devices  54.6 us (18%)
  other arithmetic  27.7 us (9%)
  local copies, waits for them, and re-layouts  17.7 us (6%)
  between operations  16.4 us (5%)
    pallas_call x6, Pallas kernels, kernel_call(): pl.pallas_call(body, out_shape=outs, in_specs=[smem] * scalars + [vmem] *...  62.6 us
    ppermute x30, waiting for transfers between devices, hop(): return lax.ppermute(block, f'bit{bit}', [(0, 1), (1, 0)])  58.5 us
    ppermute x30, starting transfers between devices, hop(): return lax.ppermute(block, f'bit{bit}', [(0, 1), (1, 0)])  36.1 us
    ppermute x4, waiting for transfers between devices, cross(): return lax.ppermute(block, 'feat', [(i, i ^ mask) for i in range(GROUPS)])  33.6 us
    ppermute x4, waiting for transfers between devices, away(): lax.ppermute(block, ('bit0', 'feat'), [(b, a) for a, b in home_pairs(mask)])  25.8 us
    convert_element_type x11, other arithmetic, add_rounded(): return (first.astype(F32) + second.astype(F32)).astype(BF16)  13.4 us
    ppermute x4, starting transfers between devices, away(): lax.ppermute(block, ('bit0', 'feat'), [(b, a) for a, b in home_pairs(mask)])  10.7 us
    unnamed x76, local copies, waits for them, and re-layouts  7.22 us
  transfers between devices with their start and end apart: 45, of which 21 were waited for; matrix products, arithmetic and copies ran while one was open for 11% of the time, Pallas kernels for 11%

profile of v3, /device:TPU:0, one launch (start us, length us, event | category | flops | bytes accessed | tf_op | source)
XLA Modules:
  0.0 303.7 jit_solution(17471854007633397645)
XLA Ops:
  7.2 1.7 collective-permute-start.1
  8.9 3.3 %collective-permute-start.2 = (bf16[256,1024]{1,0:T(8,128)(2,1)}, bf16[256,1024]{1,0:T(8,128)(2,1)S(1)}, u32[]{:S(2)}, u32[]{:S(2)}) collective-permute-start(bf16[256,1024]{1,0:T(8,128)(2,1)} %hidden_ref.1), channel_id=1, source_target_pairs={{2,0},{0,1},{6,2},{4,3},{3,4},{1,5},{7,6},{5,7},{10,8},{8,9},{14,1... | collective-permute-start | bytes 1572872 | tf_op jit(solution)/shard_map/ppermute | solution.py:65
  16.3 2.2 collective-permute-start
  18.5 1.2 fusion.17
  19.7 1.6 collective-permute-start.3
  22.3 5.9 %collective-permute-done.3 = bf16[3,2,176,128]{3,2,1,0:T(8,128)(2,1)S(1)} collective-permute-done((bf16[3,2,176,128]{3,2,1,0:T(8,128)(2,1)S(1)}, bf16[3,2,176,128]{3,2,1,0:T(8,128)(2,1)S(1)}, u32[]{:S(2)}, u32[]{:S(2)}) %collective-permute-start.3) | collective-permute-done | bytes 270368 | tf_op jit(solution)/shard_map/ppermute | solution.py:44
  28.3 16.9 %collective-permute-done.6 = bf16[32,2688]{1,0:T(8,128)(2,1)S(1)} collective-permute-done((bf16[32,2688]{1,0:T(8,128)(2,1)S(1)}, bf16[32,2688]{1,0:T(8,128)(2,1)S(1)}, u32[]{:S(2)}, u32[]{:S(2)}) %collective-permute-start.6) | collective-permute-done | bytes 172064 | tf_op jit(solution)/shard_map/ppermute | solution.py:48
  46.5 5.0 %collective-permute-done.7 = bf16[64,1920]{1,0:T(8,128)(2,1)S(1)} collective-permute-done((bf16[64,1920]{1,0:T(8,128)(2,1)S(1)}, bf16[64,1920]{1,0:T(8,128)(2,1)S(1)}, u32[]{:S(2)}, u32[]{:S(2)}) %collective-permute-start.7) | collective-permute-done | bytes 245792 | tf_op jit(solution)/shard_map/ppermute | solution.py:48
  51.7 1.6 collective-permute-start.8
  53.3 1.6 collective-permute-start.9
  54.9 1.0 pad_maximum_fusion.3
  58.1 9.5 %collective-permute-done.9 = bf16[128,1152]{1,0:T(8,128)(2,1)S(1)} collective-permute-done((bf16[128,1152]{1,0:T(8,128)(2,1)S(1)}, bf16[128,1152]{1,0:T(8,128)(2,1)S(1)}, u32[]{:S(2)}, u32[]{:S(2)}) %collective-permute-start.9) | collective-permute-done | bytes 294944 | tf_op jit(solution)/shard_map/ppermute | solution.py:44
  67.7 2.1 collective-permute-start.10
  70.0 5.5 %collective-permute-done.10 = bf16[4,4,32,384]{3,2,1,0:T(8,128)(2,1)S(1)} collective-permute-done((bf16[4,4,32,384]{3,2,1,0:T(8,128)(2,1)S(1)}, bf16[4,4,32,384]{3,2,1,0:T(8,128)(2,1)S(1)}, u32[]{:S(2)}, u32[]{:S(2)}) %collective-permute-start.10) | collective-permute-done | bytes 393248 | tf_op jit(solution)/shard_map/ppermute | solution.py:44
  75.8 5.2 %shard_map.203 = (bf16[4,256,1024]{2,1,0:T(8,128)(2,1)S(1)}, bf16[1024,384]{1,0:T(8,128)(2,1)S(1)}, bf16[256,512]{1,0:T(8,128)(2,1)S(1)}, bf16[256,512]{1,0:T(8,...) custom-call(s32[1]{0:T(128)S(6)} %select_n.316.first_ref, s32[1]{0:T(128)} %bitcast.7.group_ref, ...), custom_call_target="tpu_custom_call" | custom-call | flops 8589934592 | bytes 8388616 | tf_op jit(solution)/shard_map/pallas_call | solution.py:98
  81.0 1.0 copy-done.10
  82.0 2.0 collective-permute-start.16
  85.0 1.7 collective-permute-start.13
  86.7 0.9 collective-permute-start.12
  87.7 9.0 %collective-permute-done.16.refs_5_.refs_7_ = bf16[256,1024]{1,0:T(8,128)(2,1)S(1)} collective-permute-done((bf16[256,1024]{1,0:T(8,128)(2,1)S(1)}, bf16[256,1024]{1,0:T(8,128)(2,1)S(1)}, u32[]{:S(2)}, u32[]{:S(2)}) %collective-permute-start.16) | collective-permute-done | bytes 524320 | tf_op jit(solution)/shard_map/ppermute | solution.py:44
  97.4 6.3 %collective-permute-done.13.a1_ref = bf16[256,512]{1,0:T(8,128)(2,1)S(1)} collective-permute-done((bf16[256,512]{1,0:T(8,128)(2,1)S(1)}, bf16[256,512]{1,0:T(8,128)(2,1)S(1)}, u32[]{:S(2)}, u32[]{:S(2)}) %collective-permute-start.13) | collective-permute-done | bytes 262176 | tf_op jit(solution)/shard_map/ppermute | solution.py:61
  103.7 0.9 shard_map.204
  104.7 1.0 copy-done.2
  107.1 1.3 collective-permute-start.17
  108.4 7.9 %collective-permute-done.17.refs_2_.refs_4_ = bf16[256,1024]{1,0:T(8,128)(2,1)S(1)} collective-permute-done((bf16[256,1024]{1,0:T(8,128)(2,1)S(1)}, bf16[256,1024]{1,0:T(8,128)(2,1)S(1)}, u32[]{:S(2)}, u32[]{:S(2)}) %collective-permute-start.17) | collective-permute-done | bytes 524320 | tf_op jit(solution)/shard_map/ppermute | solution.py:44
  116.4 12.0 %collective-permute-start.19 = (bf16[512,1024]{1,0:T(8,128)(2,1)S(1)}, bf16[512,1024]{1,0:T(8,128)(2,1)}, u32[]{:S(2)}, u32[]{:S(2)}) collective-permute-start(bf16[512,1024]{1,0:T(8,128)(2,1)S(1)} %pad_maximum_fusion.4), channel_id=1, source_target_pairs={{0,4},{4,0},{1,5},{5,1},{2,6},{6,2},{3,7},{7,3},{8,12},{12,8},{9,1... | collective-permute-start | bytes 3145736 | tf_op jit(solution)/shard_map/ppermute | solution.py:44
  128.3 2.4 collective-permute-done.19.refs_3_.refs_5_
  131.2 29.2 %shard_map.205 = (bf16[2,256,1024]{2,1,0:T(8,128)(2,1)}, bf16[2,256,1024]{2,1,0:T(8,128)(2,1)}, bf16[2,256,1024]{2,1,0:T(8,128)(2,1)}, bf16[2,256,1024]{2,1,0:T(...) custom-call(s32[1]{0:T(128)} %bitcast.43.refs_0_, ...), custom_call_target="tpu_custom_call" | custom-call | flops 15032385536 | bytes 17039364 | tf_op jit(solution)/shard_map/pallas_call | solution.py:98
  160.4 1.6 collective-permute-start.23
  162.0 1.3 collective-permute-done.20.near_ref
  163.3 1.6 fusion.19
  164.9 1.5 collective-permute-start.22
  166.4 7.5 %shard_map.208 = (bf16[4,352,512]{2,1,0:T(8,128)(2,1)}, bf16[4,352,512]{2,1,0:T(8,128)(2,1)}) custom-call(s32[1]{0:T(128)} %bitcast.43.refs_0_, bf16[704,1024]{1,0:T(8,128)(2,1)} %get-tuple-element.135.refs_1_, bf16[704,1024]{1,0:T(8,128)(2,1)} %get-tuple-element.136.refs_2_, bf16[256,1024]{1,0:T(8,128)(2,1)} %copy-done.6, bf16[256,1024]{1,0:T(8,128)(2,1)} %copy-done.27, ...), custom_call_target="tpu_custom_call" | custom-call | flops 4294967296 | bytes 9961476 | tf_op jit(solution)/shard_map/pallas_call | solution.py:98
  173.9 5.3 %collective-permute-done.23 = bf16[4,176,512]{2,1,0:T(8,128)(2,1)S(1)} collective-permute-done((bf16[4,176,512]{2,1,0:T(8,128)(2,1)}, bf16[4,176,512]{2,1,0:T(8,128)(2,1)S(1)}, u32[]{:S(2)}, u32[]{:S(2)}) %collective-permute-start.23) | collective-permute-done | bytes 720928 | tf_op jit(solution)/shard_map/ppermute | solution.py:44
  179.2 1.5 collective-permute-start.31
  180.7 1.1 add_convert_fusion.1
  181.7 6.4 %shard_map.206 = (f32[256,1024]{1,0:T(8,128)}, bf16[256,512]{1,0:T(8,128)(2,1)}, bf16[256,512]{1,0:T(8,128)(2,1)}, bf16[1024,1152]{1,0:T(8,128)(2,1)}) custom-call(s32[1]{0:T(128)} %bitcast.member_ref, bf16[2,256,1024]{2,1,0:T(8,128)(2,1)} %get-tuple-element.106.own_ref, bf16[2,256,1024]{2,1,0:T(8,128)(2,1)} %copy-done.12, bf16[256,1024]{1,0:T(8,128)(2,1)} %copy-done.25, ...), custom_call_target="tpu_custom_call" | custom-call | flops 1073741824 | bytes 11042820 | tf_op jit(solution)/shard_map/pallas_call | solution.py:98
  188.2 1.6 collective-permute-start.24
  189.8 4.1 %collective-permute-start.25 = (bf16[256,512]{1,0:T(8,128)(2,1)}, bf16[256,512]{1,0:T(8,128)(2,1)S(1)}, u32[]{:S(2)}, u32[]{:S(2)}) collective-permute-start(bf16[256,512]{1,0:T(8,128)(2,1)} %get-tuple-element.117), channel_id=1, source_target_pairs={{2,0},{0,1},{6,2},{4,3},{3,4},{1,5},{7,6},{5,7},{10,8},{8,9},{14,1... | collective-permute-start | bytes 786440 | tf_op jit(solution)/shard_map/ppermute | solution.py:65
  194.0 25.8 %collective-permute-done.25.g1_ref = bf16[256,512]{1,0:T(8,128)(2,1)S(1)} collective-permute-done((bf16[256,512]{1,0:T(8,128)(2,1)}, bf16[256,512]{1,0:T(8,128)(2,1)S(1)}, u32[]{:S(2)}, u32[]{:S(2)}) %collective-permute-start.25) | collective-permute-done | bytes 262176 | tf_op jit(solution)/shard_map/ppermute | solution.py:65
  219.7 2.0 constant_dynamic-slice_fusion.1
  221.7 1.1 copy.88
  222.9 1.0 copy-done.18
  224.6 2.9 add_convert_fusion
  228.6 1.5 fusion
  231.7 13.4 %shard_map.207 = (bf16[2,256,1024]{2,1,0:T(8,128)(2,1)}, bf16[2,256,1024]{2,1,0:T(8,128)(2,1)}, bf16[1024,384]{1,0:T(8,128)(2,1)}) custom-call(s32[1]{0:T(128)S(6)} %select_n.316.first_ref, s32[1]{0:T(128)} %bitcast.7.group_ref, bf16[256,512]{1,0:T(8,128)(2,1)} %copy-done.31, bf16[256,512]{1,0:T(8,128)(2,1)} %copy-done.32, bf16[256,512]{1,0:T(8,128)(2,1)} %copy-done.35, ...), custom_call_target="tpu_custom_call" | custom-call | flops 12884901888 | bytes 9437192 | tf_op jit(solution)/shard_map/pallas_call | solution.py:98
  245.6 1.3 fusion.18
  246.9 1.4 collective-permute-start.28
  248.3 1.2 fusion.3
  251.0 2.6 fusion.20
  253.6 1.7 collective-permute-start.32
  255.3 2.5 collective-permute-start.38
  257.8 2.9 collective-permute-done.33
  261.5 1.0 collective-permute-start.34
  262.5 0.9 collective-permute-start.37
  263.4 1.2 maximum_convert_fusion
  264.8 3.0 collective-permute-done.34
  267.9 1.0 fusion.22
  268.9 1.9 collective-permute-done.37
  274.2 2.5 fusion.10
  276.7 3.3 %collective-permute-done.40 = bf16[1056,128]{1,0:T(8,128)(2,1)S(1)} collective-permute-done((bf16[1056,128]{1,0:T(8,128)(2,1)S(1)}, bf16[1056,128]{1,0:T(8,128)(2,1)S(1)}, u32[]{:S(2)}, u32[]{:S(2)}) %collective-permute-start.40) | collective-permute-done | bytes 270368 | tf_op jit(solution)/shard_map/ppermute | solution.py:44
  280.5 3.1 %collective-permute-done.39 = bf16[2,32,1920]{2,1,0:T(8,128)(2,1)S(1)} collective-permute-done((bf16[2,32,1920]{2,1,0:T(8,128)(2,1)S(1)}, bf16[2,32,1920]{2,1,0:T(8,128)(2,1)S(1)}, u32[]{:S(2)}, u32[]{:S(2)}) %collective-permute-start.39) | collective-permute-done | bytes 245792 | tf_op jit(solution)/shard_map/ppermute | solution.py:48
  283.7 1.0 slice_bitcast_fusion.1
  284.7 8.6 %collective-permute-done.41 = bf16[32,2688]{1,0:T(8,128)(2,1)S(1)} collective-permute-done((bf16[32,2688]{1,0:T(8,128)(2,1)S(1)}, bf16[32,2688]{1,0:T(8,128)(2,1)S(1)}, u32[]{:S(2)}, u32[]{:S(2)}) %collective-permute-start.41) | collective-permute-done | bytes 172064 | tf_op jit(solution)/shard_map/ppermute | solution.py:48
  (226 shorter events, 25.4 us)
Async XLA Ops:
  7.2 124.0 %all-gather.3.cloned.1.call-start = ((), (), s32[]{:S(2)}) async-start(), calls=%async_computation.4 | async-start | bytes 4866048 | tf_op jit(solution)/shard_map/all_gather | solution.py:525
  7.2 38.1 %collective-permute-start.1 = (bf16[256,1024]{1,0:T(8,128)(2,1)}, bf16[256,1024]{1,0:T(8,128)(2,1)S(1)}, u32[]{:S(2)}, u32[]{:S(2)}) collective-permute-start(bf16[256,1024]{1,0:T(8,128)(2,1)} %hidden_ref.1), channel_id=1, source_target_pairs={{0,0},{2,1},{4,2},{6,3},{1,4},{3,5},{5,6},{7,7},{8,8},{10,9},{12,1... | collective-permute-start | bytes 1572872 | tf_op jit(solution)/shard_map/ppermute | solution.py:65
  8.9 36.4 %collective-permute-start.2 = (bf16[256,1024]{1,0:T(8,128)(2,1)}, bf16[256,1024]{1,0:T(8,128)(2,1)S(1)}, u32[]{:S(2)}, u32[]{:S(2)}) collective-permute-start(bf16[256,1024]{1,0:T(8,128)(2,1)} %hidden_ref.1), channel_id=1, source_target_pairs={{2,0},{0,1},{6,2},{4,3},{3,4},{1,5},{7,6},{5,7},{10,8},{8,9},{14,1... | collective-permute-start | bytes 1572872 | tf_op jit(solution)/shard_map/ppermute | solution.py:65
  15.4 5.8 %copy-start.33 = (bf16[32]{0:T(256)(128)(2,1)S(1)}, bf16[32]{0:T(256)(128)(2,1)}, u32[]{:S(2)}) copy-start(bf16[32]{0:T(256)(128)(2,1)} %param.21) | copy-start | bytes 196
  16.3 5.1 %collective-permute-start = (bf16[80,384]{1,0:T(8,128)(2,1)S(1)}, bf16[80,384]{1,0:T(8,128)(2,1)S(1)}, u32[]{:S(2)}, u32[]{:S(2)}) collective-permute-start(bf16[80,384]{1,0:T(8,128)(2,1)S(1)} %concatenate.114), channel_id=1, source_target_pairs={{0,4},{4,0},{1,5},{5,1},{2,6},{6,2},{3,7},{7,3},{8,12},{12,8},{9,1... | collective-permute-start | bytes 184328 | tf_op jit(solution)/shard_map/ppermute | solution.py:44
  18.5 3.1 %copy-start.24 = (bf16[1024,32]{0,1:T(8,128)(2,1)S(1)}, bf16[1024,32]{0,1:T(8,128)(2,1)}, u32[]{:S(2)}) copy-start(bf16[1024,32]{0,1:T(8,128)(2,1)} %param.16) | copy-start | bytes 196612
  19.7 8.5 %collective-permute-start.3 = (bf16[3,2,176,128]{3,2,1,0:T(8,128)(2,1)S(1)}, bf16[3,2,176,128]{3,2,1,0:T(8,128)(2,1)S(1)}, u32[]{:S(2)}, u32[]{:S(2)}) collective-permute-start(bf16[3,2,176,128]{3,2,1,0:T(8,128)(2,1)S(1)} %dynamic-slice_bitcast_fusion.3), channel_id=1, source_target_pairs={{0,8},{8,0},{1,9},{9,1},{2,10},{10,2},{3,11},{11,3},{4,12},{12,4},... | collective-permute-start | bytes 811016 | tf_op jit(solution)/shard_map/ppermute | solution.py:44
  21.6 23.6 %collective-permute-start.6 = (bf16[32,2688]{1,0:T(8,128)(2,1)S(1)}, bf16[32,2688]{1,0:T(8,128)(2,1)S(1)}, u32[]{:S(2)}, u32[]{:S(2)}) collective-permute-start(bf16[32,2688]{1,0:T(8,128)(2,1)S(1)} %pad_maximum_fusion.15), channel_id=1, source_target_pairs={{0,2},{1,3},{2,0},{3,1},{4,6},{5,7},{6,4},{7,5},{8,10},{9,11},{10,... | collective-permute-start | bytes 516104 | tf_op jit(solution)/shard_map/ppermute | solution.py:48
  28.2 17.2 %collective-permute-start.4 = (bf16[3,176,256]{2,1,0:T(8,128)(2,1)S(1)}, bf16[3,176,256]{2,1,0:T(8,128)(2,1)S(1)}, u32[]{:S(2)}, u32[]{:S(2)}) collective-permute-start(bf16[3,176,256]{2,1,0:T(8,128)(2,1)S(1)} %pad_maximum_fusion.8), channel_id=1, source_target_pairs={{0,4},{4,0},{1,5},{5,1},{2,6},{6,2},{3,7},{7,3},{8,12},{12,8},{9,1... | collective-permute-start | bytes 811016 | tf_op jit(solution)/shard_map/ppermute | solution.py:44
  45.3 6.3 %collective-permute-start.7 = (bf16[64,1920]{1,0:T(8,128)(2,1)S(1)}, bf16[64,1920]{1,0:T(8,128)(2,1)S(1)}, u32[]{:S(2)}, u32[]{:S(2)}) collective-permute-start(bf16[64,1920]{1,0:T(8,128)(2,1)S(1)} %pad_maximum_fusion.13), channel_id=1, source_target_pairs={{0,1},{1,0},{2,3},{3,2},{4,5},{5,4},{6,7},{7,6},{8,9},{9,8},{10,11... | collective-permute-start | bytes 737288 | tf_op jit(solution)/shard_map/ppermute | solution.py:48
  46.4 217.1 %reduce-scatter.3.cloned.1.call-start = ((), (), s32[]{:S(2)}) async-start(), calls=%async_computation.2 | async-start | bytes 901120 | tf_op jit(solution)/shard_map/reduce_scatter | solution.py:622
  51.7 5.7 %collective-permute-start.8 = (bf16[2,4,32,384]{3,0,2,1:T(2,128)(2,1)S(1)}, bf16[2,4,32,384]{3,0,2,1:T(2,128)(2,1)S(1)}, u32[]{:S(2)}, u32[]{:S(2)}) collective-permute-start(bf16[2,4,32,384]{3,0,2,1:T(2,128)(2,1)S(1)} %bitcast.210), channel_id=1, source_target_pairs={{0,8},{8,0},{1,9},{9,1},{2,10},{10,2},{3,11},{11,3},{4,12},{12,4},... | collective-permute-start | bytes 589832 | tf_op jit(solution)/shard_map/ppermute | solution.py:44
  53.3 14.3 %collective-permute-start.9 = (bf16[128,1152]{1,0:T(8,128)(2,1)S(1)}, bf16[128,1152]{1,0:T(8,128)(2,1)S(1)}, u32[]{:S(2)}, u32[]{:S(2)}) collective-permute-start(bf16[128,1152]{1,0:T(8,128)(2,1)S(1)} %bitcast.186), channel_id=1, source_target_pairs={{0,16},{16,0},{1,17},{17,1},{2,18},{18,2},{3,19},{19,3},{4,20},{20... | collective-permute-start | bytes 884744 | tf_op jit(solution)/shard_map/ppermute | solution.py:44
  55.9 19.8 %collective-permute-start.5 = (bf16[512,1024]{1,0:T(8,128)(2,1)}, bf16[512,1024]{1,0:T(8,128)(2,1)S(1)}, u32[]{:S(2)}, u32[]{:S(2)}) collective-permute-start(bf16[512,1024]{1,0:T(8,128)(2,1)} %pad_maximum_fusion.3), channel_id=1, source_target_pairs={{0,4},{4,0},{1,5},{5,1},{2,6},{6,2},{3,7},{7,3},{8,12},{12,8},{9,1... | collective-permute-start | bytes 3145736 | tf_op jit(solution)/shard_map/ppermute | solution.py:44
  67.7 14.4 %collective-permute-start.14 = (bf16[2,128,1152]{2,1,0:T(8,128)(2,1)S(1)}, bf16[2,128,1152]{2,1,0:T(8,128)(2,1)S(1)}, u32[]{:S(2)}, u32[]{:S(2)}) collective-permute-start(bf16[2,128,1152]{2,1,0:T(8,128)(2,1)S(1)} %maximum_select_fusion.4), channel_id=1, source_target_pairs={{0,8},{8,0},{1,9},{9,1},{2,10},{10,2},{3,11},{11,3},{4,12},{12,4},... | collective-permute-start | bytes 1769480 | tf_op jit(solution)/shard_map/ppermute | solution.py:44
  67.7 7.8 %collective-permute-start.10 = (bf16[4,4,32,384]{3,2,1,0:T(8,128)(2,1)S(1)}, bf16[4,4,32,384]{3,2,1,0:T(8,128)(2,1)S(1)}, u32[]{:S(2)}, u32[]{:S(2)}) collective-permute-start(bf16[4,4,32,384]{3,2,1,0:T(8,128)(2,1)S(1)} %bitcast.201), channel_id=1, source_target_pairs={{0,16},{16,0},{1,17},{17,1},{2,18},{18,2},{3,19},{19,3},{4,20},{20... | collective-permute-start | bytes 1179656 | tf_op jit(solution)/shard_map/ppermute | solution.py:44
  75.7 5.3 %copy-start.4 = (bf16[2,4,4,32,384]{4,3,2,1,0:T(8,128)(2,1)}, bf16[2,4,4,32,384]{4,3,2,1,0:T(8,128)(2,1)S(1)}, u32[]{:S(2)}) copy-start(bf16[2,4,4,32,384]{4,3,2,1,0:T(8,128)(2,1)S(1)} %maximum_select_fusion.2) | copy-start | bytes 2359300
  75.7 6.3 %copy-start.13 = (bf16[256,1024]{1,0:T(8,128)(2,1)S(1)}, bf16[256,1024]{1,0:T(8,128)(2,1)}, u32[]{:S(2)}) copy-start(bf16[256,1024]{1,0:T(8,128)(2,1)} %refs_6_.1) | copy-start | bytes 1572868
  82.0 2.3 copy-start.9
  82.0 2.3 copy-start.11
  82.0 2.6 collective-permute-start.11
  82.0 14.6 %collective-permute-start.16 = (bf16[256,1024]{1,0:T(8,128)(2,1)S(1)}, bf16[256,1024]{1,0:T(8,128)(2,1)S(1)}, u32[]{:S(2)}, u32[]{:S(2)}) collective-permute-start(bf16[256,1024]{1,0:T(8,128)(2,1)S(1)} %copy-done.13), channel_id=1, source_target_pairs={{0,8},{8,0},{1,9},{9,1},{2,10},{10,2},{3,11},{11,3},{4,12},{12,4},... | collective-permute-start | bytes 1572872 | tf_op jit(solution)/shard_map/ppermute | solution.py:44
  84.6 12.2 %collective-permute-start.15 = (bf16[2,2,128,1152]{3,2,1,0:T(8,128)(2,1)S(1)}, bf16[2,2,128,1152]{3,2,1,0:T(8,128)(2,1)S(1)}, u32[]{:S(2)}, u32[]{:S(2)}) collective-permute-start(bf16[2,2,128,1152]{3,2,1,0:T(8,128)(2,1)S(1)} %maximum_select_fusion.1), channel_id=1, source_target_pairs={{0,4},{4,0},{1,5},{5,1},{2,6},{6,2},{3,7},{7,3},{8,12},{12,8},{9,1... | collective-permute-start | bytes 3538952 | tf_op jit(solution)/shard_map/ppermute | solution.py:44
  85.0 18.7 %collective-permute-start.13 = (bf16[256,512]{1,0:T(8,128)(2,1)S(1)}, bf16[256,512]{1,0:T(8,128)(2,1)S(1)}, u32[]{:S(2)}, u32[]{:S(2)}) collective-permute-start(bf16[256,512]{1,0:T(8,128)(2,1)S(1)} %pad_maximum_fusion.11), channel_id=1, source_target_pairs={{0,2},{1,0},{2,6},{3,4},{4,3},{5,1},{6,7},{7,5},{8,10},{9,8},{10,1... | collective-permute-start | bytes 786440 | tf_op jit(solution)/shard_map/ppermute | solution.py:61
  86.7 17.0 %collective-permute-start.12 = (bf16[256,512]{1,0:T(8,128)(2,1)S(1)}, bf16[256,512]{1,0:T(8,128)(2,1)S(1)}, u32[]{:S(2)}, u32[]{:S(2)}) collective-permute-start(bf16[256,512]{1,0:T(8,128)(2,1)S(1)} %pad_maximum_fusion.10), channel_id=1, source_target_pairs={{0,0},{1,2},{2,4},{3,6},{4,1},{5,3},{6,5},{7,7},{8,8},{9,10},{10,1... | collective-permute-start | bytes 786440 | tf_op jit(solution)/shard_map/ppermute | solution.py:61
  96.7 19.6 %collective-permute-start.18 = (bf16[512,1024]{1,0:T(8,128)(2,1)S(1)}, bf16[512,1024]{1,0:T(8,128)(2,1)S(1)}, u32[]{:S(2)}, u32[]{:S(2)}) collective-permute-start(bf16[512,1024]{1,0:T(8,128)(2,1)S(1)} %pad_maximum_fusion.5), channel_id=1, source_target_pairs={{0,4},{4,0},{1,5},{5,1},{2,6},{6,2},{3,7},{7,3},{8,12},{12,8},{9,1... | collective-permute-start | bytes 3145736 | tf_op jit(solution)/shard_map/ppermute | solution.py:44
  96.8 6.9 %copy-start.1 = (bf16[256,1024]{1,0:T(8,128)(2,1)S(1)}, bf16[256,1024]{1,0:T(8,128)(2,1)}, u32[]{:S(2)}) copy-start(bf16[256,1024]{1,0:T(8,128)(2,1)} %hidden_ref.1) | copy-start | bytes 1572868
  97.4 7.3 %copy-start = (bf16[2,2,2,128,1152]{4,3,2,1,0:T(8,128)(2,1)}, bf16[2,2,2,128,1152]{4,3,2,1,0:T(8,128)(2,1)S(1)}, u32[]{:S(2)}) copy-start(bf16[2,2,2,128,1152]{4,3,2,1,0:T(8,128)(2,1)S(1)} %maximum_select_fusion) | copy-start | bytes 7077892
  107.1 24.1 %copy-start.6 = (bf16[256,1024]{1,0:T(8,128)(2,1)}, bf16[256,1024]{1,0:T(8,128)(2,1)S(1)}, u32[]{:S(2)}) copy-start(bf16[256,1024]{1,0:T(8,128)(2,1)S(1)} %get-tuple-element.97.refs_1_.refs_3_) | copy-start | bytes 1572868
  107.1 9.2 %collective-permute-start.17 = (bf16[256,1024]{1,0:T(8,128)(2,1)S(1)}, bf16[256,1024]{1,0:T(8,128)(2,1)S(1)}, u32[]{:S(2)}, u32[]{:S(2)}) collective-permute-start(bf16[256,1024]{1,0:T(8,128)(2,1)S(1)} %get-tuple-element.97.refs_1_.refs_3_), channel_id=1, source_target_pairs={{0,8},{8,0},{1,9},{9,1},{2,10},{10,2},{3,11},{11,3},{4,12},{12,4},... | collective-permute-start | bytes 1572872 | tf_op jit(solution)/shard_map/ppermute | solution.py:44
  116.3 14.9 %copy-start.27 = (bf16[256,1024]{1,0:T(8,128)(2,1)}, bf16[256,1024]{1,0:T(8,128)(2,1)S(1)}, u32[]{:S(2)}) copy-start(bf16[256,1024]{1,0:T(8,128)(2,1)S(1)} %collective-permute-done.17.refs_2_.refs_4_) | copy-start | bytes 1572868
  116.4 14.8 %copy-start.34 = (bf16[512,1024]{1,0:T(8,128)(2,1)}, bf16[512,1024]{1,0:T(8,128)(2,1)S(1)}, u32[]{:S(2)}) copy-start(bf16[512,1024]{1,0:T(8,128)(2,1)S(1)} %collective-permute-done.18.refs_6_.refs_8_) | copy-start | bytes 3145732
  116.4 14.4 %collective-permute-start.19 = (bf16[512,1024]{1,0:T(8,128)(2,1)S(1)}, bf16[512,1024]{1,0:T(8,128)(2,1)}, u32[]{:S(2)}, u32[]{:S(2)}) collective-permute-start(bf16[512,1024]{1,0:T(8,128)(2,1)S(1)} %pad_maximum_fusion.4), channel_id=1, source_target_pairs={{0,4},{4,0},{1,5},{5,1},{2,6},{6,2},{3,7},{7,3},{8,12},{12,8},{9,1... | collective-permute-start | bytes 3145736 | tf_op jit(solution)/shard_map/ppermute | solution.py:44
  160.4 2.9 collective-permute-start.20
  160.4 18.8 %collective-permute-start.23 = (bf16[4,176,512]{2,1,0:T(8,128)(2,1)}, bf16[4,176,512]{2,1,0:T(8,128)(2,1)S(1)}, u32[]{:S(2)}, u32[]{:S(2)}) collective-permute-start(bf16[4,176,512]{2,1,0:T(8,128)(2,1)} %get-tuple-element.111), channel_id=1, source_target_pairs={{0,16},{16,0},{1,17},{17,1},{2,18},{18,2},{3,19},{19,3},{4,20},{20... | collective-permute-start | bytes 2162696 | tf_op jit(solution)/shard_map/ppermute | solution.py:44
  163.3 10.6 %copy-start.12 = (bf16[2,256,1024]{2,1,0:T(8,128)(2,1)}, bf16[2,256,1024]{2,1,0:T(8,128)(2,1)S(1)}, u32[]{:S(2)}) copy-start(bf16[2,256,1024]{2,1,0:T(8,128)(2,1)S(1)} %collective-permute-done.20.near_ref) | copy-start | bytes 3145732
  164.9 15.8 %collective-permute-start.22 = (bf16[256,1024]{1,0:T(8,128)(2,1)S(1)}, bf16[256,1024]{1,0:T(8,128)(2,1)S(1)}, u32[]{:S(2)}, u32[]{:S(2)}) collective-permute-start(bf16[256,1024]{1,0:T(8,128)(2,1)S(1)} %fusion.19), channel_id=1, source_target_pairs={{0,8},{8,0},{1,9},{9,1},{2,10},{10,2},{3,11},{11,3},{4,12},{12,4},... | collective-permute-start | bytes 1572872 | tf_op jit(solution)/shard_map/ppermute | solution.py:44
  166.4 56.4 %collective-permute-start.21 = (bf16[2,256,1024]{2,1,0:T(8,128)(2,1)}, bf16[2,256,1024]{2,1,0:T(8,128)(2,1)S(1)}, u32[]{:S(2)}, u32[]{:S(2)}) collective-permute-start(bf16[2,256,1024]{2,1,0:T(8,128)(2,1)} %get-tuple-element.105), channel_id=1, source_target_pairs={{0,4},{4,0},{1,5},{5,1},{2,6},{6,2},{3,7},{7,3},{8,12},{12,8},{9,1... | collective-permute-start | bytes 3145736 | tf_op jit(solution)/shard_map/ppermute | solution.py:44
  166.4 14.2 %copy-start.23 = (bf16[4,176,512]{2,1,0:T(8,128)(2,1)S(1)}, bf16[4,176,512]{2,1,0:T(8,128)(2,1)}, u32[]{:S(2)}) copy-start(bf16[4,176,512]{2,1,0:T(8,128)(2,1)} %get-tuple-element.109) | copy-start | bytes 2162692
  179.2 45.4 %collective-permute-start.31 = (bf16[4,352,512]{2,1,0:T(8,128)(2,1)}, bf16[4,352,512]{2,1,0:T(8,128)(2,1)}, u32[]{:S(2)}, u32[]{:S(2)}) collective-permute-start(bf16[4,352,512]{2,1,0:T(8,128)(2,1)} %get-tuple-element.140), channel_id=1, source_target_pairs={{0,16},{16,0},{1,17},{17,1},{2,18},{18,2},{3,19},{19,3},{4,20},{20... | collective-permute-start | bytes 4325384 | tf_op jit(solution)/shard_map/ppermute | solution.py:44
  188.2 5.8 %collective-permute-start.24 = (bf16[256,512]{1,0:T(8,128)(2,1)}, bf16[256,512]{1,0:T(8,128)(2,1)S(1)}, u32[]{:S(2)}, u32[]{:S(2)}) collective-permute-start(bf16[256,512]{1,0:T(8,128)(2,1)} %get-tuple-element.116), channel_id=1, source_target_pairs={{0,0},{2,1},{4,2},{6,3},{1,4},{3,5},{5,6},{7,7},{8,8},{10,9},{12,1... | collective-permute-start | bytes 786440 | tf_op jit(solution)/shard_map/ppermute | solution.py:65
  189.8 30.0 %collective-permute-start.25 = (bf16[256,512]{1,0:T(8,128)(2,1)}, bf16[256,512]{1,0:T(8,128)(2,1)S(1)}, u32[]{:S(2)}, u32[]{:S(2)}) collective-permute-start(bf16[256,512]{1,0:T(8,128)(2,1)} %get-tuple-element.117), channel_id=1, source_target_pairs={{2,0},{0,1},{6,2},{4,3},{3,4},{1,5},{7,6},{5,7},{10,8},{8,9},{14,1... | collective-permute-start | bytes 786440 | tf_op jit(solution)/shard_map/ppermute | solution.py:65
  193.9 69.5 %reduce-scatter.5.cloned.1.call-start = ((), (), s32[]{:S(2)}) async-start(), calls=%async_computation.3 | async-start | bytes 1802240 | tf_op jit(solution)/shard_map/reduce_scatter | solution.py:622
  194.0 29.9 %copy-start.31 = (bf16[256,512]{1,0:T(8,128)(2,1)}, bf16[256,512]{1,0:T(8,128)(2,1)S(1)}, u32[]{:S(2)}) copy-start(bf16[256,512]{1,0:T(8,128)(2,1)S(1)} %collective-permute-done.24.g0_ref) | copy-start | bytes 786436
  219.7 4.1 %copy-start.32 = (bf16[256,512]{1,0:T(8,128)(2,1)}, bf16[256,512]{1,0:T(8,128)(2,1)S(1)}, u32[]{:S(2)}) copy-start(bf16[256,512]{1,0:T(8,128)(2,1)S(1)} %collective-permute-done.25.g1_ref) | copy-start | bytes 786436
  221.7 2.9 copy-start.14
  223.8 3.7 %collective-permute-start.26 = (bf16[2,2,4,32,1152]{4,3,2,0,1:T(8,128)(2,1)}, bf16[2,2,4,32,1152]{4,3,2,0,1:T(8,128)(2,1)S(1)}, u32[]{:S(2)}, u32[]{:S(2)}) collective-permute-start(bf16[2,2,4,32,1152]{4,3,2,0,1:T(8,128)(2,1)} %bitcast.181), channel_id=1, source_target_pairs={{0,4},{4,0},{1,5},{5,1},{2,6},{6,2},{3,7},{7,3},{8,12},{12,8},{9,1... | collective-permute-start | bytes 3538952 | tf_op jit(solution)/shard_map/ppermute | solution.py:44
  227.5 3.5 %collective-permute-start.29 = (bf16[256,512]{1,0:T(8,128)(2,1)}, bf16[256,512]{1,0:T(8,128)(2,1)S(1)}, u32[]{:S(2)}, u32[]{:S(2)}) collective-permute-start(bf16[256,512]{1,0:T(8,128)(2,1)} %pad_maximum_fusion.12), channel_id=1, source_target_pairs={{0,4},{4,0},{1,5},{5,1},{2,6},{6,2},{3,7},{7,3},{8,12},{12,8},{9,1... | collective-permute-start | bytes 786440 | tf_op jit(solution)/shard_map/ppermute | solution.py:44
  230.2 16.7 %collective-permute-start.27 = (bf16[2,4,32,1152]{3,2,1,0:T(8,128)(2,1)S(1)}, bf16[2,4,32,1152]{3,2,1,0:T(8,128)(2,1)}, u32[]{:S(2)}, u32[]{:S(2)}) collective-permute-start(bf16[2,4,32,1152]{3,2,1,0:T(8,128)(2,1)S(1)} %dynamic-slice_bitcast_fusion), channel_id=1, source_target_pairs={{0,8},{8,0},{1,9},{9,1},{2,10},{10,2},{3,11},{11,3},{4,12},{12,4},... | collective-permute-start | bytes 1769480 | tf_op jit(solution)/shard_map/ppermute | solution.py:44
  231.7 13.8 %copy-start.16 = (bf16[2,256,1024]{2,1,0:T(8,128)(2,1)S(1)}, bf16[2,256,1024]{2,1,0:T(8,128)(2,1)}, u32[]{:S(2)}) copy-start(bf16[2,256,1024]{2,1,0:T(8,128)(2,1)} %get-tuple-element.101) | copy-start | bytes 3145732
  245.1 4.4 %collective-permute-start.30 = (bf16[2,256,1024]{2,1,0:T(8,128)(2,1)}, bf16[2,256,1024]{2,1,0:T(8,128)(2,1)}, u32[]{:S(2)}, u32[]{:S(2)}) collective-permute-start(bf16[2,256,1024]{2,1,0:T(8,128)(2,1)} %get-tuple-element.134), channel_id=1, source_target_pairs={{0,4},{4,0},{1,5},{5,1},{2,6},{6,2},{3,7},{7,3},{8,12},{12,8},{9,1... | collective-permute-start | bytes 3145736 | tf_op jit(solution)/shard_map/ppermute | solution.py:44
  245.6 3.9 %copy-start.22 = (bf16[1024,384]{1,0:T(8,128)(2,1)S(1)}, bf16[1024,384]{1,0:T(8,128)(2,1)}, u32[]{:S(2)}) copy-start(bf16[1024,384]{1,0:T(8,128)(2,1)} %get-tuple-element.143) | copy-start | bytes 2359300
  246.9 4.1 %copy-start.21 = (bf16[2,256,1024]{2,1,0:T(8,128)(2,1)S(1)}, bf16[2,256,1024]{2,1,0:T(8,128)(2,1)}, u32[]{:S(2)}) copy-start(bf16[2,256,1024]{2,1,0:T(8,128)(2,1)} %get-tuple-element.132) | copy-start | bytes 3145732
  246.9 14.5 %collective-permute-start.28 = (bf16[256,1024]{1,0:T(8,128)(2,1)S(1)}, bf16[256,1024]{1,0:T(8,128)(2,1)}, u32[]{:S(2)}, u32[]{:S(2)}) collective-permute-start(bf16[256,1024]{1,0:T(8,128)(2,1)S(1)} %fusion.18), channel_id=1, source_target_pairs={{0,8},{8,0},{1,9},{9,1},{2,10},{10,2},{3,11},{11,3},{4,12},{12,4},... | collective-permute-start | bytes 1572872 | tf_op jit(solution)/shard_map/ppermute | solution.py:44
  249.6 11.1 %collective-permute-start.33 = (bf16[2,2,4,32,384]{4,3,2,1,0:T(8,128)(2,1)S(1)}, bf16[2,2,4,32,384]{4,3,2,1,0:T(8,128)(2,1)S(1)}, u32[]{:S(2)}, u32[]{:S(2)}) collective-permute-start(bf16[2,2,4,32,384]{4,3,2,1,0:T(8,128)(2,1)S(1)} %dynamic-slice_bitcast_fusion.1), channel_id=1, source_target_pairs={{0,16},{16,0},{1,17},{17,1},{2,18},{18,2},{3,19},{19,3},{4,20},{20... | collective-permute-start | bytes 1179656 | tf_op jit(solution)/shard_map/ppermute | solution.py:44
  253.6 19.0 %collective-permute-start.32 = (bf16[256,1024]{1,0:T(8,128)(2,1)}, bf16[256,1024]{1,0:T(8,128)(2,1)S(1)}, u32[]{:S(2)}, u32[]{:S(2)}) collective-permute-start(bf16[256,1024]{1,0:T(8,128)(2,1)} %get-tuple-element.141), channel_id=1, source_target_pairs={{0,0},{1,2},{2,4},{3,6},{4,1},{5,3},{6,5},{7,7},{8,8},{9,10},{10,1... | collective-permute-start | bytes 1572872 | tf_op jit(solution)/shard_map/ppermute | solution.py:61
  255.3 17.3 %collective-permute-start.38 = (bf16[256,1024]{1,0:T(8,128)(2,1)S(1)}, bf16[256,1024]{1,0:T(8,128)(2,1)S(1)}, u32[]{:S(2)}, u32[]{:S(2)}) collective-permute-start(bf16[256,1024]{1,0:T(8,128)(2,1)S(1)} %get-tuple-element.151), channel_id=1, source_target_pairs={{0,2},{1,0},{2,6},{3,4},{4,3},{5,1},{6,7},{7,5},{8,10},{9,8},{10,1... | collective-permute-start | bytes 1572872 | tf_op jit(solution)/shard_map/ppermute | solution.py:61
  261.5 6.4 %collective-permute-start.34 = (bf16[2,4,32,384]{3,2,1,0:T(8,128)(2,1)}, bf16[2,4,32,384]{3,2,1,0:T(8,128)(2,1)}, u32[]{:S(2)}, u32[]{:S(2)}) collective-permute-start(bf16[2,4,32,384]{3,2,1,0:T(8,128)(2,1)} %dynamic-slice_bitcast_fusion.4), channel_id=1, source_target_pairs={{0,8},{8,0},{1,9},{9,1},{2,10},{10,2},{3,11},{11,3},{4,12},{12,4},... | collective-permute-start | bytes 589832 | tf_op jit(solution)/shard_map/ppermute | solution.py:44
  262.5 8.3 %collective-permute-start.37 = (bf16[4,32,1152]{2,1,0:T(8,128)(2,1)}, bf16[4,32,1152]{2,1,0:T(8,128)(2,1)S(1)}, u32[]{:S(2)}, u32[]{:S(2)}) collective-permute-start(bf16[4,32,1152]{2,1,0:T(8,128)(2,1)} %dynamic-slice_bitcast_fusion.2), channel_id=1, source_target_pairs={{0,16},{16,0},{1,17},{17,1},{2,18},{18,2},{3,19},{19,3},{4,20},{20... | collective-permute-start | bytes 884744 | tf_op jit(solution)/shard_map/ppermute | solution.py:44
  264.7 6.2 %collective-permute-start.35 = (f32[528,256]{1,0:T(8,128)S(1)}, f32[528,256]{1,0:T(8,128)S(1)}, u32[]{:S(2)}, u32[]{:S(2)}) collective-permute-start(f32[528,256]{1,0:T(8,128)S(1)} %pad_maximum_fusion.7), channel_id=1, source_target_pairs={{0,4},{4,0},{1,5},{5,1},{2,6},{6,2},{3,7},{7,3},{8,12},{12,8},{9,1... | collective-permute-start | bytes 1622024 | tf_op jit(solution)/shard_map/ppermute | solution.py:44
  270.9 1.4 collective-permute-start.36
  271.0 8.9 %collective-permute-start.40 = (bf16[1056,128]{1,0:T(8,128)(2,1)S(1)}, bf16[1056,128]{1,0:T(8,128)(2,1)S(1)}, u32[]{:S(2)}, u32[]{:S(2)}) collective-permute-start(bf16[1056,128]{1,0:T(8,128)(2,1)S(1)} %pad_maximum_fusion.9), channel_id=1, source_target_pairs={{0,8},{8,0},{1,9},{9,1},{2,10},{10,2},{3,11},{11,3},{4,12},{12,4},... | collective-permute-start | bytes 811016 | tf_op jit(solution)/shard_map/ppermute | solution.py:44
  272.4 11.1 %collective-permute-start.39 = (bf16[2,32,1920]{2,1,0:T(8,128)(2,1)S(1)}, bf16[2,32,1920]{2,1,0:T(8,128)(2,1)S(1)}, u32[]{:S(2)}, u32[]{:S(2)}) collective-permute-start(bf16[2,32,1920]{2,1,0:T(8,128)(2,1)S(1)} %pad_maximum_fusion.14), channel_id=1, source_target_pairs={{0,1},{1,0},{2,3},{3,2},{4,5},{5,4},{6,7},{7,6},{8,9},{9,8},{10,11... | collective-permute-start | bytes 737288 | tf_op jit(solution)/shard_map/ppermute | solution.py:48
  283.6 9.7 %collective-permute-start.41 = (bf16[32,2688]{1,0:T(8,128)(2,1)S(1)}, bf16[32,2688]{1,0:T(8,128)(2,1)S(1)}, u32[]{:S(2)}, u32[]{:S(2)}) collective-permute-start(bf16[32,2688]{1,0:T(8,128)(2,1)S(1)} %pad_maximum_fusion.16), channel_id=1, source_target_pairs={{0,2},{1,3},{2,0},{3,1},{4,6},{5,7},{6,4},{7,5},{8,10},{9,11},{10,... | collective-permute-start | bytes 516104 | tf_op jit(solution)/shard_map/ppermute | solution.py:48
  (17 other events, 21.7 us)
Sparse Core Ops, SparseCore 0:
  46.5 84.6 all-gather.2
  194.0 23.9 reduce-scatter.2
  227.6 30.5 reduce-scatter.4

commit v4 on v3

--- a/solution.py
+++ b/solution.py
@@ -243,10 +243,7 @@
     term_ref[...] = term.T.astype(BF16)
 
 
-def middle_body(
-    member_ref, a0_ref, a1_ref, hidden_ref, w_ref,
-    middle_ref, mlp_ref, att_ref, gain_ref,
-):
+def project(member_ref, a0_ref, a1_ref, hidden_ref, w_ref, att_ref):
     member = member_ref[0]
     part = a0_ref.shape[1] // 2
     for m, mask in enumerate((0, 1, 2, 3)):
@@ -254,25 +251,27 @@
         att_ref[:, block_at(member ^ mask, part)] = (a0_ref, a1_ref)[m // 2][:, at : at + part]
     width = att_ref.shape[1]
     pick_gain = jnp.where(lane_in(LANES, 0, 1), jnp.ones((8, LANES), BF16), 0)
-    gain = dot_last(pick_gain, w_ref[:, width:])
-    gain_ref[...] = gain
+    gain = dot_last(pick_gain, w_ref[:, width:])[:1]
     middle = hidden_ref[...].astype(F32) + dot_last(att_ref[...], w_ref[:, :width])
+    scale = lax.rsqrt(jnp.mean(middle * middle, axis=1, keepdims=True) + EPSILON)
+    return middle, scale, gain
+
+
+def middle_body(member_ref, a0_ref, a1_ref, hidden_ref, w_ref, mlp_ref, att_ref):
+    middle, scale, gain = project(member_ref, a0_ref, a1_ref, hidden_ref, w_ref, att_ref)
+    mlp_ref[...] = (middle * scale * gain).astype(BF16)
+
+
+def middle_back_body(
+    blocks, member_ref, core_ref, own_ref, near_ref, far_ref, a0_ref, a1_ref, hidden_ref, cot_ref, w_ref,
+    grad_ref, g0_ref, g1_ref, kept_ref, sent_ref, middle_ref, attended_ref, att_ref, out_ref,
+):
+    middle, scale, gain = project(member_ref, a0_ref, a1_ref, hidden_ref, w_ref, attended_ref)
     middle_ref[...] = middle
-    scale = lax.rsqrt(jnp.mean(middle * middle, axis=1, keepdims=True) + EPSILON)
-    mlp_ref[...] = (middle * scale * gain[:1]).astype(BF16)
-
-
-def middle_back_body(
-    member_ref, own_ref, near_ref, far_ref, middle_ref, gain_ref, cot_ref, attended_ref, w_ref,
-    grad_ref, g0_ref, g1_ref, out_ref, att_ref,
-):
     member = member_ref[0]
     width = att_ref.shape[1]
     part = g0_ref.shape[1] // 2
-    gain = gain_ref[:1]
     mlp_grad = own_ref[0].astype(F32) + near_ref[0].astype(F32) + far_ref[...].astype(F32)
-    middle = middle_ref[...]
-    scale = lax.rsqrt(jnp.mean(middle * middle, axis=1, keepdims=True) + EPSILON)
     normed = middle * scale
     scaled = mlp_grad * gain
     inner = jnp.mean(normed * scaled, axis=1, keepdims=True)
@@ -286,6 +285,13 @@
     out_ref[:, :width] = dot_first(bar, attended_ref[...]).astype(BF16)
     term = jnp.sum(mlp_grad * normed, axis=0, keepdims=True)
     out_ref[:, width:] = jnp.broadcast_to(term, (LANES, term.shape[1])).T.astype(BF16)
+    block = out_ref.shape[0] // blocks
+    for n in range(blocks // 2):
+        low = out_ref[2 * n * block : (2 * n + 1) * block, :]
+        high = out_ref[(2 * n + 1) * block : (2 * n + 2) * block, :]
+        rows = slice(n * block, (n + 1) * block)
+        kept_ref[rows, :] = jnp.where(core_ref[0] == 0, low, high)
+        sent_ref[rows, :] = jnp.where(core_ref[0] == 0, high, low)
 
 
 def start_copies(pairs, sems, first):
@@ -551,16 +557,12 @@
     cots = pair_with(cotangent, cot_far)
     out = [jnp.concatenate([part[:, at : at + vw] for part in (out, sent)], axis=1) for at in (0, vw)]
     out = [home(out[0], 0), home(out[1], 2)]
-    middle, mlp_in, attended, gain8 = kernel_call(
+    (mlp_in,) = kernel_call(
         middle_body,
-        [
-            ((tokens, width), F32),
-            ((tokens, width), BF16),
-            ((tokens, H * DV), BF16),
-            ((8, width), F32),
-        ],
+        [((tokens, width), BF16)],
         (member_arr, *out, hidden_in, output_mat),
         scalars=1,
+        scratch=(pltpu.VMEM((tokens, H * DV), BF16),),
         flops=2**30,
         limit=12,
     )
@@ -621,20 +623,25 @@
     sums = [reduce_terms(terms[h::2]) for h in range(2)]
     totals = [lax.psum_scatter(term, "feat") for term in sums]
 
-    middle_grad, *att_grad, output_term = kernel_call(
-        middle_back_body,
+    middle_grad, *att_grad, output_kept, output_sent, middle = kernel_call(
+        partial(middle_back_body, size),
         [((tokens, width), F32)]
         + [((tokens, 2 * vw), BF16)] * 2
-        + [((width, H * DV + LANES), BF16)],
-        (member_arr, grads, grads_sent, after(grad_far, sums[0]), middle, gain8, cotangent, attended, output_mat),
-        scalars=1,
-        scratch=(pltpu.VMEM((tokens, H * DV), BF16),),
+        + [((width // 2, H * DV + LANES), BF16)] * 2
+        + [((tokens, width), F32)],
+        (member_arr, core.reshape(1), grads, grads_sent, after(grad_far, sums[0]), *out, hidden_in, cotangent, output_mat),
+        scalars=2,
+        scratch=(
+            pltpu.VMEM((tokens, H * DV), BF16),
+            pltpu.VMEM((tokens, H * DV), BF16),
+            pltpu.VMEM((width, H * DV + LANES), BF16),
+        ),
         flops=2**30,
         limit=56,
     )
     att_grad = [away(part, mask) for part, mask in zip(att_grad, (0, 2))]
-    output_term = after(output_term, *att_grad).reshape((2,) * bits + (GROUPS, rows, H * DV + LANES))
-    output_term = reduce_bits(output_term, [0], range(bits))
+    output_term = add_rounded(output_kept, swap_bit(after(output_sent, *att_grad), 0))
+    output_term = output_term.reshape((2,) * len(links) + (GROUPS, rows, H * DV + LANES))
     att_sent = jnp.concatenate([part[:, vw:] for part in att_grad], axis=1)
     att_grad.append(swap_bit(after(att_sent, sums[0]), 0))
     output_term = reduce_bits(output_term, links[:1], links)

time: 306 us -> 300 us (0.980)
  local copies, waits for them, and re-layouts: 17.7 us -> 11.5 us
    dynamic_slice x5 -> x3, local copies, waits for them, and re-layouts: 3.2 us -> 0.1 us  [pick(): return lax.dynamic_index_in_dim(blocks, index, axis, keepdims=False)]
    unnamed x76 -> x74, local copies, waits for them, and re-layouts: 7.22 us -> 4.15 us
  transfers between devices with their start and end apart: 45 -> 45, of which waited for: 21 -> 22; matrix products, arithmetic and copies ran while one was open for 11% -> 10% of each run, Pallas kernels for 11% -> 11%
where the time goes in v4:
time: 300 us; the launch traced here: 298 us
  waiting for transfers between devices  127 us (42%)
  Pallas kernels  63.6 us (21%)
  starting transfers between devices  52.7 us (18%)
  other arithmetic  26.3 us (9%)
  between operations  16.4 us (5%)
  local copies, waits for them, and re-layouts  11.5 us (4%)
    pallas_call x6, Pallas kernels, kernel_call(): pl.pallas_call(body, out_shape=outs, in_specs=[smem] * scalars + [vmem] *...  63.6 us
    ppermute x30, waiting for transfers between devices, hop(): return lax.ppermute(block, f'bit{bit}', [(0, 1), (1, 0)])  59.3 us
    ppermute x30, starting transfers between devices, hop(): return lax.ppermute(block, f'bit{bit}', [(0, 1), (1, 0)])  35.1 us
    ppermute x4, waiting for transfers between devices, cross(): return lax.ppermute(block, 'feat', [(i, i ^ mask) for i in range(GROUPS)])  33.4 us
    ppermute x4, waiting for transfers between devices, away(): lax.ppermute(block, ('bit0', 'feat'), [(b, a) for a, b in home_pairs(mask)])  25.7 us
    convert_element_type x11, other arithmetic, add_rounded(): return (first.astype(F32) + second.astype(F32)).astype(BF16)  12 us
    ppermute x4, starting transfers between devices, away(): lax.ppermute(block, ('bit0', 'feat'), [(b, a) for a, b in home_pairs(mask)])  9.5 us
    ppermute x4, starting transfers between devices, home(): return lax.ppermute(block, ('bit0', 'feat'), home_pairs(mask))  7.09 us
  transfers between devices with their start and end apart: 45, of which 22 were waited for; matrix products, arithmetic and copies ran while one was open for 10% of the time, Pallas kernels for 11%

profile of v4, /device:TPU:0, one launch (start us, length us, event | category | flops | bytes accessed | tf_op | source)
XLA Modules:
  0.0 297.7 jit_solution(5658192556391609901)
XLA Ops:
  7.2 1.7 collective-permute-start.1
  8.9 3.3 %collective-permute-start.2 = (bf16[256,1024]{1,0:T(8,128)(2,1)}, bf16[256,1024]{1,0:T(8,128)(2,1)S(1)}, u32[]{:S(2)}, u32[]{:S(2)}) collective-permute-start(bf16[256,1024]{1,0:T(8,128)(2,1)} %hidden_ref.3), channel_id=1, source_target_pairs={{2,0},{0,1},{6,2},{4,3},{3,4},{1,5},{7,6},{5,7},{10,8},{8,9},{14,1... | collective-permute-start | bytes 1572872 | tf_op jit(solution)/shard_map/ppermute | solution.py:65
  12.9 0.9 reshape.375
  16.3 2.2 collective-permute-start
  18.5 1.2 fusion.16
  19.7 1.6 collective-permute-start.3
  22.3 5.9 %collective-permute-done.3 = bf16[3,2,176,128]{3,2,1,0:T(8,128)(2,1)S(1)} collective-permute-done((bf16[3,2,176,128]{3,2,1,0:T(8,128)(2,1)S(1)}, bf16[3,2,176,128]{3,2,1,0:T(8,128)(2,1)S(1)}, u32[]{:S(2)}, u32[]{:S(2)}) %collective-permute-start.3) | collective-permute-done | bytes 270368 | tf_op jit(solution)/shard_map/ppermute | solution.py:44
  28.3 16.9 %collective-permute-done.6 = bf16[32,2688]{1,0:T(8,128)(2,1)S(1)} collective-permute-done((bf16[32,2688]{1,0:T(8,128)(2,1)S(1)}, bf16[32,2688]{1,0:T(8,128)(2,1)S(1)}, u32[]{:S(2)}, u32[]{:S(2)}) %collective-permute-start.6) | collective-permute-done | bytes 172064 | tf_op jit(solution)/shard_map/ppermute | solution.py:48
  45.5 0.9 pad_maximum_fusion.6
  46.5 5.0 %collective-permute-done.7 = bf16[64,1920]{1,0:T(8,128)(2,1)S(1)} collective-permute-done((bf16[64,1920]{1,0:T(8,128)(2,1)S(1)}, bf16[64,1920]{1,0:T(8,128)(2,1)S(1)}, u32[]{:S(2)}, u32[]{:S(2)}) %collective-permute-start.7) | collective-permute-done | bytes 245792 | tf_op jit(solution)/shard_map/ppermute | solution.py:48
  51.7 1.6 collective-permute-start.8
  53.3 1.6 collective-permute-start.9
  54.9 1.0 pad_maximum_fusion.3
  58.1 9.5 %collective-permute-done.9 = bf16[128,1152]{1,0:T(8,128)(2,1)S(1)} collective-permute-done((bf16[128,1152]{1,0:T(8,128)(2,1)S(1)}, bf16[128,1152]{1,0:T(8,128)(2,1)S(1)}, u32[]{:S(2)}, u32[]{:S(2)}) %collective-permute-start.9) | collective-permute-done | bytes 294944 | tf_op jit(solution)/shard_map/ppermute | solution.py:44
  67.7 2.1 collective-permute-start.10
  70.0 5.5 %collective-permute-done.10 = bf16[4,4,32,384]{3,2,1,0:T(8,128)(2,1)S(1)} collective-permute-done((bf16[4,4,32,384]{3,2,1,0:T(8,128)(2,1)S(1)}, bf16[4,4,32,384]{3,2,1,0:T(8,128)(2,1)S(1)}, u32[]{:S(2)}, u32[]{:S(2)}) %collective-permute-start.10) | collective-permute-done | bytes 393248 | tf_op jit(solution)/shard_map/ppermute | solution.py:44
  75.8 5.4 %shard_map.203 = (bf16[4,256,1024]{2,1,0:T(8,128)(2,1)S(1)}, bf16[1024,384]{1,0:T(8,128)(2,1)S(1)}, bf16[256,512]{1,0:T(8,128)(2,1)S(1)}, bf16[256,512]{1,0:T(8,...) custom-call(s32[1]{0:T(128)S(6)} %select_n.309.first_ref, s32[1]{0:T(128)} %bitcast.9.group_ref, ...), custom_call_target="tpu_custom_call" | custom-call | flops 8589934592 | bytes 8388616 | tf_op jit(solution)/shard_map/pallas_call | solution.py:98
  81.1 1.0 copy-done.9
  82.2 2.0 collective-permute-start.16
  85.2 1.7 collective-permute-start.13
  86.9 0.9 collective-permute-start.12
  87.8 8.9 %collective-permute-done.16.refs_5_.refs_7_ = bf16[256,1024]{1,0:T(8,128)(2,1)S(1)} collective-permute-done((bf16[256,1024]{1,0:T(8,128)(2,1)S(1)}, bf16[256,1024]{1,0:T(8,128)(2,1)S(1)}, u32[]{:S(2)}, u32[]{:S(2)}) %collective-permute-start.16) | collective-permute-done | bytes 524320 | tf_op jit(solution)/shard_map/ppermute | solution.py:44
  98.0 5.9 %collective-permute-done.13.a1_ref = bf16[256,512]{1,0:T(8,128)(2,1)S(1)} collective-permute-done((bf16[256,512]{1,0:T(8,128)(2,1)S(1)}, bf16[256,512]{1,0:T(8,128)(2,1)S(1)}, u32[]{:S(2)}, u32[]{:S(2)}) %collective-permute-start.13) | collective-permute-done | bytes 262176 | tf_op jit(solution)/shard_map/ppermute | solution.py:61
  104.0 1.0 shard_map.204.refs_1_.refs_3_
  105.0 1.3 collective-permute-start.17
  106.2 8.0 %collective-permute-done.17.refs_2_.refs_4_ = bf16[256,1024]{1,0:T(8,128)(2,1)S(1)} collective-permute-done((bf16[256,1024]{1,0:T(8,128)(2,1)S(1)}, bf16[256,1024]{1,0:T(8,128)(2,1)S(1)}, u32[]{:S(2)}, u32[]{:S(2)}) %collective-permute-start.17) | collective-permute-done | bytes 524320 | tf_op jit(solution)/shard_map/ppermute | solution.py:44
  114.3 11.8 %collective-permute-start.19 = (bf16[512,1024]{1,0:T(8,128)(2,1)S(1)}, bf16[512,1024]{1,0:T(8,128)(2,1)S(1)}, u32[]{:S(2)}, u32[]{:S(2)}) collective-permute-start(bf16[512,1024]{1,0:T(8,128)(2,1)S(1)} %pad_maximum_fusion.4), channel_id=1, source_target_pairs={{0,4},{4,0},{1,5},{5,1},{2,6},{6,2},{3,7},{7,3},{8,12},{12,8},{9,1... | collective-permute-start | bytes 3145736 | tf_op jit(solution)/shard_map/ppermute | solution.py:44
  126.1 2.3 collective-permute-done.19.refs_3_.refs_5_
  128.4 2.7 all-gather.3.cloned.1.call-done
  131.2 29.5 %shard_map.205 = (bf16[2,256,1024]{2,1,0:T(8,128)(2,1)}, bf16[2,256,1024]{2,1,0:T(8,128)(2,1)}, bf16[2,256,1024]{2,1,0:T(8,128)(2,1)}, bf16[2,256,1024]{2,1,0:T(...) custom-call(s32[1]{0:T(128)} %bitcast.2.refs_0_, ...), custom_call_target="tpu_custom_call" | custom-call | flops 15032385536 | bytes 17039364 | tf_op jit(solution)/shard_map/pallas_call | solution.py:98
  160.8 1.5 collective-permute-start.22
  162.3 1.3 collective-permute-done.20.near_ref
  163.6 1.6 fusion.17
  165.2 1.5 collective-permute-start.21
  166.8 7.5 %shard_map.208 = (bf16[4,352,512]{2,1,0:T(8,128)(2,1)}, bf16[4,352,512]{2,1,0:T(8,128)(2,1)}) custom-call(s32[1]{0:T(128)} %bitcast.2.refs_0_, bf16[704,1024]{1,0:T(8,128)(2,1)} %get-tuple-element.131.refs_1_, bf16[704,1024]{1,0:T(8,128)(2,1)} %get-tuple-element.132.refs_2_, bf16[256,1024]{1,0:T(8,128)(2,1)} %copy-done.4, bf16[256,1024]{1,0:T(8,128)(2,1)} %copy-done.24, ...), custom_call_target="tpu_custom_call" | custom-call | flops 4294967296 | bytes 9961476 | tf_op jit(solution)/shard_map/pallas_call | solution.py:98
  174.3 5.3 %collective-permute-done.22 = bf16[4,176,512]{2,1,0:T(8,128)(2,1)S(1)} collective-permute-done((bf16[4,176,512]{2,1,0:T(8,128)(2,1)}, bf16[4,176,512]{2,1,0:T(8,128)(2,1)S(1)}, u32[]{:S(2)}, u32[]{:S(2)}) %collective-permute-start.22) | collective-permute-done | bytes 720928 | tf_op jit(solution)/shard_map/ppermute | solution.py:44
  179.5 1.5 collective-permute-start.31
  181.0 1.1 add_convert_fusion.2
  182.1 6.9 %shard_map.206 = (f32[256,1024]{1,0:T(8,128)}, bf16[256,512]{1,0:T(8,128)(2,1)}, bf16[256,512]{1,0:T(8,128)(2,1)}, bf16[512,1152]{1,0:T(8,128)(2,1)}, bf16[512,1152]{1,0:T(8,128)(2,1)}, /*index=5*/f32[256,1024]{1,0:T(8,128)}) custom-call(s32[1]{0:T(128)} %bitcast.member_ref, s32[1]{0:T(128)} %bitcast.1.core_ref, ...), custom_call_target="tpu_custom_call" | custom-call | flops 1073741824 | bytes 11534344 | tf_op jit(solution)/shard_map/pallas_call | solution.py:98
  189.0 1.7 collective-permute-start.24
  190.8 2.8 collective-permute-start.25
  193.6 25.7 %collective-permute-done.25.g1_ref = bf16[256,512]{1,0:T(8,128)(2,1)S(1)} collective-permute-done((bf16[256,512]{1,0:T(8,128)(2,1)}, bf16[256,512]{1,0:T(8,128)(2,1)S(1)}, u32[]{:S(2)}, u32[]{:S(2)}) %collective-permute-start.25) | collective-permute-done | bytes 262176 | tf_op jit(solution)/shard_map/ppermute | solution.py:65
  220.1 1.5 add_convert_fusion
  223.0 1.5 add_convert_fusion.1
  226.1 13.4 %shard_map.207 = (bf16[2,256,1024]{2,1,0:T(8,128)(2,1)}, bf16[2,256,1024]{2,1,0:T(8,128)(2,1)}, bf16[1024,384]{1,0:T(8,128)(2,1)}) custom-call(s32[1]{0:T(128)S(6)} %select_n.309.first_ref, s32[1]{0:T(128)} %bitcast.9.group_ref, bf16[256,512]{1,0:T(8,128)(2,1)} %copy-done.29, bf16[256,512]{1,0:T(8,128)(2,1)} %copy-done.30, bf16[256,512]{1,0:T(8,128)(2,1)} %copy-done.34, ...), custom_call_target="tpu_custom_call" | custom-call | flops 12884901888 | bytes 9437192 | tf_op jit(solution)/shard_map/pallas_call | solution.py:98
  240.0 1.3 fusion.18
  241.3 1.4 collective-permute-start.28
  242.7 1.2 fusion.2
  245.2 2.6 fusion.19
  247.8 1.7 collective-permute-start.32
  249.5 2.8 collective-permute-start.38
  252.2 2.8 collective-permute-done.33
  255.9 0.9 collective-permute-start.34
  256.8 0.9 collective-permute-start.37
  257.7 1.2 maximum_convert_fusion
  259.1 3.0 %collective-permute-done.34 = bf16[2,4,32,384]{3,2,1,0:T(8,128)(2,1)} collective-permute-done((bf16[2,4,32,384]{3,2,1,0:T(8,128)(2,1)}, bf16[2,4,32,384]{3,2,1,0:T(8,128)(2,1)}, u32[]{:S(2)}, u32[]{:S(2)}) %collective-permute-start.34) | collective-permute-done | bytes 196640 | tf_op jit(solution)/shard_map/ppermute | solution.py:44
  262.2 1.0 fusion.21
  263.2 1.9 collective-permute-done.37
  265.4 0.8 collective-permute-start.40
  268.5 2.5 fusion.9
  271.1 3.2 %collective-permute-done.40 = bf16[1056,128]{1,0:T(8,128)(2,1)S(1)} collective-permute-done((bf16[1056,128]{1,0:T(8,128)(2,1)S(1)}, bf16[1056,128]{1,0:T(8,128)(2,1)S(1)}, u32[]{:S(2)}, u32[]{:S(2)}) %collective-permute-start.40) | collective-permute-done | bytes 270368 | tf_op jit(solution)/shard_map/ppermute | solution.py:44
  274.8 2.9 collective-permute-done.39
  277.8 1.0 slice_bitcast_fusion.1
  278.8 8.6 %collective-permute-done.41 = bf16[32,2688]{1,0:T(8,128)(2,1)S(1)} collective-permute-done((bf16[32,2688]{1,0:T(8,128)(2,1)S(1)}, bf16[32,2688]{1,0:T(8,128)(2,1)S(1)}, u32[]{:S(2)}, u32[]{:S(2)}) %collective-permute-start.41) | collective-permute-done | bytes 172064 | tf_op jit(solution)/shard_map/ppermute | solution.py:48
  (222 shorter events, 21.4 us)
Async XLA Ops:
  7.2 124.0 %all-gather.3.cloned.1.call-start = ((), (), s32[]{:S(2)}) async-start(), calls=%async_computation.4 | async-start | bytes 4866048 | tf_op jit(solution)/shard_map/all_gather | solution.py:531
  7.2 38.1 %collective-permute-start.1 = (bf16[256,1024]{1,0:T(8,128)(2,1)}, bf16[256,1024]{1,0:T(8,128)(2,1)S(1)}, u32[]{:S(2)}, u32[]{:S(2)}) collective-permute-start(bf16[256,1024]{1,0:T(8,128)(2,1)} %hidden_ref.3), channel_id=1, source_target_pairs={{0,0},{2,1},{4,2},{6,3},{1,4},{3,5},{5,6},{7,7},{8,8},{10,9},{12,1... | collective-permute-start | bytes 1572872 | tf_op jit(solution)/shard_map/ppermute | solution.py:65
  8.9 36.4 %collective-permute-start.2 = (bf16[256,1024]{1,0:T(8,128)(2,1)}, bf16[256,1024]{1,0:T(8,128)(2,1)S(1)}, u32[]{:S(2)}, u32[]{:S(2)}) collective-permute-start(bf16[256,1024]{1,0:T(8,128)(2,1)} %hidden_ref.3), channel_id=1, source_target_pairs={{2,0},{0,1},{6,2},{4,3},{3,4},{1,5},{7,6},{5,7},{10,8},{8,9},{14,1... | collective-permute-start | bytes 1572872 | tf_op jit(solution)/shard_map/ppermute | solution.py:65
  15.4 5.8 %copy-start.31 = (bf16[32]{0:T(256)(128)(2,1)S(1)}, bf16[32]{0:T(256)(128)(2,1)}, u32[]{:S(2)}) copy-start(bf16[32]{0:T(256)(128)(2,1)} %param.21) | copy-start | bytes 196
  16.3 5.1 %collective-permute-start = (bf16[80,384]{1,0:T(8,128)(2,1)S(1)}, bf16[80,384]{1,0:T(8,128)(2,1)S(1)}, u32[]{:S(2)}, u32[]{:S(2)}) collective-permute-start(bf16[80,384]{1,0:T(8,128)(2,1)S(1)} %concatenate.114), channel_id=1, source_target_pairs={{0,4},{4,0},{1,5},{5,1},{2,6},{6,2},{3,7},{7,3},{8,12},{12,8},{9,1... | collective-permute-start | bytes 184328 | tf_op jit(solution)/shard_map/ppermute | solution.py:44
  18.5 3.1 %copy-start.22 = (bf16[1024,32]{0,1:T(8,128)(2,1)S(1)}, bf16[1024,32]{0,1:T(8,128)(2,1)}, u32[]{:S(2)}) copy-start(bf16[1024,32]{0,1:T(8,128)(2,1)} %param.16) | copy-start | bytes 196612
  19.7 8.5 %collective-permute-start.3 = (bf16[3,2,176,128]{3,2,1,0:T(8,128)(2,1)S(1)}, bf16[3,2,176,128]{3,2,1,0:T(8,128)(2,1)S(1)}, u32[]{:S(2)}, u32[]{:S(2)}) collective-permute-start(bf16[3,2,176,128]{3,2,1,0:T(8,128)(2,1)S(1)} %dynamic-slice_bitcast_fusion.3), channel_id=1, source_target_pairs={{0,8},{8,0},{1,9},{9,1},{2,10},{10,2},{3,11},{11,3},{4,12},{12,4},... | collective-permute-start | bytes 811016 | tf_op jit(solution)/shard_map/ppermute | solution.py:44
  21.6 23.6 %collective-permute-start.6 = (bf16[32,2688]{1,0:T(8,128)(2,1)S(1)}, bf16[32,2688]{1,0:T(8,128)(2,1)S(1)}, u32[]{:S(2)}, u32[]{:S(2)}) collective-permute-start(bf16[32,2688]{1,0:T(8,128)(2,1)S(1)} %pad_maximum_fusion.15), channel_id=1, source_target_pairs={{0,2},{1,3},{2,0},{3,1},{4,6},{5,7},{6,4},{7,5},{8,10},{9,11},{10,... | collective-permute-start | bytes 516104 | tf_op jit(solution)/shard_map/ppermute | solution.py:48
  28.2 17.2 %collective-permute-start.4 = (bf16[3,176,256]{2,1,0:T(8,128)(2,1)S(1)}, bf16[3,176,256]{2,1,0:T(8,128)(2,1)S(1)}, u32[]{:S(2)}, u32[]{:S(2)}) collective-permute-start(bf16[3,176,256]{2,1,0:T(8,128)(2,1)S(1)} %pad_maximum_fusion.8), channel_id=1, source_target_pairs={{0,4},{4,0},{1,5},{5,1},{2,6},{6,2},{3,7},{7,3},{8,12},{12,8},{9,1... | collective-permute-start | bytes 811016 | tf_op jit(solution)/shard_map/ppermute | solution.py:44
  45.3 6.3 %collective-permute-start.7 = (bf16[64,1920]{1,0:T(8,128)(2,1)S(1)}, bf16[64,1920]{1,0:T(8,128)(2,1)S(1)}, u32[]{:S(2)}, u32[]{:S(2)}) collective-permute-start(bf16[64,1920]{1,0:T(8,128)(2,1)S(1)} %pad_maximum_fusion.13), channel_id=1, source_target_pairs={{0,1},{1,0},{2,3},{3,2},{4,5},{5,4},{6,7},{7,6},{8,9},{9,8},{10,11... | collective-permute-start | bytes 737288 | tf_op jit(solution)/shard_map/ppermute | solution.py:48
  46.4 211.4 %reduce-scatter.3.cloned.1.call-start = ((), (), s32[]{:S(2)}) async-start(), calls=%async_computation.2 | async-start | bytes 901120 | tf_op jit(solution)/shard_map/reduce_scatter | solution.py:624
  51.7 5.7 %collective-permute-start.8 = (bf16[2,4,32,384]{3,0,2,1:T(2,128)(2,1)S(1)}, bf16[2,4,32,384]{3,0,2,1:T(2,128)(2,1)S(1)}, u32[]{:S(2)}, u32[]{:S(2)}) collective-permute-start(bf16[2,4,32,384]{3,0,2,1:T(2,128)(2,1)S(1)} %bitcast.206), channel_id=1, source_target_pairs={{0,8},{8,0},{1,9},{9,1},{2,10},{10,2},{3,11},{11,3},{4,12},{12,4},... | collective-permute-start | bytes 589832 | tf_op jit(solution)/shard_map/ppermute | solution.py:44
  53.3 14.3 %collective-permute-start.9 = (bf16[128,1152]{1,0:T(8,128)(2,1)S(1)}, bf16[128,1152]{1,0:T(8,128)(2,1)S(1)}, u32[]{:S(2)}, u32[]{:S(2)}) collective-permute-start(bf16[128,1152]{1,0:T(8,128)(2,1)S(1)} %bitcast.183), channel_id=1, source_target_pairs={{0,16},{16,0},{1,17},{17,1},{2,18},{18,2},{3,19},{19,3},{4,20},{20... | collective-permute-start | bytes 884744 | tf_op jit(solution)/shard_map/ppermute | solution.py:44
  55.9 19.8 %collective-permute-start.5 = (bf16[512,1024]{1,0:T(8,128)(2,1)}, bf16[512,1024]{1,0:T(8,128)(2,1)S(1)}, u32[]{:S(2)}, u32[]{:S(2)}) collective-permute-start(bf16[512,1024]{1,0:T(8,128)(2,1)} %pad_maximum_fusion.3), channel_id=1, source_target_pairs={{0,4},{4,0},{1,5},{5,1},{2,6},{6,2},{3,7},{7,3},{8,12},{12,8},{9,1... | collective-permute-start | bytes 3145736 | tf_op jit(solution)/shard_map/ppermute | solution.py:44
  67.7 14.5 %collective-permute-start.14 = (bf16[2,128,1152]{2,1,0:T(8,128)(2,1)S(1)}, bf16[2,128,1152]{2,1,0:T(8,128)(2,1)S(1)}, u32[]{:S(2)}, u32[]{:S(2)}) collective-permute-start(bf16[2,128,1152]{2,1,0:T(8,128)(2,1)S(1)} %maximum_select_fusion.4), channel_id=1, source_target_pairs={{0,8},{8,0},{1,9},{9,1},{2,10},{10,2},{3,11},{11,3},{4,12},{12,4},... | collective-permute-start | bytes 1769480 | tf_op jit(solution)/shard_map/ppermute | solution.py:44
  67.7 7.8 %collective-permute-start.10 = (bf16[4,4,32,384]{3,2,1,0:T(8,128)(2,1)S(1)}, bf16[4,4,32,384]{3,2,1,0:T(8,128)(2,1)S(1)}, u32[]{:S(2)}, u32[]{:S(2)}) collective-permute-start(bf16[4,4,32,384]{3,2,1,0:T(8,128)(2,1)S(1)} %bitcast.197), channel_id=1, source_target_pairs={{0,16},{16,0},{1,17},{17,1},{2,18},{18,2},{3,19},{19,3},{4,20},{20... | collective-permute-start | bytes 1179656 | tf_op jit(solution)/shard_map/ppermute | solution.py:44
  75.7 5.4 %copy-start.3 = (bf16[2,4,4,32,384]{4,3,2,1,0:T(8,128)(2,1)}, bf16[2,4,4,32,384]{4,3,2,1,0:T(8,128)(2,1)S(1)}, u32[]{:S(2)}) copy-start(bf16[2,4,4,32,384]{4,3,2,1,0:T(8,128)(2,1)S(1)} %maximum_select_fusion.2) | copy-start | bytes 2359300
  75.7 6.4 %copy-start.12 = (bf16[256,1024]{1,0:T(8,128)(2,1)S(1)}, bf16[256,1024]{1,0:T(8,128)(2,1)}, u32[]{:S(2)}) copy-start(bf16[256,1024]{1,0:T(8,128)(2,1)} %refs_6_.1) | copy-start | bytes 1572868
  82.1 2.3 copy-start.10
  82.1 2.6 collective-permute-start.11
  82.2 14.6 %collective-permute-start.16 = (bf16[256,1024]{1,0:T(8,128)(2,1)S(1)}, bf16[256,1024]{1,0:T(8,128)(2,1)S(1)}, u32[]{:S(2)}, u32[]{:S(2)}) collective-permute-start(bf16[256,1024]{1,0:T(8,128)(2,1)S(1)} %copy-done.12), channel_id=1, source_target_pairs={{0,8},{8,0},{1,9},{9,1},{2,10},{10,2},{3,11},{11,3},{4,12},{12,4},... | collective-permute-start | bytes 1572872 | tf_op jit(solution)/shard_map/ppermute | solution.py:44
  84.7 12.2 %collective-permute-start.15 = (bf16[2,2,128,1152]{3,2,1,0:T(8,128)(2,1)S(1)}, bf16[2,2,128,1152]{3,2,1,0:T(8,128)(2,1)S(1)}, u32[]{:S(2)}, u32[]{:S(2)}) collective-permute-start(bf16[2,2,128,1152]{3,2,1,0:T(8,128)(2,1)S(1)} %maximum_select_fusion.1), channel_id=1, source_target_pairs={{0,4},{4,0},{1,5},{5,1},{2,6},{6,2},{3,7},{7,3},{8,12},{12,8},{9,1... | collective-permute-start | bytes 3538952 | tf_op jit(solution)/shard_map/ppermute | solution.py:44
  85.2 18.8 %collective-permute-start.13 = (bf16[256,512]{1,0:T(8,128)(2,1)S(1)}, bf16[256,512]{1,0:T(8,128)(2,1)S(1)}, u32[]{:S(2)}, u32[]{:S(2)}) collective-permute-start(bf16[256,512]{1,0:T(8,128)(2,1)S(1)} %pad_maximum_fusion.11), channel_id=1, source_target_pairs={{0,2},{1,0},{2,6},{3,4},{4,3},{5,1},{6,7},{7,5},{8,10},{9,8},{10,1... | collective-permute-start | bytes 786440 | tf_op jit(solution)/shard_map/ppermute | solution.py:61
  86.9 17.1 %collective-permute-start.12 = (bf16[256,512]{1,0:T(8,128)(2,1)S(1)}, bf16[256,512]{1,0:T(8,128)(2,1)S(1)}, u32[]{:S(2)}, u32[]{:S(2)}) collective-permute-start(bf16[256,512]{1,0:T(8,128)(2,1)S(1)} %pad_maximum_fusion.10), channel_id=1, source_target_pairs={{0,0},{1,2},{2,4},{3,6},{4,1},{5,3},{6,5},{7,7},{8,8},{9,10},{10,1... | collective-permute-start | bytes 786440 | tf_op jit(solution)/shard_map/ppermute | solution.py:61
  96.9 17.4 %collective-permute-start.18 = (bf16[512,1024]{1,0:T(8,128)(2,1)S(1)}, bf16[512,1024]{1,0:T(8,128)(2,1)S(1)}, u32[]{:S(2)}, u32[]{:S(2)}) collective-permute-start(bf16[512,1024]{1,0:T(8,128)(2,1)S(1)} %pad_maximum_fusion.5), channel_id=1, source_target_pairs={{0,4},{4,0},{1,5},{5,1},{2,6},{6,2},{3,7},{7,3},{8,12},{12,8},{9,1... | collective-permute-start | bytes 3145736 | tf_op jit(solution)/shard_map/ppermute | solution.py:44
  97.6 6.4 %copy-start.1 = (bf16[256,1024]{1,0:T(8,128)(2,1)S(1)}, bf16[256,1024]{1,0:T(8,128)(2,1)}, u32[]{:S(2)}) copy-start(bf16[256,1024]{1,0:T(8,128)(2,1)} %hidden_ref.3) | copy-start | bytes 1572868
  98.0 6.9 %copy-start = (bf16[2,2,2,128,1152]{4,3,2,1,0:T(8,128)(2,1)}, bf16[2,2,2,128,1152]{4,3,2,1,0:T(8,128)(2,1)S(1)}, u32[]{:S(2)}) copy-start(bf16[2,2,2,128,1152]{4,3,2,1,0:T(8,128)(2,1)S(1)} %maximum_select_fusion) | copy-start | bytes 7077892
  105.0 26.2 %copy-start.4 = (bf16[256,1024]{1,0:T(8,128)(2,1)}, bf16[256,1024]{1,0:T(8,128)(2,1)S(1)}, u32[]{:S(2)}) copy-start(bf16[256,1024]{1,0:T(8,128)(2,1)S(1)} %shard_map.204.refs_1_.refs_3_) | copy-start | bytes 1572868
  105.0 9.2 %collective-permute-start.17 = (bf16[256,1024]{1,0:T(8,128)(2,1)S(1)}, bf16[256,1024]{1,0:T(8,128)(2,1)S(1)}, u32[]{:S(2)}, u32[]{:S(2)}) collective-permute-start(bf16[256,1024]{1,0:T(8,128)(2,1)S(1)} %shard_map.204.refs_1_.refs_3_), channel_id=1, source_target_pairs={{0,8},{8,0},{1,9},{9,1},{2,10},{10,2},{3,11},{11,3},{4,12},{12,4},... | collective-permute-start | bytes 1572872 | tf_op jit(solution)/shard_map/ppermute | solution.py:44
  114.2 16.9 %copy-start.24 = (bf16[256,1024]{1,0:T(8,128)(2,1)}, bf16[256,1024]{1,0:T(8,128)(2,1)S(1)}, u32[]{:S(2)}) copy-start(bf16[256,1024]{1,0:T(8,128)(2,1)S(1)} %collective-permute-done.17.refs_2_.refs_4_) | copy-start | bytes 1572868
  114.3 11.8 %copy-start.32 = (bf16[512,1024]{1,0:T(8,128)(2,1)}, bf16[512,1024]{1,0:T(8,128)(2,1)S(1)}, u32[]{:S(2)}) copy-start(bf16[512,1024]{1,0:T(8,128)(2,1)S(1)} %collective-permute-done.18.refs_6_.refs_8_) | copy-start | bytes 3145732
  114.3 14.1 %collective-permute-start.19 = (bf16[512,1024]{1,0:T(8,128)(2,1)S(1)}, bf16[512,1024]{1,0:T(8,128)(2,1)S(1)}, u32[]{:S(2)}, u32[]{:S(2)}) collective-permute-start(bf16[512,1024]{1,0:T(8,128)(2,1)S(1)} %pad_maximum_fusion.4), channel_id=1, source_target_pairs={{0,4},{4,0},{1,5},{5,1},{2,6},{6,2},{3,7},{7,3},{8,12},{12,8},{9,1... | collective-permute-start | bytes 3145736 | tf_op jit(solution)/shard_map/ppermute | solution.py:44
  128.4 2.8 copy-start.33
  160.7 2.9 collective-permute-start.20
  160.8 18.8 %collective-permute-start.22 = (bf16[4,176,512]{2,1,0:T(8,128)(2,1)}, bf16[4,176,512]{2,1,0:T(8,128)(2,1)S(1)}, u32[]{:S(2)}, u32[]{:S(2)}) collective-permute-start(bf16[4,176,512]{2,1,0:T(8,128)(2,1)} %get-tuple-element.104), channel_id=1, source_target_pairs={{0,16},{16,0},{1,17},{17,1},{2,18},{18,2},{3,19},{19,3},{4,20},{20... | collective-permute-start | bytes 2162696 | tf_op jit(solution)/shard_map/ppermute | solution.py:44
  163.6 10.6 %copy-start.11 = (bf16[2,256,1024]{2,1,0:T(8,128)(2,1)}, bf16[2,256,1024]{2,1,0:T(8,128)(2,1)S(1)}, u32[]{:S(2)}) copy-start(bf16[2,256,1024]{2,1,0:T(8,128)(2,1)S(1)} %collective-permute-done.20.near_ref) | copy-start | bytes 3145732
  165.2 15.8 %collective-permute-start.21 = (bf16[256,1024]{1,0:T(8,128)(2,1)S(1)}, bf16[256,1024]{1,0:T(8,128)(2,1)S(1)}, u32[]{:S(2)}, u32[]{:S(2)}) collective-permute-start(bf16[256,1024]{1,0:T(8,128)(2,1)S(1)} %fusion.17), channel_id=1, source_target_pairs={{0,8},{8,0},{1,9},{9,1},{2,10},{10,2},{3,11},{11,3},{4,12},{12,4},... | collective-permute-start | bytes 1572872 | tf_op jit(solution)/shard_map/ppermute | solution.py:44
  166.8 52.6 %collective-permute-start.23 = (bf16[2,256,1024]{2,1,0:T(8,128)(2,1)}, bf16[2,256,1024]{2,1,0:T(8,128)(2,1)}, u32[]{:S(2)}, u32[]{:S(2)}) collective-permute-start(bf16[2,256,1024]{2,1,0:T(8,128)(2,1)} %get-tuple-element.109), channel_id=1, source_target_pairs={{0,4},{4,0},{1,5},{5,1},{2,6},{6,2},{3,7},{7,3},{8,12},{12,8},{9,1... | collective-permute-start | bytes 3145736 | tf_op jit(solution)/shard_map/ppermute | solution.py:44
  166.8 14.3 %copy-start.21 = (bf16[4,176,512]{2,1,0:T(8,128)(2,1)S(1)}, bf16[4,176,512]{2,1,0:T(8,128)(2,1)}, u32[]{:S(2)}) copy-start(bf16[4,176,512]{2,1,0:T(8,128)(2,1)} %get-tuple-element.102) | copy-start | bytes 2162692
  179.5 40.6 %collective-permute-start.31 = (bf16[4,352,512]{2,1,0:T(8,128)(2,1)}, bf16[4,352,512]{2,1,0:T(8,128)(2,1)S(1)}, u32[]{:S(2)}, u32[]{:S(2)}) collective-permute-start(bf16[4,352,512]{2,1,0:T(8,128)(2,1)} %get-tuple-element.136), channel_id=1, source_target_pairs={{0,16},{16,0},{1,17},{17,1},{2,18},{18,2},{3,19},{19,3},{4,20},{20... | collective-permute-start | bytes 4325384 | tf_op jit(solution)/shard_map/ppermute | solution.py:44
  189.0 31.1 %copy-start.13 = (bf16[4,352,512]{2,1,0:T(8,128)(2,1)S(1)}, bf16[4,352,512]{2,1,0:T(8,128)(2,1)}, u32[]{:S(2)}) copy-start(bf16[4,352,512]{2,1,0:T(8,128)(2,1)} %get-tuple-element.134) | copy-start | bytes 4325380
  189.0 4.6 %collective-permute-start.24 = (bf16[256,512]{1,0:T(8,128)(2,1)}, bf16[256,512]{1,0:T(8,128)(2,1)S(1)}, u32[]{:S(2)}, u32[]{:S(2)}) collective-permute-start(bf16[256,512]{1,0:T(8,128)(2,1)} %get-tuple-element.112), channel_id=1, source_target_pairs={{0,0},{2,1},{4,2},{6,3},{1,4},{3,5},{5,6},{7,7},{8,8},{10,9},{12,1... | collective-permute-start | bytes 786440 | tf_op jit(solution)/shard_map/ppermute | solution.py:65
  190.8 28.6 %collective-permute-start.25 = (bf16[256,512]{1,0:T(8,128)(2,1)}, bf16[256,512]{1,0:T(8,128)(2,1)S(1)}, u32[]{:S(2)}, u32[]{:S(2)}) collective-permute-start(bf16[256,512]{1,0:T(8,128)(2,1)} %get-tuple-element.113), channel_id=1, source_target_pairs={{2,0},{0,1},{6,2},{4,3},{3,4},{1,5},{7,6},{5,7},{10,8},{8,9},{14,1... | collective-permute-start | bytes 786440 | tf_op jit(solution)/shard_map/ppermute | solution.py:65
  193.5 64.2 %reduce-scatter.5.cloned.1.call-start = ((), (), s32[]{:S(2)}) async-start(), calls=%async_computation.3 | async-start | bytes 1802240 | tf_op jit(solution)/shard_map/reduce_scatter | solution.py:624
  193.6 28.1 %copy-start.29 = (bf16[256,512]{1,0:T(8,128)(2,1)}, bf16[256,512]{1,0:T(8,128)(2,1)S(1)}, u32[]{:S(2)}) copy-start(bf16[256,512]{1,0:T(8,128)(2,1)S(1)} %collective-permute-done.24.g0_ref) | copy-start | bytes 786436
  219.4 3.2 %collective-permute-start.26 = (bf16[512,1152]{1,0:T(8,128)(2,1)}, bf16[512,1152]{1,0:T(8,128)(2,1)}, u32[]{:S(2)}, u32[]{:S(2)}) collective-permute-start(bf16[512,1152]{1,0:T(8,128)(2,1)} %get-tuple-element.115), channel_id=1, source_target_pairs={{0,4},{4,0},{1,5},{5,1},{2,6},{6,2},{3,7},{7,3},{8,12},{12,8},{9,1... | collective-permute-start | bytes 3538952 | tf_op jit(solution)/shard_map/ppermute | solution.py:44
  222.5 2.8 collective-permute-start.29
  224.6 16.7 %collective-permute-start.27 = (bf16[2,4,32,1152]{3,2,1,0:T(8,128)(2,1)S(1)}, bf16[2,4,32,1152]{3,2,1,0:T(8,128)(2,1)}, u32[]{:S(2)}, u32[]{:S(2)}) collective-permute-start(bf16[2,4,32,1152]{3,2,1,0:T(8,128)(2,1)S(1)} %dynamic-slice_bitcast_fusion), channel_id=1, source_target_pairs={{0,8},{8,0},{1,9},{9,1},{2,10},{10,2},{3,11},{11,3},{4,12},{12,4},... | collective-permute-start | bytes 1769480 | tf_op jit(solution)/shard_map/ppermute | solution.py:44
  226.1 13.6 %copy-start.2 = (bf16[256,1024]{1,0:T(8,128)(2,1)S(1)}, bf16[256,1024]{1,0:T(8,128)(2,1)}, u32[]{:S(2)}) copy-start(bf16[256,1024]{1,0:T(8,128)(2,1)} %hidden_ref.3) | copy-start | bytes 1572868
  226.1 13.8 %copy-start.15 = (bf16[2,256,1024]{2,1,0:T(8,128)(2,1)S(1)}, bf16[2,256,1024]{2,1,0:T(8,128)(2,1)}, u32[]{:S(2)}) copy-start(bf16[2,256,1024]{2,1,0:T(8,128)(2,1)} %get-tuple-element.107) | copy-start | bytes 3145732
  239.5 4.4 %collective-permute-start.30 = (bf16[2,256,1024]{2,1,0:T(8,128)(2,1)}, bf16[2,256,1024]{2,1,0:T(8,128)(2,1)}, u32[]{:S(2)}, u32[]{:S(2)}) collective-permute-start(bf16[2,256,1024]{2,1,0:T(8,128)(2,1)} %get-tuple-element.130), channel_id=1, source_target_pairs={{0,4},{4,0},{1,5},{5,1},{2,6},{6,2},{3,7},{7,3},{8,12},{12,8},{9,1... | collective-permute-start | bytes 3145736 | tf_op jit(solution)/shard_map/ppermute | solution.py:44
  239.9 3.9 %copy-start.20 = (bf16[1024,384]{1,0:T(8,128)(2,1)S(1)}, bf16[1024,384]{1,0:T(8,128)(2,1)}, u32[]{:S(2)}) copy-start(bf16[1024,384]{1,0:T(8,128)(2,1)} %get-tuple-element.139) | copy-start | bytes 2359300
  241.3 3.9 %copy-start.19 = (bf16[2,256,1024]{2,1,0:T(8,128)(2,1)S(1)}, bf16[2,256,1024]{2,1,0:T(8,128)(2,1)}, u32[]{:S(2)}) copy-start(bf16[2,256,1024]{2,1,0:T(8,128)(2,1)} %get-tuple-element.128) | copy-start | bytes 3145732
  241.3 14.6 %collective-permute-start.28 = (bf16[256,1024]{1,0:T(8,128)(2,1)S(1)}, bf16[256,1024]{1,0:T(8,128)(2,1)S(1)}, u32[]{:S(2)}, u32[]{:S(2)}) collective-permute-start(bf16[256,1024]{1,0:T(8,128)(2,1)S(1)} %fusion.18), channel_id=1, source_target_pairs={{0,8},{8,0},{1,9},{9,1},{2,10},{10,2},{3,11},{11,3},{4,12},{12,4},... | collective-permute-start | bytes 1572872 | tf_op jit(solution)/shard_map/ppermute | solution.py:44
  244.0 11.1 %collective-permute-start.33 = (bf16[2,2,4,32,384]{4,3,2,1,0:T(8,128)(2,1)S(1)}, bf16[2,2,4,32,384]{4,3,2,1,0:T(8,128)(2,1)S(1)}, u32[]{:S(2)}, u32[]{:S(2)}) collective-permute-start(bf16[2,2,4,32,384]{4,3,2,1,0:T(8,128)(2,1)S(1)} %dynamic-slice_bitcast_fusion.1), channel_id=1, source_target_pairs={{0,16},{16,0},{1,17},{17,1},{2,18},{18,2},{3,19},{19,3},{4,20},{20... | collective-permute-start | bytes 1179656 | tf_op jit(solution)/shard_map/ppermute | solution.py:44
  247.8 19.1 %collective-permute-start.32 = (bf16[256,1024]{1,0:T(8,128)(2,1)}, bf16[256,1024]{1,0:T(8,128)(2,1)S(1)}, u32[]{:S(2)}, u32[]{:S(2)}) collective-permute-start(bf16[256,1024]{1,0:T(8,128)(2,1)} %get-tuple-element.137), channel_id=1, source_target_pairs={{0,0},{1,2},{2,4},{3,6},{4,1},{5,3},{6,5},{7,7},{8,8},{9,10},{10,1... | collective-permute-start | bytes 1572872 | tf_op jit(solution)/shard_map/ppermute | solution.py:61
  249.5 17.4 %collective-permute-start.38 = (bf16[256,1024]{1,0:T(8,128)(2,1)}, bf16[256,1024]{1,0:T(8,128)(2,1)S(1)}, u32[]{:S(2)}, u32[]{:S(2)}) collective-permute-start(bf16[256,1024]{1,0:T(8,128)(2,1)} %get-tuple-element.147), channel_id=1, source_target_pairs={{0,2},{1,0},{2,6},{3,4},{4,3},{5,1},{6,7},{7,5},{8,10},{9,8},{10,1... | collective-permute-start | bytes 1572872 | tf_op jit(solution)/shard_map/ppermute | solution.py:61
  255.9 6.3 %collective-permute-start.34 = (bf16[2,4,32,384]{3,2,1,0:T(8,128)(2,1)}, bf16[2,4,32,384]{3,2,1,0:T(8,128)(2,1)}, u32[]{:S(2)}, u32[]{:S(2)}) collective-permute-start(bf16[2,4,32,384]{3,2,1,0:T(8,128)(2,1)} %dynamic-slice_bitcast_fusion.4), channel_id=1, source_target_pairs={{0,8},{8,0},{1,9},{9,1},{2,10},{10,2},{3,11},{11,3},{4,12},{12,4},... | collective-permute-start | bytes 589832 | tf_op jit(solution)/shard_map/ppermute | solution.py:44
  256.8 8.3 %collective-permute-start.37 = (bf16[4,32,1152]{2,1,0:T(8,128)(2,1)}, bf16[4,32,1152]{2,1,0:T(8,128)(2,1)S(1)}, u32[]{:S(2)}, u32[]{:S(2)}) collective-permute-start(bf16[4,32,1152]{2,1,0:T(8,128)(2,1)} %dynamic-slice_bitcast_fusion.2), channel_id=1, source_target_pairs={{0,16},{16,0},{1,17},{17,1},{2,18},{18,2},{3,19},{19,3},{4,20},{20... | collective-permute-start | bytes 884744 | tf_op jit(solution)/shard_map/ppermute | solution.py:44
  259.0 6.2 %collective-permute-start.35 = (f32[528,256]{1,0:T(8,128)S(1)}, f32[528,256]{1,0:T(8,128)S(1)}, u32[]{:S(2)}, u32[]{:S(2)}) collective-permute-start(f32[528,256]{1,0:T(8,128)S(1)} %pad_maximum_fusion.7), channel_id=1, source_target_pairs={{0,4},{4,0},{1,5},{5,1},{2,6},{6,2},{3,7},{7,3},{8,12},{12,8},{9,1... | collective-permute-start | bytes 1622024 | tf_op jit(solution)/shard_map/ppermute | solution.py:44
  265.2 1.4 collective-permute-start.36
  265.4 8.9 %collective-permute-start.40 = (bf16[1056,128]{1,0:T(8,128)(2,1)S(1)}, bf16[1056,128]{1,0:T(8,128)(2,1)S(1)}, u32[]{:S(2)}, u32[]{:S(2)}) collective-permute-start(bf16[1056,128]{1,0:T(8,128)(2,1)S(1)} %pad_maximum_fusion.9), channel_id=1, source_target_pairs={{0,8},{8,0},{1,9},{9,1},{2,10},{10,2},{3,11},{11,3},{4,12},{12,4},... | collective-permute-start | bytes 811016 | tf_op jit(solution)/shard_map/ppermute | solution.py:44
  266.8 10.9 %collective-permute-start.39 = (bf16[2,32,1920]{2,1,0:T(8,128)(2,1)S(1)}, bf16[2,32,1920]{2,1,0:T(8,128)(2,1)S(1)}, u32[]{:S(2)}, u32[]{:S(2)}) collective-permute-start(bf16[2,32,1920]{2,1,0:T(8,128)(2,1)S(1)} %pad_maximum_fusion.14), channel_id=1, source_target_pairs={{0,1},{1,0},{2,3},{3,2},{4,5},{5,4},{6,7},{7,6},{8,9},{9,8},{10,11... | collective-permute-start | bytes 737288 | tf_op jit(solution)/shard_map/ppermute | solution.py:48
  277.7 9.6 %collective-permute-start.41 = (bf16[32,2688]{1,0:T(8,128)(2,1)S(1)}, bf16[32,2688]{1,0:T(8,128)(2,1)S(1)}, u32[]{:S(2)}, u32[]{:S(2)}) collective-permute-start(bf16[32,2688]{1,0:T(8,128)(2,1)S(1)} %pad_maximum_fusion.16), channel_id=1, source_target_pairs={{0,2},{1,3},{2,0},{3,1},{4,6},{5,7},{6,4},{7,5},{8,10},{9,11},{10,... | collective-permute-start | bytes 516104 | tf_op jit(solution)/shard_map/ppermute | solution.py:48
  (16 other events, 23.3 us)
Sparse Core Ops, SparseCore 0:
  46.5 84.6 all-gather.2
  193.7 24.9 reduce-scatter.2
  221.8 30.8 reduce-scatter.4

commit v5 on v4

--- a/solution.py
+++ b/solution.py
@@ -304,7 +304,7 @@
     return copies
 
 
-def forward_units(x_blocks, c_blocks, weights_ref, hidden_refs, put):
+def forward_units(x_blocks, c_blocks, weights_ref, hidden_refs, ready, put):
     wg_ref, wu_ref, wd_ref = (weights_ref.at[m] for m in range(3))
     total = weights_ref.shape[1]
     edges = list(range(0, total, TILE)) + [total]
@@ -314,12 +314,13 @@
     for b, (x_ref, c_ref) in enumerate(zip(x_blocks, c_blocks)):
         rows = slice(b * tokens, (b + 1) * tokens)
         x_rows = x_ref[...]
-        c_rows = c_ref[...]
         kept = []
         for low, high in spans:
             gate = dot_last(x_rows, wg_ref[low:high, :])
             up = dot_last(x_rows, wu_ref[low:high, :])
-            back = dot_last(c_rows, wd_ref[low:high, :])
+            if b == 0 and low == 0:
+                ready()
+            back = dot_last(c_ref[...], wd_ref[low:high, :])
             sig = 1.0 / (1.0 + jnp.exp(-gate))
             silu = gate * sig
             act = (silu * up).astype(BF16)
@@ -368,22 +369,32 @@
     term_refs, refs = refs[:parts], refs[parts:]
     rows_ref, weights_ref, hidden_refs, branch_buf, grad_buf, term_buf, sems = *refs[:2], refs[2:5], *refs[5:]
     tokens = sources[0].shape[0]
-    pairs = [
+    rows = [
         (source, rows_ref.at[n // 3, pl.ds(tokens * (n % 3), source.shape[0]), :])
         for n, source in enumerate(sources)
     ]
     count, slots, _, part = piece_ref.shape
-    pairs += [
-        (
-            piece_ref.at[y, s, pl.ds(m * units, units), :],
-            weights_ref.at[m, pl.ds(s * units, units), pl.ds(y * part, part)],
-        )
+    mats = [
+        [
+            (
+                piece_ref.at[y, s, pl.ds(m * units, units), :],
+                weights_ref.at[m, pl.ds(s * units, units), pl.ds(y * part, part)],
+            )
+            for y in range(count)
+            for s in range(slots)
+        ]
         for m in range(3)
-        for y in range(count)
-        for s in range(slots)
     ]
-    for copy in start_copies(pairs, sems, 0):
+    early = rows[:3] + mats[0] + mats[1]
+    pairs = early + rows[3:] + mats[2]
+    loads = start_copies(pairs, sems, 0)
+    for copy in loads[: len(early)]:
         copy.wait()
+
+    def ready():
+        for copy in loads[len(early) :]:
+            copy.wait()
+
     x_blocks, c_blocks = (
         [rows_ref.at[n, pl.ds(tokens * b, tokens), :] for b in range(SPLIT)] for n in range(2)
     )
@@ -401,7 +412,7 @@
         done += [(ref.at[:, lanes], out.at[:, lanes]) for ref, out in outs]
         stores.extend(start_copies(done, sems, len(pairs) + len(stores)))
 
-    forward_units(x_blocks, c_blocks, weights_ref, hidden_refs, put)
+    forward_units(x_blocks, c_blocks, weights_ref, hidden_refs, ready, put)
     for n, term_ref in enumerate(term_refs):
         index = index_ref[0] if n == parts - 1 else 1 - index_ref[0]
         weight_terms(units, index, 0, hidden_refs[1], rows_ref.at[0], term_buf.at[n])

time: 300 us -> 299 us (level)
  no operation moved by 1% of the time
where the time goes in v5:
time: 299 us; the launch traced here: 297 us
  waiting for transfers between devices  127 us (42%)
  Pallas kernels  63.3 us (21%)
  starting transfers between devices  52.8 us (18%)
  other arithmetic  26.3 us (9%)
  between operations  16.4 us (5%)
  local copies, waits for them, and re-layouts  11.5 us (4%)
    pallas_call x6, Pallas kernels, kernel_call(): pl.pallas_call(body, out_shape=outs, in_specs=[smem] * scalars + [vmem] *...  63.3 us
    ppermute x30, waiting for transfers between devices, hop(): return lax.ppermute(block, f'bit{bit}', [(0, 1), (1, 0)])  59.3 us
    ppermute x30, starting transfers between devices, hop(): return lax.ppermute(block, f'bit{bit}', [(0, 1), (1, 0)])  35.3 us
    ppermute x4, waiting for transfers between devices, cross(): return lax.ppermute(block, 'feat', [(i, i ^ mask) for i in range(GROUPS)])  33.4 us
    ppermute x4, waiting for transfers between devices, away(): lax.ppermute(block, ('bit0', 'feat'), [(b, a) for a, b in home_pairs(mask)])  25.7 us
    convert_element_type x11, other arithmetic, add_rounded(): return (first.astype(F32) + second.astype(F32)).astype(BF16)  12 us
    ppermute x4, starting transfers between devices, away(): lax.ppermute(block, ('bit0', 'feat'), [(b, a) for a, b in home_pairs(mask)])  9.47 us
    ppermute x4, starting transfers between devices, home(): return lax.ppermute(block, ('bit0', 'feat'), home_pairs(mask))  7.09 us
  transfers between devices with their start and end apart: 45, of which 22 were waited for; matrix products, arithmetic and copies ran while one was open for 10% of the time, Pallas kernels for 11%

profile of v5, /device:TPU:0, one launch (start us, length us, event | category | flops | bytes accessed | tf_op | source)
XLA Modules:
  0.0 297.4 jit_solution(9514116274340424409)
XLA Ops:
  7.2 1.7 collective-permute-start.1
  8.9 3.3 %collective-permute-start.2 = (bf16[256,1024]{1,0:T(8,128)(2,1)}, bf16[256,1024]{1,0:T(8,128)(2,1)S(1)}, u32[]{:S(2)}, u32[]{:S(2)}) collective-permute-start(bf16[256,1024]{1,0:T(8,128)(2,1)} %hidden_ref.3), channel_id=1, source_target_pairs={{2,0},{0,1},{6,2},{4,3},{3,4},{1,5},{7,6},{5,7},{10,8},{8,9},{14,1... | collective-permute-start | bytes 1572872 | tf_op jit(solution)/shard_map/ppermute | solution.py:65
  12.9 0.9 reshape.375
  16.3 2.2 collective-permute-start
  18.5 1.2 fusion.16
  19.7 1.6 collective-permute-start.3
  22.3 5.9 %collective-permute-done.3 = bf16[3,2,176,128]{3,2,1,0:T(8,128)(2,1)S(1)} collective-permute-done((bf16[3,2,176,128]{3,2,1,0:T(8,128)(2,1)S(1)}, bf16[3,2,176,128]{3,2,1,0:T(8,128)(2,1)S(1)}, u32[]{:S(2)}, u32[]{:S(2)}) %collective-permute-start.3) | collective-permute-done | bytes 270368 | tf_op jit(solution)/shard_map/ppermute | solution.py:44
  28.3 16.9 %collective-permute-done.6 = bf16[32,2688]{1,0:T(8,128)(2,1)S(1)} collective-permute-done((bf16[32,2688]{1,0:T(8,128)(2,1)S(1)}, bf16[32,2688]{1,0:T(8,128)(2,1)S(1)}, u32[]{:S(2)}, u32[]{:S(2)}) %collective-permute-start.6) | collective-permute-done | bytes 172064 | tf_op jit(solution)/shard_map/ppermute | solution.py:48
  45.5 0.9 pad_maximum_fusion.6
  46.5 5.0 %collective-permute-done.7 = bf16[64,1920]{1,0:T(8,128)(2,1)S(1)} collective-permute-done((bf16[64,1920]{1,0:T(8,128)(2,1)S(1)}, bf16[64,1920]{1,0:T(8,128)(2,1)S(1)}, u32[]{:S(2)}, u32[]{:S(2)}) %collective-permute-start.7) | collective-permute-done | bytes 245792 | tf_op jit(solution)/shard_map/ppermute | solution.py:48
  51.7 1.6 collective-permute-start.8
  53.3 1.6 collective-permute-start.9
  54.9 1.0 pad_maximum_fusion.3
  58.1 9.5 %collective-permute-done.9 = bf16[128,1152]{1,0:T(8,128)(2,1)S(1)} collective-permute-done((bf16[128,1152]{1,0:T(8,128)(2,1)S(1)}, bf16[128,1152]{1,0:T(8,128)(2,1)S(1)}, u32[]{:S(2)}, u32[]{:S(2)}) %collective-permute-start.9) | collective-permute-done | bytes 294944 | tf_op jit(solution)/shard_map/ppermute | solution.py:44
  67.7 2.1 collective-permute-start.10
  70.0 5.5 %collective-permute-done.10 = bf16[4,4,32,384]{3,2,1,0:T(8,128)(2,1)S(1)} collective-permute-done((bf16[4,4,32,384]{3,2,1,0:T(8,128)(2,1)S(1)}, bf16[4,4,32,384]{3,2,1,0:T(8,128)(2,1)S(1)}, u32[]{:S(2)}, u32[]{:S(2)}) %collective-permute-start.10) | collective-permute-done | bytes 393248 | tf_op jit(solution)/shard_map/ppermute | solution.py:44
  75.8 5.4 %shard_map.203 = (bf16[4,256,1024]{2,1,0:T(8,128)(2,1)S(1)}, bf16[1024,384]{1,0:T(8,128)(2,1)S(1)}, bf16[256,512]{1,0:T(8,128)(2,1)S(1)}, bf16[256,512]{1,0:T(8,...) custom-call(s32[1]{0:T(128)S(6)} %select_n.309.first_ref, s32[1]{0:T(128)} %bitcast.9.group_ref, ...), custom_call_target="tpu_custom_call" | custom-call | flops 8589934592 | bytes 8388616 | tf_op jit(solution)/shard_map/pallas_call | solution.py:98
  81.1 1.0 copy-done.9
  82.2 2.0 collective-permute-start.16
  85.2 1.7 collective-permute-start.13
  86.9 0.9 collective-permute-start.12
  87.8 8.9 %collective-permute-done.16.refs_5_.refs_7_ = bf16[256,1024]{1,0:T(8,128)(2,1)S(1)} collective-permute-done((bf16[256,1024]{1,0:T(8,128)(2,1)S(1)}, bf16[256,1024]{1,0:T(8,128)(2,1)S(1)}, u32[]{:S(2)}, u32[]{:S(2)}) %collective-permute-start.16) | collective-permute-done | bytes 524320 | tf_op jit(solution)/shard_map/ppermute | solution.py:44
  98.0 5.9 %collective-permute-done.13.a1_ref = bf16[256,512]{1,0:T(8,128)(2,1)S(1)} collective-permute-done((bf16[256,512]{1,0:T(8,128)(2,1)S(1)}, bf16[256,512]{1,0:T(8,128)(2,1)S(1)}, u32[]{:S(2)}, u32[]{:S(2)}) %collective-permute-start.13) | collective-permute-done | bytes 262176 | tf_op jit(solution)/shard_map/ppermute | solution.py:61
  104.0 1.0 shard_map.204.refs_1_.refs_3_
  105.0 1.3 collective-permute-start.17
  106.2 8.0 %collective-permute-done.17.refs_2_.refs_4_ = bf16[256,1024]{1,0:T(8,128)(2,1)S(1)} collective-permute-done((bf16[256,1024]{1,0:T(8,128)(2,1)S(1)}, bf16[256,1024]{1,0:T(8,128)(2,1)S(1)}, u32[]{:S(2)}, u32[]{:S(2)}) %collective-permute-start.17) | collective-permute-done | bytes 524320 | tf_op jit(solution)/shard_map/ppermute | solution.py:44
  114.3 11.8 %collective-permute-start.19 = (bf16[512,1024]{1,0:T(8,128)(2,1)S(1)}, bf16[512,1024]{1,0:T(8,128)(2,1)S(1)}, u32[]{:S(2)}, u32[]{:S(2)}) collective-permute-start(bf16[512,1024]{1,0:T(8,128)(2,1)S(1)} %pad_maximum_fusion.4), channel_id=1, source_target_pairs={{0,4},{4,0},{1,5},{5,1},{2,6},{6,2},{3,7},{7,3},{8,12},{12,8},{9,1... | collective-permute-start | bytes 3145736 | tf_op jit(solution)/shard_map/ppermute | solution.py:44
  126.1 2.3 collective-permute-done.19.refs_3_.refs_5_
  128.4 2.7 all-gather.3.cloned.1.call-done
  131.2 29.2 %shard_map.205 = (bf16[2,256,1024]{2,1,0:T(8,128)(2,1)}, bf16[2,256,1024]{2,1,0:T(8,128)(2,1)}, bf16[2,256,1024]{2,1,0:T(8,128)(2,1)}, bf16[2,256,1024]{2,1,0:T(...) custom-call(s32[1]{0:T(128)} %bitcast.2.refs_0_, ...), custom_call_target="tpu_custom_call" | custom-call | flops 15032385536 | bytes 17039364 | tf_op jit(solution)/shard_map/pallas_call | solution.py:98
  160.5 1.6 collective-permute-start.22
  162.0 1.3 collective-permute-done.20.near_ref
  163.3 1.6 fusion.17
  164.9 1.5 collective-permute-start.21
  166.5 7.5 %shard_map.208 = (bf16[4,352,512]{2,1,0:T(8,128)(2,1)}, bf16[4,352,512]{2,1,0:T(8,128)(2,1)}) custom-call(s32[1]{0:T(128)} %bitcast.2.refs_0_, bf16[704,1024]{1,0:T(8,128)(2,1)} %get-tuple-element.131.refs_1_, bf16[704,1024]{1,0:T(8,128)(2,1)} %get-tuple-element.132.refs_2_, bf16[256,1024]{1,0:T(8,128)(2,1)} %copy-done.4, bf16[256,1024]{1,0:T(8,128)(2,1)} %copy-done.24, ...), custom_call_target="tpu_custom_call" | custom-call | flops 4294967296 | bytes 9961476 | tf_op jit(solution)/shard_map/pallas_call | solution.py:98
  174.0 5.3 %collective-permute-done.22 = bf16[4,176,512]{2,1,0:T(8,128)(2,1)S(1)} collective-permute-done((bf16[4,176,512]{2,1,0:T(8,128)(2,1)}, bf16[4,176,512]{2,1,0:T(8,128)(2,1)S(1)}, u32[]{:S(2)}, u32[]{:S(2)}) %collective-permute-start.22) | collective-permute-done | bytes 720928 | tf_op jit(solution)/shard_map/ppermute | solution.py:44
  179.2 1.5 collective-permute-start.31
  180.7 1.1 add_convert_fusion.2
  181.8 6.9 %shard_map.206 = (f32[256,1024]{1,0:T(8,128)}, bf16[256,512]{1,0:T(8,128)(2,1)}, bf16[256,512]{1,0:T(8,128)(2,1)}, bf16[512,1152]{1,0:T(8,128)(2,1)}, bf16[512,1152]{1,0:T(8,128)(2,1)}, /*index=5*/f32[256,1024]{1,0:T(8,128)}) custom-call(s32[1]{0:T(128)} %bitcast.member_ref, s32[1]{0:T(128)} %bitcast.1.core_ref, ...), custom_call_target="tpu_custom_call" | custom-call | flops 1073741824 | bytes 11534344 | tf_op jit(solution)/shard_map/pallas_call | solution.py:98
  188.8 1.7 collective-permute-start.24
  190.5 2.7 collective-permute-start.25
  193.3 25.7 %collective-permute-done.25.g1_ref = bf16[256,512]{1,0:T(8,128)(2,1)S(1)} collective-permute-done((bf16[256,512]{1,0:T(8,128)(2,1)}, bf16[256,512]{1,0:T(8,128)(2,1)S(1)}, u32[]{:S(2)}, u32[]{:S(2)}) %collective-permute-start.25) | collective-permute-done | bytes 262176 | tf_op jit(solution)/shard_map/ppermute | solution.py:65
  219.8 1.5 add_convert_fusion
  222.6 1.5 add_convert_fusion.1
  225.8 13.4 %shard_map.207 = (bf16[2,256,1024]{2,1,0:T(8,128)(2,1)}, bf16[2,256,1024]{2,1,0:T(8,128)(2,1)}, bf16[1024,384]{1,0:T(8,128)(2,1)}) custom-call(s32[1]{0:T(128)S(6)} %select_n.309.first_ref, s32[1]{0:T(128)} %bitcast.9.group_ref, bf16[256,512]{1,0:T(8,128)(2,1)} %copy-done.29, bf16[256,512]{1,0:T(8,128)(2,1)} %copy-done.30, bf16[256,512]{1,0:T(8,128)(2,1)} %copy-done.34, ...), custom_call_target="tpu_custom_call" | custom-call | flops 12884901888 | bytes 9437192 | tf_op jit(solution)/shard_map/pallas_call | solution.py:98
  239.6 1.3 fusion.18
  241.0 1.4 collective-permute-start.28
  242.3 1.2 fusion.2
  244.9 2.6 fusion.19
  247.5 1.7 collective-permute-start.32
  249.2 2.8 collective-permute-start.38
  251.9 2.8 collective-permute-done.33
  255.6 0.9 collective-permute-start.34
  256.5 1.0 collective-permute-start.37
  257.5 1.2 maximum_convert_fusion
  258.9 3.0 collective-permute-done.34
  261.9 1.0 fusion.21
  262.9 1.9 collective-permute-done.37
  265.1 0.8 collective-permute-start.40
  268.3 2.5 fusion.9
  270.8 3.2 %collective-permute-done.40 = bf16[1056,128]{1,0:T(8,128)(2,1)S(1)} collective-permute-done((bf16[1056,128]{1,0:T(8,128)(2,1)S(1)}, bf16[1056,128]{1,0:T(8,128)(2,1)S(1)}, u32[]{:S(2)}, u32[]{:S(2)}) %collective-permute-start.40) | collective-permute-done | bytes 270368 | tf_op jit(solution)/shard_map/ppermute | solution.py:44
  274.5 2.9 collective-permute-done.39
  277.5 1.0 slice_bitcast_fusion.1
  278.5 8.6 %collective-permute-done.41 = bf16[32,2688]{1,0:T(8,128)(2,1)S(1)} collective-permute-done((bf16[32,2688]{1,0:T(8,128)(2,1)S(1)}, bf16[32,2688]{1,0:T(8,128)(2,1)S(1)}, u32[]{:S(2)}, u32[]{:S(2)}) %collective-permute-start.41) | collective-permute-done | bytes 172064 | tf_op jit(solution)/shard_map/ppermute | solution.py:48
  (222 shorter events, 21.4 us)
Async XLA Ops:
  7.2 124.0 %all-gather.3.cloned.1.call-start = ((), (), s32[]{:S(2)}) async-start(), calls=%async_computation.4 | async-start | bytes 4866048 | tf_op jit(solution)/shard_map/all_gather | solution.py:542
  7.2 38.1 %collective-permute-start.1 = (bf16[256,1024]{1,0:T(8,128)(2,1)}, bf16[256,1024]{1,0:T(8,128)(2,1)S(1)}, u32[]{:S(2)}, u32[]{:S(2)}) collective-permute-start(bf16[256,1024]{1,0:T(8,128)(2,1)} %hidden_ref.3), channel_id=1, source_target_pairs={{0,0},{2,1},{4,2},{6,3},{1,4},{3,5},{5,6},{7,7},{8,8},{10,9},{12,1... | collective-permute-start | bytes 1572872 | tf_op jit(solution)/shard_map/ppermute | solution.py:65
  8.9 36.4 %collective-permute-start.2 = (bf16[256,1024]{1,0:T(8,128)(2,1)}, bf16[256,1024]{1,0:T(8,128)(2,1)S(1)}, u32[]{:S(2)}, u32[]{:S(2)}) collective-permute-start(bf16[256,1024]{1,0:T(8,128)(2,1)} %hidden_ref.3), channel_id=1, source_target_pairs={{2,0},{0,1},{6,2},{4,3},{3,4},{1,5},{7,6},{5,7},{10,8},{8,9},{14,1... | collective-permute-start | bytes 1572872 | tf_op jit(solution)/shard_map/ppermute | solution.py:65
  15.4 5.8 %copy-start.31 = (bf16[32]{0:T(256)(128)(2,1)S(1)}, bf16[32]{0:T(256)(128)(2,1)}, u32[]{:S(2)}) copy-start(bf16[32]{0:T(256)(128)(2,1)} %param.21) | copy-start | bytes 196
  16.3 5.1 %collective-permute-start = (bf16[80,384]{1,0:T(8,128)(2,1)S(1)}, bf16[80,384]{1,0:T(8,128)(2,1)S(1)}, u32[]{:S(2)}, u32[]{:S(2)}) collective-permute-start(bf16[80,384]{1,0:T(8,128)(2,1)S(1)} %concatenate.114), channel_id=1, source_target_pairs={{0,4},{4,0},{1,5},{5,1},{2,6},{6,2},{3,7},{7,3},{8,12},{12,8},{9,1... | collective-permute-start | bytes 184328 | tf_op jit(solution)/shard_map/ppermute | solution.py:44
  18.5 3.1 %copy-start.22 = (bf16[1024,32]{0,1:T(8,128)(2,1)S(1)}, bf16[1024,32]{0,1:T(8,128)(2,1)}, u32[]{:S(2)}) copy-start(bf16[1024,32]{0,1:T(8,128)(2,1)} %param.16) | copy-start | bytes 196612
  19.7 8.5 %collective-permute-start.3 = (bf16[3,2,176,128]{3,2,1,0:T(8,128)(2,1)S(1)}, bf16[3,2,176,128]{3,2,1,0:T(8,128)(2,1)S(1)}, u32[]{:S(2)}, u32[]{:S(2)}) collective-permute-start(bf16[3,2,176,128]{3,2,1,0:T(8,128)(2,1)S(1)} %dynamic-slice_bitcast_fusion.3), channel_id=1, source_target_pairs={{0,8},{8,0},{1,9},{9,1},{2,10},{10,2},{3,11},{11,3},{4,12},{12,4},... | collective-permute-start | bytes 811016 | tf_op jit(solution)/shard_map/ppermute | solution.py:44
  21.6 23.6 %collective-permute-start.6 = (bf16[32,2688]{1,0:T(8,128)(2,1)S(1)}, bf16[32,2688]{1,0:T(8,128)(2,1)S(1)}, u32[]{:S(2)}, u32[]{:S(2)}) collective-permute-start(bf16[32,2688]{1,0:T(8,128)(2,1)S(1)} %pad_maximum_fusion.15), channel_id=1, source_target_pairs={{0,2},{1,3},{2,0},{3,1},{4,6},{5,7},{6,4},{7,5},{8,10},{9,11},{10,... | collective-permute-start | bytes 516104 | tf_op jit(solution)/shard_map/ppermute | solution.py:48
  28.2 17.2 %collective-permute-start.4 = (bf16[3,176,256]{2,1,0:T(8,128)(2,1)S(1)}, bf16[3,176,256]{2,1,0:T(8,128)(2,1)S(1)}, u32[]{:S(2)}, u32[]{:S(2)}) collective-permute-start(bf16[3,176,256]{2,1,0:T(8,128)(2,1)S(1)} %pad_maximum_fusion.8), channel_id=1, source_target_pairs={{0,4},{4,0},{1,5},{5,1},{2,6},{6,2},{3,7},{7,3},{8,12},{12,8},{9,1... | collective-permute-start | bytes 811016 | tf_op jit(solution)/shard_map/ppermute | solution.py:44
  45.3 6.3 %collective-permute-start.7 = (bf16[64,1920]{1,0:T(8,128)(2,1)S(1)}, bf16[64,1920]{1,0:T(8,128)(2,1)S(1)}, u32[]{:S(2)}, u32[]{:S(2)}) collective-permute-start(bf16[64,1920]{1,0:T(8,128)(2,1)S(1)} %pad_maximum_fusion.13), channel_id=1, source_target_pairs={{0,1},{1,0},{2,3},{3,2},{4,5},{5,4},{6,7},{7,6},{8,9},{9,8},{10,11... | collective-permute-start | bytes 737288 | tf_op jit(solution)/shard_map/ppermute | solution.py:48
  46.4 211.2 %reduce-scatter.3.cloned.1.call-start = ((), (), s32[]{:S(2)}) async-start(), calls=%async_computation.2 | async-start | bytes 901120 | tf_op jit(solution)/shard_map/reduce_scatter | solution.py:635
  51.7 5.7 %collective-permute-start.8 = (bf16[2,4,32,384]{3,0,2,1:T(2,128)(2,1)S(1)}, bf16[2,4,32,384]{3,0,2,1:T(2,128)(2,1)S(1)}, u32[]{:S(2)}, u32[]{:S(2)}) collective-permute-start(bf16[2,4,32,384]{3,0,2,1:T(2,128)(2,1)S(1)} %bitcast.206), channel_id=1, source_target_pairs={{0,8},{8,0},{1,9},{9,1},{2,10},{10,2},{3,11},{11,3},{4,12},{12,4},... | collective-permute-start | bytes 589832 | tf_op jit(solution)/shard_map/ppermute | solution.py:44
  53.3 14.3 %collective-permute-start.9 = (bf16[128,1152]{1,0:T(8,128)(2,1)S(1)}, bf16[128,1152]{1,0:T(8,128)(2,1)S(1)}, u32[]{:S(2)}, u32[]{:S(2)}) collective-permute-start(bf16[128,1152]{1,0:T(8,128)(2,1)S(1)} %bitcast.183), channel_id=1, source_target_pairs={{0,16},{16,0},{1,17},{17,1},{2,18},{18,2},{3,19},{19,3},{4,20},{20... | collective-permute-start | bytes 884744 | tf_op jit(solution)/shard_map/ppermute | solution.py:44
  55.9 19.8 %collective-permute-start.5 = (bf16[512,1024]{1,0:T(8,128)(2,1)}, bf16[512,1024]{1,0:T(8,128)(2,1)S(1)}, u32[]{:S(2)}, u32[]{:S(2)}) collective-permute-start(bf16[512,1024]{1,0:T(8,128)(2,1)} %pad_maximum_fusion.3), channel_id=1, source_target_pairs={{0,4},{4,0},{1,5},{5,1},{2,6},{6,2},{3,7},{7,3},{8,12},{12,8},{9,1... | collective-permute-start | bytes 3145736 | tf_op jit(solution)/shard_map/ppermute | solution.py:44
  67.7 14.5 %collective-permute-start.14 = (bf16[2,128,1152]{2,1,0:T(8,128)(2,1)S(1)}, bf16[2,128,1152]{2,1,0:T(8,128)(2,1)S(1)}, u32[]{:S(2)}, u32[]{:S(2)}) collective-permute-start(bf16[2,128,1152]{2,1,0:T(8,128)(2,1)S(1)} %maximum_select_fusion.4), channel_id=1, source_target_pairs={{0,8},{8,0},{1,9},{9,1},{2,10},{10,2},{3,11},{11,3},{4,12},{12,4},... | collective-permute-start | bytes 1769480 | tf_op jit(solution)/shard_map/ppermute | solution.py:44
  67.7 7.8 %collective-permute-start.10 = (bf16[4,4,32,384]{3,2,1,0:T(8,128)(2,1)S(1)}, bf16[4,4,32,384]{3,2,1,0:T(8,128)(2,1)S(1)}, u32[]{:S(2)}, u32[]{:S(2)}) collective-permute-start(bf16[4,4,32,384]{3,2,1,0:T(8,128)(2,1)S(1)} %bitcast.197), channel_id=1, source_target_pairs={{0,16},{16,0},{1,17},{17,1},{2,18},{18,2},{3,19},{19,3},{4,20},{20... | collective-permute-start | bytes 1179656 | tf_op jit(solution)/shard_map/ppermute | solution.py:44
  75.7 5.4 %copy-start.3 = (bf16[2,4,4,32,384]{4,3,2,1,0:T(8,128)(2,1)}, bf16[2,4,4,32,384]{4,3,2,1,0:T(8,128)(2,1)S(1)}, u32[]{:S(2)}) copy-start(bf16[2,4,4,32,384]{4,3,2,1,0:T(8,128)(2,1)S(1)} %maximum_select_fusion.2) | copy-start | bytes 2359300
  75.7 6.4 %copy-start.12 = (bf16[256,1024]{1,0:T(8,128)(2,1)S(1)}, bf16[256,1024]{1,0:T(8,128)(2,1)}, u32[]{:S(2)}) copy-start(bf16[256,1024]{1,0:T(8,128)(2,1)} %refs_6_.1) | copy-start | bytes 1572868
  82.1 2.3 copy-start.10
  82.1 2.6 collective-permute-start.11
  82.2 14.6 %collective-permute-start.16 = (bf16[256,1024]{1,0:T(8,128)(2,1)S(1)}, bf16[256,1024]{1,0:T(8,128)(2,1)S(1)}, u32[]{:S(2)}, u32[]{:S(2)}) collective-permute-start(bf16[256,1024]{1,0:T(8,128)(2,1)S(1)} %copy-done.12), channel_id=1, source_target_pairs={{0,8},{8,0},{1,9},{9,1},{2,10},{10,2},{3,11},{11,3},{4,12},{12,4},... | collective-permute-start | bytes 1572872 | tf_op jit(solution)/shard_map/ppermute | solution.py:44
  84.7 12.2 %collective-permute-start.15 = (bf16[2,2,128,1152]{3,2,1,0:T(8,128)(2,1)S(1)}, bf16[2,2,128,1152]{3,2,1,0:T(8,128)(2,1)S(1)}, u32[]{:S(2)}, u32[]{:S(2)}) collective-permute-start(bf16[2,2,128,1152]{3,2,1,0:T(8,128)(2,1)S(1)} %maximum_select_fusion.1), channel_id=1, source_target_pairs={{0,4},{4,0},{1,5},{5,1},{2,6},{6,2},{3,7},{7,3},{8,12},{12,8},{9,1... | collective-permute-start | bytes 3538952 | tf_op jit(solution)/shard_map/ppermute | solution.py:44
  85.2 18.8 %collective-permute-start.13 = (bf16[256,512]{1,0:T(8,128)(2,1)S(1)}, bf16[256,512]{1,0:T(8,128)(2,1)S(1)}, u32[]{:S(2)}, u32[]{:S(2)}) collective-permute-start(bf16[256,512]{1,0:T(8,128)(2,1)S(1)} %pad_maximum_fusion.11), channel_id=1, source_target_pairs={{0,2},{1,0},{2,6},{3,4},{4,3},{5,1},{6,7},{7,5},{8,10},{9,8},{10,1... | collective-permute-start | bytes 786440 | tf_op jit(solution)/shard_map/ppermute | solution.py:61
  86.9 17.1 %collective-permute-start.12 = (bf16[256,512]{1,0:T(8,128)(2,1)S(1)}, bf16[256,512]{1,0:T(8,128)(2,1)S(1)}, u32[]{:S(2)}, u32[]{:S(2)}) collective-permute-start(bf16[256,512]{1,0:T(8,128)(2,1)S(1)} %pad_maximum_fusion.10), channel_id=1, source_target_pairs={{0,0},{1,2},{2,4},{3,6},{4,1},{5,3},{6,5},{7,7},{8,8},{9,10},{10,1... | collective-permute-start | bytes 786440 | tf_op jit(solution)/shard_map/ppermute | solution.py:61
  96.9 17.4 %collective-permute-start.18 = (bf16[512,1024]{1,0:T(8,128)(2,1)S(1)}, bf16[512,1024]{1,0:T(8,128)(2,1)S(1)}, u32[]{:S(2)}, u32[]{:S(2)}) collective-permute-start(bf16[512,1024]{1,0:T(8,128)(2,1)S(1)} %pad_maximum_fusion.5), channel_id=1, source_target_pairs={{0,4},{4,0},{1,5},{5,1},{2,6},{6,2},{3,7},{7,3},{8,12},{12,8},{9,1... | collective-permute-start | bytes 3145736 | tf_op jit(solution)/shard_map/ppermute | solution.py:44
  97.6 6.4 %copy-start.1 = (bf16[256,1024]{1,0:T(8,128)(2,1)S(1)}, bf16[256,1024]{1,0:T(8,128)(2,1)}, u32[]{:S(2)}) copy-start(bf16[256,1024]{1,0:T(8,128)(2,1)} %hidden_ref.3) | copy-start | bytes 1572868
  98.0 6.9 %copy-start = (bf16[2,2,2,128,1152]{4,3,2,1,0:T(8,128)(2,1)}, bf16[2,2,2,128,1152]{4,3,2,1,0:T(8,128)(2,1)S(1)}, u32[]{:S(2)}) copy-start(bf16[2,2,2,128,1152]{4,3,2,1,0:T(8,128)(2,1)S(1)} %maximum_select_fusion) | copy-start | bytes 7077892
  105.0 26.2 %copy-start.4 = (bf16[256,1024]{1,0:T(8,128)(2,1)}, bf16[256,1024]{1,0:T(8,128)(2,1)S(1)}, u32[]{:S(2)}) copy-start(bf16[256,1024]{1,0:T(8,128)(2,1)S(1)} %shard_map.204.refs_1_.refs_3_) | copy-start | bytes 1572868
  105.0 9.2 %collective-permute-start.17 = (bf16[256,1024]{1,0:T(8,128)(2,1)S(1)}, bf16[256,1024]{1,0:T(8,128)(2,1)S(1)}, u32[]{:S(2)}, u32[]{:S(2)}) collective-permute-start(bf16[256,1024]{1,0:T(8,128)(2,1)S(1)} %shard_map.204.refs_1_.refs_3_), channel_id=1, source_target_pairs={{0,8},{8,0},{1,9},{9,1},{2,10},{10,2},{3,11},{11,3},{4,12},{12,4},... | collective-permute-start | bytes 1572872 | tf_op jit(solution)/shard_map/ppermute | solution.py:44
  114.2 16.9 %copy-start.24 = (bf16[256,1024]{1,0:T(8,128)(2,1)}, bf16[256,1024]{1,0:T(8,128)(2,1)S(1)}, u32[]{:S(2)}) copy-start(bf16[256,1024]{1,0:T(8,128)(2,1)S(1)} %collective-permute-done.17.refs_2_.refs_4_) | copy-start | bytes 1572868
  114.3 11.8 %copy-start.32 = (bf16[512,1024]{1,0:T(8,128)(2,1)}, bf16[512,1024]{1,0:T(8,128)(2,1)S(1)}, u32[]{:S(2)}) copy-start(bf16[512,1024]{1,0:T(8,128)(2,1)S(1)} %collective-permute-done.18.refs_6_.refs_8_) | copy-start | bytes 3145732
  114.3 14.1 %collective-permute-start.19 = (bf16[512,1024]{1,0:T(8,128)(2,1)S(1)}, bf16[512,1024]{1,0:T(8,128)(2,1)S(1)}, u32[]{:S(2)}, u32[]{:S(2)}) collective-permute-start(bf16[512,1024]{1,0:T(8,128)(2,1)S(1)} %pad_maximum_fusion.4), channel_id=1, source_target_pairs={{0,4},{4,0},{1,5},{5,1},{2,6},{6,2},{3,7},{7,3},{8,12},{12,8},{9,1... | collective-permute-start | bytes 3145736 | tf_op jit(solution)/shard_map/ppermute | solution.py:44
  128.4 2.8 copy-start.33
  160.4 2.9 collective-permute-start.20
  160.5 18.8 %collective-permute-start.22 = (bf16[4,176,512]{2,1,0:T(8,128)(2,1)}, bf16[4,176,512]{2,1,0:T(8,128)(2,1)S(1)}, u32[]{:S(2)}, u32[]{:S(2)}) collective-permute-start(bf16[4,176,512]{2,1,0:T(8,128)(2,1)} %get-tuple-element.104), channel_id=1, source_target_pairs={{0,16},{16,0},{1,17},{17,1},{2,18},{18,2},{3,19},{19,3},{4,20},{20... | collective-permute-start | bytes 2162696 | tf_op jit(solution)/shard_map/ppermute | solution.py:44
  163.3 10.6 %copy-start.11 = (bf16[2,256,1024]{2,1,0:T(8,128)(2,1)}, bf16[2,256,1024]{2,1,0:T(8,128)(2,1)S(1)}, u32[]{:S(2)}) copy-start(bf16[2,256,1024]{2,1,0:T(8,128)(2,1)S(1)} %collective-permute-done.20.near_ref) | copy-start | bytes 3145732
  164.9 15.8 %collective-permute-start.21 = (bf16[256,1024]{1,0:T(8,128)(2,1)S(1)}, bf16[256,1024]{1,0:T(8,128)(2,1)S(1)}, u32[]{:S(2)}, u32[]{:S(2)}) collective-permute-start(bf16[256,1024]{1,0:T(8,128)(2,1)S(1)} %fusion.17), channel_id=1, source_target_pairs={{0,8},{8,0},{1,9},{9,1},{2,10},{10,2},{3,11},{11,3},{4,12},{12,4},... | collective-permute-start | bytes 1572872 | tf_op jit(solution)/shard_map/ppermute | solution.py:44
  166.4 52.6 %collective-permute-start.23 = (bf16[2,256,1024]{2,1,0:T(8,128)(2,1)}, bf16[2,256,1024]{2,1,0:T(8,128)(2,1)}, u32[]{:S(2)}, u32[]{:S(2)}) collective-permute-start(bf16[2,256,1024]{2,1,0:T(8,128)(2,1)} %get-tuple-element.109), channel_id=1, source_target_pairs={{0,4},{4,0},{1,5},{5,1},{2,6},{6,2},{3,7},{7,3},{8,12},{12,8},{9,1... | collective-permute-start | bytes 3145736 | tf_op jit(solution)/shard_map/ppermute | solution.py:44
  166.5 14.3 %copy-start.21 = (bf16[4,176,512]{2,1,0:T(8,128)(2,1)S(1)}, bf16[4,176,512]{2,1,0:T(8,128)(2,1)}, u32[]{:S(2)}) copy-start(bf16[4,176,512]{2,1,0:T(8,128)(2,1)} %get-tuple-element.102) | copy-start | bytes 2162692
  179.2 40.6 %collective-permute-start.31 = (bf16[4,352,512]{2,1,0:T(8,128)(2,1)}, bf16[4,352,512]{2,1,0:T(8,128)(2,1)S(1)}, u32[]{:S(2)}, u32[]{:S(2)}) collective-permute-start(bf16[4,352,512]{2,1,0:T(8,128)(2,1)} %get-tuple-element.136), channel_id=1, source_target_pairs={{0,16},{16,0},{1,17},{17,1},{2,18},{18,2},{3,19},{19,3},{4,20},{20... | collective-permute-start | bytes 4325384 | tf_op jit(solution)/shard_map/ppermute | solution.py:44
  188.7 31.1 %copy-start.13 = (bf16[4,352,512]{2,1,0:T(8,128)(2,1)S(1)}, bf16[4,352,512]{2,1,0:T(8,128)(2,1)}, u32[]{:S(2)}) copy-start(bf16[4,352,512]{2,1,0:T(8,128)(2,1)} %get-tuple-element.134) | copy-start | bytes 4325380
  188.8 4.5 %collective-permute-start.24 = (bf16[256,512]{1,0:T(8,128)(2,1)}, bf16[256,512]{1,0:T(8,128)(2,1)S(1)}, u32[]{:S(2)}, u32[]{:S(2)}) collective-permute-start(bf16[256,512]{1,0:T(8,128)(2,1)} %get-tuple-element.112), channel_id=1, source_target_pairs={{0,0},{2,1},{4,2},{6,3},{1,4},{3,5},{5,6},{7,7},{8,8},{10,9},{12,1... | collective-permute-start | bytes 786440 | tf_op jit(solution)/shard_map/ppermute | solution.py:65
  190.5 28.6 %collective-permute-start.25 = (bf16[256,512]{1,0:T(8,128)(2,1)}, bf16[256,512]{1,0:T(8,128)(2,1)S(1)}, u32[]{:S(2)}, u32[]{:S(2)}) collective-permute-start(bf16[256,512]{1,0:T(8,128)(2,1)} %get-tuple-element.113), channel_id=1, source_target_pairs={{2,0},{0,1},{6,2},{4,3},{3,4},{1,5},{7,6},{5,7},{10,8},{8,9},{14,1... | collective-permute-start | bytes 786440 | tf_op jit(solution)/shard_map/ppermute | solution.py:65
  193.2 64.3 %reduce-scatter.5.cloned.1.call-start = ((), (), s32[]{:S(2)}) async-start(), calls=%async_computation.3 | async-start | bytes 1802240 | tf_op jit(solution)/shard_map/reduce_scatter | solution.py:635
  193.3 28.1 %copy-start.29 = (bf16[256,512]{1,0:T(8,128)(2,1)}, bf16[256,512]{1,0:T(8,128)(2,1)S(1)}, u32[]{:S(2)}) copy-start(bf16[256,512]{1,0:T(8,128)(2,1)S(1)} %collective-permute-done.24.g0_ref) | copy-start | bytes 786436
  219.0 3.2 %collective-permute-start.26 = (bf16[512,1152]{1,0:T(8,128)(2,1)}, bf16[512,1152]{1,0:T(8,128)(2,1)}, u32[]{:S(2)}, u32[]{:S(2)}) collective-permute-start(bf16[512,1152]{1,0:T(8,128)(2,1)} %get-tuple-element.115), channel_id=1, source_target_pairs={{0,4},{4,0},{1,5},{5,1},{2,6},{6,2},{3,7},{7,3},{8,12},{12,8},{9,1... | collective-permute-start | bytes 3538952 | tf_op jit(solution)/shard_map/ppermute | solution.py:44
  222.2 2.8 collective-permute-start.29
  224.3 16.7 %collective-permute-start.27 = (bf16[2,4,32,1152]{3,2,1,0:T(8,128)(2,1)S(1)}, bf16[2,4,32,1152]{3,2,1,0:T(8,128)(2,1)}, u32[]{:S(2)}, u32[]{:S(2)}) collective-permute-start(bf16[2,4,32,1152]{3,2,1,0:T(8,128)(2,1)S(1)} %dynamic-slice_bitcast_fusion), channel_id=1, source_target_pairs={{0,8},{8,0},{1,9},{9,1},{2,10},{10,2},{3,11},{11,3},{4,12},{12,4},... | collective-permute-start | bytes 1769480 | tf_op jit(solution)/shard_map/ppermute | solution.py:44
  225.8 13.6 %copy-start.2 = (bf16[256,1024]{1,0:T(8,128)(2,1)S(1)}, bf16[256,1024]{1,0:T(8,128)(2,1)}, u32[]{:S(2)}) copy-start(bf16[256,1024]{1,0:T(8,128)(2,1)} %hidden_ref.3) | copy-start | bytes 1572868
  225.8 13.8 %copy-start.15 = (bf16[2,256,1024]{2,1,0:T(8,128)(2,1)S(1)}, bf16[2,256,1024]{2,1,0:T(8,128)(2,1)}, u32[]{:S(2)}) copy-start(bf16[2,256,1024]{2,1,0:T(8,128)(2,1)} %get-tuple-element.107) | copy-start | bytes 3145732
  239.2 4.4 %collective-permute-start.30 = (bf16[2,256,1024]{2,1,0:T(8,128)(2,1)}, bf16[2,256,1024]{2,1,0:T(8,128)(2,1)}, u32[]{:S(2)}, u32[]{:S(2)}) collective-permute-start(bf16[2,256,1024]{2,1,0:T(8,128)(2,1)} %get-tuple-element.130), channel_id=1, source_target_pairs={{0,4},{4,0},{1,5},{5,1},{2,6},{6,2},{3,7},{7,3},{8,12},{12,8},{9,1... | collective-permute-start | bytes 3145736 | tf_op jit(solution)/shard_map/ppermute | solution.py:44
  239.6 3.9 %copy-start.20 = (bf16[1024,384]{1,0:T(8,128)(2,1)S(1)}, bf16[1024,384]{1,0:T(8,128)(2,1)}, u32[]{:S(2)}) copy-start(bf16[1024,384]{1,0:T(8,128)(2,1)} %get-tuple-element.139) | copy-start | bytes 2359300
  241.0 4.0 %copy-start.19 = (bf16[2,256,1024]{2,1,0:T(8,128)(2,1)S(1)}, bf16[2,256,1024]{2,1,0:T(8,128)(2,1)}, u32[]{:S(2)}) copy-start(bf16[2,256,1024]{2,1,0:T(8,128)(2,1)} %get-tuple-element.128) | copy-start | bytes 3145732
  241.0 14.6 %collective-permute-start.28 = (bf16[256,1024]{1,0:T(8,128)(2,1)S(1)}, bf16[256,1024]{1,0:T(8,128)(2,1)S(1)}, u32[]{:S(2)}, u32[]{:S(2)}) collective-permute-start(bf16[256,1024]{1,0:T(8,128)(2,1)S(1)} %fusion.18), channel_id=1, source_target_pairs={{0,8},{8,0},{1,9},{9,1},{2,10},{10,2},{3,11},{11,3},{4,12},{12,4},... | collective-permute-start | bytes 1572872 | tf_op jit(solution)/shard_map/ppermute | solution.py:44
  243.6 11.1 %collective-permute-start.33 = (bf16[2,2,4,32,384]{4,3,2,1,0:T(8,128)(2,1)S(1)}, bf16[2,2,4,32,384]{4,3,2,1,0:T(8,128)(2,1)S(1)}, u32[]{:S(2)}, u32[]{:S(2)}) collective-permute-start(bf16[2,2,4,32,384]{4,3,2,1,0:T(8,128)(2,1)S(1)} %dynamic-slice_bitcast_fusion.1), channel_id=1, source_target_pairs={{0,16},{16,0},{1,17},{17,1},{2,18},{18,2},{3,19},{19,3},{4,20},{20... | collective-permute-start | bytes 1179656 | tf_op jit(solution)/shard_map/ppermute | solution.py:44
  247.5 19.1 %collective-permute-start.32 = (bf16[256,1024]{1,0:T(8,128)(2,1)}, bf16[256,1024]{1,0:T(8,128)(2,1)S(1)}, u32[]{:S(2)}, u32[]{:S(2)}) collective-permute-start(bf16[256,1024]{1,0:T(8,128)(2,1)} %get-tuple-element.137), channel_id=1, source_target_pairs={{0,0},{1,2},{2,4},{3,6},{4,1},{5,3},{6,5},{7,7},{8,8},{9,10},{10,1... | collective-permute-start | bytes 1572872 | tf_op jit(solution)/shard_map/ppermute | solution.py:61
  249.2 17.4 %collective-permute-start.38 = (bf16[256,1024]{1,0:T(8,128)(2,1)}, bf16[256,1024]{1,0:T(8,128)(2,1)S(1)}, u32[]{:S(2)}, u32[]{:S(2)}) collective-permute-start(bf16[256,1024]{1,0:T(8,128)(2,1)} %get-tuple-element.147), channel_id=1, source_target_pairs={{0,2},{1,0},{2,6},{3,4},{4,3},{5,1},{6,7},{7,5},{8,10},{9,8},{10,1... | collective-permute-start | bytes 1572872 | tf_op jit(solution)/shard_map/ppermute | solution.py:61
  255.6 6.3 %collective-permute-start.34 = (bf16[2,4,32,384]{3,2,1,0:T(8,128)(2,1)}, bf16[2,4,32,384]{3,2,1,0:T(8,128)(2,1)}, u32[]{:S(2)}, u32[]{:S(2)}) collective-permute-start(bf16[2,4,32,384]{3,2,1,0:T(8,128)(2,1)} %dynamic-slice_bitcast_fusion.4), channel_id=1, source_target_pairs={{0,8},{8,0},{1,9},{9,1},{2,10},{10,2},{3,11},{11,3},{4,12},{12,4},... | collective-permute-start | bytes 589832 | tf_op jit(solution)/shard_map/ppermute | solution.py:44
  256.5 8.4 %collective-permute-start.37 = (bf16[4,32,1152]{2,1,0:T(8,128)(2,1)}, bf16[4,32,1152]{2,1,0:T(8,128)(2,1)S(1)}, u32[]{:S(2)}, u32[]{:S(2)}) collective-permute-start(bf16[4,32,1152]{2,1,0:T(8,128)(2,1)} %dynamic-slice_bitcast_fusion.2), channel_id=1, source_target_pairs={{0,16},{16,0},{1,17},{17,1},{2,18},{18,2},{3,19},{19,3},{4,20},{20... | collective-permute-start | bytes 884744 | tf_op jit(solution)/shard_map/ppermute | solution.py:44
  258.8 6.1 %collective-permute-start.35 = (f32[528,256]{1,0:T(8,128)S(1)}, f32[528,256]{1,0:T(8,128)S(1)}, u32[]{:S(2)}, u32[]{:S(2)}) collective-permute-start(f32[528,256]{1,0:T(8,128)S(1)} %pad_maximum_fusion.7), channel_id=1, source_target_pairs={{0,4},{4,0},{1,5},{5,1},{2,6},{6,2},{3,7},{7,3},{8,12},{12,8},{9,1... | collective-permute-start | bytes 1622024 | tf_op jit(solution)/shard_map/ppermute | solution.py:44
  265.0 1.4 collective-permute-start.36
  265.1 8.9 %collective-permute-start.40 = (bf16[1056,128]{1,0:T(8,128)(2,1)S(1)}, bf16[1056,128]{1,0:T(8,128)(2,1)S(1)}, u32[]{:S(2)}, u32[]{:S(2)}) collective-permute-start(bf16[1056,128]{1,0:T(8,128)(2,1)S(1)} %pad_maximum_fusion.9), channel_id=1, source_target_pairs={{0,8},{8,0},{1,9},{9,1},{2,10},{10,2},{3,11},{11,3},{4,12},{12,4},... | collective-permute-start | bytes 811016 | tf_op jit(solution)/shard_map/ppermute | solution.py:44
  266.5 10.8 %collective-permute-start.39 = (bf16[2,32,1920]{2,1,0:T(8,128)(2,1)S(1)}, bf16[2,32,1920]{2,1,0:T(8,128)(2,1)S(1)}, u32[]{:S(2)}, u32[]{:S(2)}) collective-permute-start(bf16[2,32,1920]{2,1,0:T(8,128)(2,1)S(1)} %pad_maximum_fusion.14), channel_id=1, source_target_pairs={{0,1},{1,0},{2,3},{3,2},{4,5},{5,4},{6,7},{7,6},{8,9},{9,8},{10,11... | collective-permute-start | bytes 737288 | tf_op jit(solution)/shard_map/ppermute | solution.py:48
  277.4 9.6 %collective-permute-start.41 = (bf16[32,2688]{1,0:T(8,128)(2,1)S(1)}, bf16[32,2688]{1,0:T(8,128)(2,1)S(1)}, u32[]{:S(2)}, u32[]{:S(2)}) collective-permute-start(bf16[32,2688]{1,0:T(8,128)(2,1)S(1)} %pad_maximum_fusion.16), channel_id=1, source_target_pairs={{0,2},{1,3},{2,0},{3,1},{4,6},{5,7},{6,4},{7,5},{8,10},{9,11},{10,... | collective-permute-start | bytes 516104 | tf_op jit(solution)/shard_map/ppermute | solution.py:48
  (16 other events, 23.3 us)
Sparse Core Ops, SparseCore 0:
  46.5 84.6 all-gather.2
  193.4 25.1 reduce-scatter.2
  221.5 31.0 reduce-scatter.4
